TPU v7x, 32 devices: a whole 2x2x4 slice. The times are simulated.
32 devices in a mesh: section: 2 (over x), seq: 16 (over z, y, core).
Axes of the slice: x: 2, y: 2, z: 4, core: 2. Of those that a mesh axis runs over, the one named last changes fastest.
Arguments:
- stream: bfloat16 [2, 2048, 4096], P('section', 'seq'), may hold values from -200 to 200
- cotangent: bfloat16 [2, 2048, 4096], P('section', 'seq'), may hold values from -24 to 24
- keys: bfloat16 [2, 2048, 512], P('section', 'seq'), may hold values from -30 to 30
- values: bfloat16 [2, 2048, 512], P('section', 'seq'), may hold values from -6 to 6
- gain: float32 [2, 4096], P('section'), may hold values from 0.5 to 2
- rand_blocks: int32 [16, 1], P('seq'), may hold values from 0 to 15, as said below
Outputs:
- stream_grads: bfloat16 [2, 2048, 4096], P('section', 'seq')
- key_grads: bfloat16 [2, 2048, 512], P('section', 'seq')
- value_grads: bfloat16 [2, 2048, 512], P('section', 'seq')
Inputs may be any that keep to these rules, and one draw needn't show every extreme that they name: `rand_blocks`: row d names one block, of the form d xor 2**b with b >= 1; every row d = 2**b with b >= 1 names block 0.
All inputs are finite; a program needn't handle non-finite values.
Results may differ from a plain program's by a relative error of at most 0.012.
The roundings to bfloat16 on the way count: a program that leaves them out, or rounds other values in their place, can miss the bound.
Values may be sent and summed in bfloat16 or wider, within the bound.
No kernel may reach another device: no remote copies, remote signals or barrier semaphores. Data moves between devices by JAX's collectives and lax.ppermute only.
A program may use at most 128 MiB of HBM per device.

v0:
```python
import jax
import jax.numpy as jnp
from jax import lax
from jax.sharding import PartitionSpec as P

HD = 128
RAND = 1


def extended(array, sides, width):
    for axis, dim in sides:
        peers, length = (lax.axis_size(axis), array.shape[dim])
        up = [(i, (i + 1) % peers) for i in range(peers - 1)]
        down = [(j, i) for i, j in up]
        last = lax.slice_in_dim(array, length - width, length, axis=dim)
        leading = lax.slice_in_dim(array, 0, width, axis=dim)
        before = lax.ppermute(last, axis, up)
        after = lax.ppermute(leading, axis, down)
        array = jnp.concatenate([before, array, after], axis=dim)
    return array


def broadcast(value, axis, source):
    kept = jnp.where(lax.axis_index(axis) == source, value, 0).astype(value.dtype)
    return lax.psum(kept, axis)


def swapped(value, axis, apart):
    mask = 2**apart
    pairs = [(source, source ^ mask) for source in range(lax.axis_size(axis))]
    return lax.ppermute(value, axis, pairs)


def from_behind(block, axis, distance):
    devices = range(lax.axis_size(axis))
    route = [((i - distance) % len(devices), i) for i in devices]
    return lax.ppermute(block, axis, route)


def from_behind_2(block, axis, distance):
    devices = range(lax.axis_size(axis))
    route = [(i - distance, i) for i in devices if i - distance in devices]
    return lax.ppermute(block, axis, route)


def group_terms(queries, slot_keys, slot_values, slot_valid, upstream):
    row_count = queries.shape[0]
    head_dim = slot_keys.shape[1]
    head_count = queries.shape[1] // head_dim
    factor = head_dim ** (-0.5)
    query_heads = queries.reshape(row_count, head_count, head_dim)
    grad_heads = upstream.reshape(row_count, head_count, head_dim)
    scores = jnp.where(
        slot_valid[None, None, :],
        jnp.einsum("qhd,kd->hqk", query_heads, slot_keys, preferred_element_type=jnp.float32)
        * factor,
        -1e30,
    )
    row_peak = jnp.max(scores, axis=2, keepdims=True)
    raised = jnp.exp(scores - row_peak)
    weights = raised / jnp.sum(raised, axis=2, keepdims=True)
    weights_low = weights.astype(jnp.bfloat16)
    grad_weights = jnp.einsum(
        "qhd,kd->hqk", grad_heads, slot_values, preferred_element_type=jnp.float32
    )
    row_dot = jnp.sum(weights * grad_weights, axis=2, keepdims=True)
    grad_low = (weights * (grad_weights - row_dot) * factor).astype(jnp.bfloat16)
    grad_query = jnp.einsum("hqk,kd->qhd", grad_low, slot_keys, preferred_element_type=jnp.float32)
    grad_keys = jnp.einsum("hqk,qhd->kd", grad_low, query_heads, preferred_element_type=jnp.float32)
    grad_values = jnp.einsum(
        "hqk,qhd->kd", weights_low, grad_heads, preferred_element_type=jnp.float32
    )
    return (grad_query.reshape(row_count, head_count * head_dim), grad_keys, grad_values)


def on_device(stream, cotangent, keys, values, gain, rand_blocks):
    hidden = stream[0]
    upstream = cotangent[0]
    block_rows = hidden.shape[0]
    model_width = hidden.shape[1]
    kv_width = keys.shape[2]
    groups = kv_width // HD
    query_cols = model_width // groups
    seq_count = lax.axis_size("seq")
    bit_count = seq_count.bit_length() - 1
    device = lax.axis_index("seq")
    own_blocks = jnp.concatenate([keys[0], values[0]], axis=1)
    window = extended(own_blocks, (("seq", 0),), block_rows)
    global_block = broadcast(own_blocks, "seq", 0)
    partner_rows = []
    partner_ids = []
    for bit_index in range(1, bit_count):
        partner_rows.append(swapped(own_blocks, "seq", bit_index))
        partner_ids.append(jnp.bitwise_xor(device, 1 << bit_index))
    wanted = rand_blocks[0]
    slot_index = 0
    picked = jnp.zeros_like(own_blocks)
    for position in range(len(partner_rows)):
        picked = jnp.where(
            wanted[slot_index] == partner_ids[position], partner_rows[position], picked
        )
    chosen = [picked]
    slots = jnp.concatenate([window, global_block] + chosen, axis=0)
    flags = jnp.stack(
        [device > 0, device >= 0, device < seq_count - 1, device > 0] + [device >= 0] * RAND
    )
    slot_valid = jnp.repeat(flags, block_rows)
    hidden_wide = hidden.astype(jnp.float32)
    inverse = lax.rsqrt(jnp.mean(hidden_wide * hidden_wide, axis=1, keepdims=True) + 1e-05)
    normed = hidden_wide * inverse
    gain_row = gain[0]
    queries = (normed * gain_row).astype(jnp.bfloat16)
    query_parts = []
    key_parts = []
    value_parts = []
    for group in range(groups):
        grad_query, grad_keys, grad_values = group_terms(
            queries[:, group * query_cols : (group + 1) * query_cols],
            slots[:, group * HD : (group + 1) * HD],
            slots[:, kv_width + group * HD : kv_width + (group + 1) * HD],
            slot_valid,
            upstream[:, group * query_cols : (group + 1) * query_cols],
        )
        query_parts.append(grad_query)
        key_parts.append(grad_keys)
        value_parts.append(grad_values)
    grad_query = jnp.concatenate(query_parts, axis=1)
    grad_slots = jnp.concatenate(key_parts + value_parts, axis=1)
    grad_normed = grad_query * gain_row
    grad_hidden = inverse * (
        grad_normed - normed * jnp.mean(grad_normed * normed, axis=1, keepdims=True)
    )
    handed = (upstream.astype(jnp.float32) + grad_hidden).astype(jnp.bfloat16)
    previous = from_behind(handed, "section", -1)
    self_term = grad_slots[block_rows : 2 * block_rows]
    to_prev = grad_slots[0:block_rows].astype(jnp.bfloat16)
    to_next = grad_slots[2 * block_rows : 3 * block_rows].astype(jnp.bfloat16)
    global_term = grad_slots[3 * block_rows : 4 * block_rows]
    slot_index = 0
    random_terms = [
        grad_slots[(4 + slot_index) * block_rows : (5 + slot_index) * block_rows].astype(
            jnp.bfloat16
        )
    ]
    from_prev = from_behind_2(to_next, "seq", 1)
    from_next = from_behind_2(to_prev, "seq", -1)
    returned = jnp.zeros(self_term.shape, jnp.float32)
    for bit_index in range(1, bit_count):
        outgoing = jnp.zeros_like(to_prev)
        slot_index = 0
        outgoing = jnp.where(
            wanted[slot_index] == partner_ids[bit_index - 1], random_terms[slot_index], outgoing
        )
        returned = returned + swapped(outgoing, "seq", bit_index).astype(jnp.float32)
    local_total = (
        self_term + from_prev.astype(jnp.float32) + from_next.astype(jnp.float32) + returned
    )
    combined = global_term + jnp.where(device == 0, local_total, 0.0)
    share = lax.psum_scatter(combined, "seq", scatter_dimension=0, tiled=True).astype(jnp.bfloat16)
    whole = lax.all_gather(share, "seq", axis=0, tiled=True)
    total = jnp.where(device == 0, whole, local_total.astype(jnp.bfloat16))
    return (previous[None], total[:, :kv_width][None], total[:, kv_width:][None])


def solution(mesh):
    return jax.shard_map(
        on_device,
        mesh=mesh,
        in_specs=(
            P("section", "seq", None),
            P("section", "seq", None),
            P("section", "seq", None),
            P("section", "seq", None),
            P("section", None),
            P("seq", None),
        ),
        out_specs=(P("section", "seq", None), P("section", "seq", None), P("section", "seq", None)),
        check_vma=False,
    )
```

profile of v0, /device:TPU:0, one launch (start us, length us, event | category | flops | bytes accessed | tf_op | source)
XLA Modules:
  0.0 308.1 jit_solution(4871247636303732176)
XLA Ops:
  9.0 3.2 %collective-permute-start = (bf16[128,1024]{1,0:T(8,128)(2,1)}, bf16[128,1024]{1,0:T(8,128)(2,1)}, u32[]{:S(2)}, u32[]{:S(2)}) collective-permute-start(bf16[128,1024]{1,0:T(8,128)(2,1)} %pad_maximum_fusion), channel_id=1, source_target_pairs={{0,1},{1,2},{2,3},{3,4},{4,5},{5,6},{6,7},{7,8},{8,9},{9,10},{10,1... | collective-permute-start | bytes 786440 | tf_op jit(solution)/shard_map/ppermute | solution.py:17
  13.5 6.2 %collective-permute-start.2 = (bf16[128,1024]{1,0:T(8,128)(2,1)}, bf16[128,1024]{1,0:T(8,128)(2,1)}, u32[]{:S(2)}, u32[]{:S(2)}) collective-permute-start(bf16[128,1024]{1,0:T(8,128)(2,1)} %pad_maximum_fusion), channel_id=1, source_target_pairs={{0,8},{1,9},{2,10},{3,11},{4,12},{5,13},{6,14},{7,15},{8,0},{9,1},... | collective-permute-start | bytes 786440 | tf_op jit(solution)/shard_map/ppermute | solution.py:31
  33.9 83.8 %all-reduce.2.cloned.1.call-done = bf16[128,1024]{1,0:T(8,128)(2,1)} async-done(((bf16[128,1024]{1,0:T(8,128)(2,1)}), bf16[128,1024]{1,0:T(8,128)(2,1)}) %all-reduce.2.cloned.1.call-update) | async-done | bytes 262160 | tf_op jit(solution)/shard_map/psum | solution.py:25
  124.1 3.4 %fusion.159 = (f32[8,128]{1,0:T(8,128)S(1)}, f32[8,128,640]{1,2,0:T(8,128)}) fusion(pred[640]{0:T(1024)(128)(4,1)S(1)} %broadcast_bitcast_fusion, bf16[128,8,128]{0,2,1:T(8,128)(2,1)S(1)} %bitcast.345, bf16[640,1024]{1,0:T(8,128)(2,1)} %select_dynamic-update-slice_fusion), kind=kOutput, calls=%fused_computation.183 | convolution fusion | flops 170394240 | bytes 3052160 | tf_op jit(solution)/shard_map/sub | solution.py:60
  127.4 5.0 %fusion.67 = f32[128,8,128]{2,0,1:T(8,128)S(1)} fusion(f32[640,128,8]{1,0,2:T(8,128)} %fusion.123, bf16[640,1024]{1,0:T(8,128)(2,1)} %select_dynamic-update-slice_fusion, f32[8,128,640]{1,2,0:T(8,128)} %get-tuple-element.32, f32[8,128]{1,0:T(8,128)S(1)} %get-tuple-element.31), kind=kOutput, calls=%fused_computation.86 | convolution fusion | flops 172361344 | bytes 11182080 | tf_op jit(solution)/shard_map/hqk,kd->qhd/dot_general | solution.py:68
  132.5 5.7 %fusion.109 = f32[640,1024]{1,0:T(8,128)} fusion(bf16[128,8,128]{0,2,1:T(8,128)(2,1)S(1)} %bitcast.346, f32[640,128,8]{1,0,2:T(8,128)} %fusion.123, f32[8,128,640]{1,2,0:T(8,128)} %get-tuple-element.32, f32[8,128]{1,0:T(8,128)S(1)} %get-tuple-element.31), kind=kOutput, calls=%fused_computation.112 | convolution fusion | flops 172361344 | bytes 11083776 | tf_op jit(solution)/shard_map/hqk,qhd->kd/dot_general | solution.py:69
  138.1 3.0 fusion.120
  141.1 3.4 %fusion.156 = (f32[8,128]{1,0:T(8,128)S(1)}, f32[8,128,640]{1,2,0:T(8,128)}) fusion(pred[640]{0:T(1024)(128)(4,1)S(1)} %broadcast_bitcast_fusion, bf16[128,8,128]{0,2,1:T(8,128)(2,1)S(1)} %bitcast.340, bf16[640,1024]{1,0:T(8,128)(2,1)} %select_dynamic-update-slice_fusion), kind=kOutput, calls=%fused_computation.180 | convolution fusion | flops 170394240 | bytes 3052160 | tf_op jit(solution)/shard_map/sub | solution.py:60
  144.5 2.9 fusion.121
  147.4 3.4 %fusion.157 = (f32[8,128]{1,0:T(8,128)S(1)}, f32[8,128,640]{1,2,0:T(8,128)}) fusion(pred[640]{0:T(1024)(128)(4,1)S(1)} %broadcast_bitcast_fusion, bf16[128,8,128]{0,2,1:T(8,128)(2,1)S(1)} %bitcast.342, bf16[640,1024]{1,0:T(8,128)(2,1)} %select_dynamic-update-slice_fusion), kind=kOutput, calls=%fused_computation.181 | convolution fusion | flops 170394240 | bytes 3052160 | tf_op jit(solution)/shard_map/sub | solution.py:60
  153.7 3.4 %fusion.158 = (f32[8,128]{1,0:T(8,128)S(1)}, f32[8,128,640]{1,2,0:T(8,128)}) fusion(pred[640]{0:T(1024)(128)(4,1)S(1)} %broadcast_bitcast_fusion, bf16[128,8,128]{0,2,1:T(8,128)(2,1)S(1)} %bitcast.344, bf16[640,1024]{1,0:T(8,128)(2,1)} %select_dynamic-update-slice_fusion), kind=kOutput, calls=%fused_computation.182 | convolution fusion | flops 170394240 | bytes 3052160 | tf_op jit(solution)/shard_map/sub | solution.py:60
  157.2 5.1 %fusion.76 = f32[128,8,128]{2,0,1:T(8,128)S(1)} fusion(f32[640,128,8]{1,0,2:T(8,128)} %fusion.120, bf16[640,1024]{1,0:T(8,128)(2,1)} %select_dynamic-update-slice_fusion, f32[8,128,640]{1,2,0:T(8,128)} %get-tuple-element.26, f32[8,128]{1,0:T(8,128)S(1)} %get-tuple-element.25), kind=kOutput, calls=%fused_computation.95 | convolution fusion | flops 172361344 | bytes 11182080 | tf_op jit(solution)/shard_map/hqk,kd->qhd/dot_general | solution.py:68
  162.3 5.8 %fusion.73 = f32[128,8,128]{2,0,1:T(8,128)} fusion(f32[640,128,8]{1,0,2:T(8,128)} %fusion.121, bf16[640,1024]{1,0:T(8,128)(2,1)} %select_dynamic-update-slice_fusion, f32[8,128,640]{1,2,0:T(8,128)} %get-tuple-element.28, f32[8,128]{1,0:T(8,128)S(1)} %get-tuple-element.27), kind=kOutput, calls=%fused_computation.92 | convolution fusion | flops 172361344 | bytes 11182080 | tf_op jit(solution)/shard_map/hqk,kd->qhd/dot_general | solution.py:68
  168.1 5.9 %fusion.70 = f32[128,8,128]{2,0,1:T(8,128)} fusion(f32[640,128,8]{1,0,2:T(8,128)} %fusion.122, bf16[640,1024]{1,0:T(8,128)(2,1)} %select_dynamic-update-slice_fusion, f32[8,128,640]{1,2,0:T(8,128)} %get-tuple-element.30, f32[8,128]{1,0:T(8,128)S(1)} %get-tuple-element.29), kind=kOutput, calls=%fused_computation.89 | convolution fusion | flops 172361344 | bytes 11182080 | tf_op jit(solution)/shard_map/hqk,kd->qhd/dot_general | solution.py:68
  176.8 5.8 %fusion.107 = f32[640,1024]{1,0:T(8,128)} fusion(f32[640,1024]{1,0:T(8,128)} %fusion.109, bf16[128,8,128]{0,2,1:T(8,128)(2,1)} %bitcast.343, f32[640,128,8]{1,0,2:T(8,128)} %fusion.122, f32[8,128,640]{1,2,0:T(8,128)} %get-tuple-element.30, f32[8,128]{1,0:T(8,128)S(1)} %get-tuple-element.29), kind=kOutput, calls=%fused_computation.110 | convolution fusion | flops 172361344 | bytes 11083776 | tf_op jit(solution)/shard_map/hqk,qhd->kd/dot_general | solution.py:69
  182.6 5.7 %fusion.105 = f32[640,1024]{1,0:T(8,128)} fusion(f32[640,1024]{1,0:T(8,128)} %fusion.107, bf16[128,8,128]{0,2,1:T(8,128)(2,1)} %bitcast.341, f32[640,128,8]{1,0,2:T(8,128)} %fusion.121, f32[8,128,640]{1,2,0:T(8,128)} %get-tuple-element.28, f32[8,128]{1,0:T(8,128)S(1)} %get-tuple-element.27), kind=kOutput, calls=%fused_computation.108 | convolution fusion | flops 172361344 | bytes 11083776 | tf_op jit(solution)/shard_map/hqk,qhd->kd/dot_general | solution.py:69
  188.3 5.9 %fusion.103 = f32[640,1024]{1,0:T(8,128)} fusion(f32[640,1024]{1,0:T(8,128)} %fusion.105, bf16[128,8,128]{0,2,1:T(8,128)(2,1)} %bitcast.339, f32[640,128,8]{1,0,2:T(8,128)} %fusion.120, f32[8,128,640]{1,2,0:T(8,128)} %get-tuple-element.26, f32[8,128]{1,0:T(8,128)S(1)} %get-tuple-element.25), kind=kOutput, calls=%fused_computation.106 | convolution fusion | flops 172361344 | bytes 11083776 | tf_op jit(solution)/shard_map/hqk,qhd->kd/dot_general | solution.py:69
  194.2 3.1 %fusion.81 = f32[640,1024]{1,0:T(8,128)} fusion(f32[640,1024]{1,0:T(8,128)} %fusion.103, bf16[128,8,128]{0,2,1:T(8,128)(2,1)} %bitcast.333, f32[8,128,640]{1,2,0:T(8,128)} %get-tuple-element.32, f32[8,128]{1,0:T(8,128)S(1)} %get-tuple-element.31), kind=kOutput, calls=%fused_computation.98 | convolution fusion | flops 169082880 | bytes 3215360 | tf_op jit(solution)/shard_map/hqk,qhd->kd/dot_general | solution.py:70
  204.5 3.0 collective-permute-start.10
  210.8 3.0 collective-permute-start.6
  213.9 3.1 %fusion.36 = bf16[128,4096]{0,1:T(8,128)(2,1)} fusion(f32[128,1024]{0,1:T(8,128)S(1)} %bitcast.321, f32[128,1024]{0,1:T(8,128)S(1)} %bitcast.323, f32[128,1024]{0,1:T(8,128)S(1)} %bitcast.325, f32[128,1024]{0,1:T(8,128)S(1)} %bitcast.319, bf16[1,128,4096]{1,2,0:T(8,128)(2,1)S(1)} %copy.46, f32[128]{0:T(128)S(1)} %broadcast_multiply_fusion, ...), kind=kLoop, calls=%fused_computation.58 | loop fusion | flops 6291456 | bytes 5260288 | tf_op jit(solution)/shard_map/convert_element_type | solution.py:133
  223.3 21.5 %collective-permute-done.5 = bf16[128,4096]{0,1:T(8,128)(2,1)S(1)} collective-permute-done((bf16[128,4096]{0,1:T(8,128)(2,1)}, bf16[128,4096]{0,1:T(8,128)(2,1)S(1)}, u32[]{:S(2)}, u32[]{:S(2)}) %collective-permute-start.5) | collective-permute-done | bytes 1048608 | tf_op jit(solution)/shard_map/ppermute | solution.py:37
  246.2 33.5 %reduce-scatter.2.cloned.1.call-done = f32[8,1024]{1,0:T(8,128)} async-done(((f32[128,1024]{1,0:T(8,128)}), f32[8,1024]{1,0:T(8,128)}) %reduce-scatter.2.cloned.1.call-update) | async-done | bytes 32784 | tf_op jit(solution)/shard_map/reduce_scatter | solution.py:159
  280.4 20.1 %all_gather.3 = bf16[128,1024]{1,0:T(8,128)(2,1)S(1)} all-gather(bf16[8,1024]{1,0:T(8,128)(2,1)S(1)} %convert_element_type.83), channel_id=1, replica_groups=mesh['section'=2,'seq'=16] {'seq'}, dimensions={0}, use_global_device_ids=true | all-gather | bytes 278528 | tf_op jit(solution)/shard_map/all_gather | solution.py:160
  (90 shorter events, 48.2 us)
Async XLA Ops:
  7.2 16.4 %copy-start.2 = (bf16[1,128,4096]{2,1,0:T(8,128)(2,1)S(1)}, bf16[1,128,4096]{2,1,0:T(8,128)(2,1)}, u32[]{:S(2)}) copy-start(bf16[1,128,4096]{2,1,0:T(8,128)(2,1)} %param.6) | copy-start | bytes 3145732
  7.2 110.5 %all-reduce.2.cloned.1.call-start = ((), (), s32[]{:S(2)}) async-start(), calls=%async_computation.1 | async-start | bytes 524288 | tf_op jit(solution)/shard_map/psum | solution.py:25
  9.0 15.8 %copy-start.14 = (f32[1,4096]{1,0:T(1,128)S(1)}, f32[1,4096]{1,0:T(1,128)}, u32[]{:S(2)}) copy-start(f32[1,4096]{1,0:T(1,128)} %param.10) | copy-start | bytes 49156
  9.0 19.1 %collective-permute-start = (bf16[128,1024]{1,0:T(8,128)(2,1)}, bf16[128,1024]{1,0:T(8,128)(2,1)}, u32[]{:S(2)}, u32[]{:S(2)}) collective-permute-start(bf16[128,1024]{1,0:T(8,128)(2,1)} %pad_maximum_fusion), channel_id=1, source_target_pairs={{0,1},{1,2},{2,3},{3,4},{4,5},{5,6},{6,7},{7,8},{8,9},{9,10},{10,1... | collective-permute-start | bytes 786440 | tf_op jit(solution)/shard_map/ppermute | solution.py:17
  12.2 20.0 %collective-permute-start.1 = (bf16[128,1024]{1,0:T(8,128)(2,1)}, bf16[128,1024]{1,0:T(8,128)(2,1)}, u32[]{:S(2)}, u32[]{:S(2)}) collective-permute-start(bf16[128,1024]{1,0:T(8,128)(2,1)} %pad_maximum_fusion), channel_id=1, source_target_pairs={{1,0},{2,1},{3,2},{4,3},{5,4},{6,5},{7,6},{8,7},{9,8},{10,9},{11,1... | collective-permute-start | bytes 786440 | tf_op jit(solution)/shard_map/ppermute | solution.py:18
  13.5 105.9 %collective-permute-start.2 = (bf16[128,1024]{1,0:T(8,128)(2,1)}, bf16[128,1024]{1,0:T(8,128)(2,1)}, u32[]{:S(2)}, u32[]{:S(2)}) collective-permute-start(bf16[128,1024]{1,0:T(8,128)(2,1)} %pad_maximum_fusion), channel_id=1, source_target_pairs={{0,8},{1,9},{2,10},{3,11},{4,12},{5,13},{6,14},{7,15},{8,0},{9,1},... | collective-permute-start | bytes 786440 | tf_op jit(solution)/shard_map/ppermute | solution.py:31
  19.7 99.7 %collective-permute-start.3 = (bf16[128,1024]{1,0:T(8,128)(2,1)}, bf16[128,1024]{1,0:T(8,128)(2,1)}, u32[]{:S(2)}, u32[]{:S(2)}) collective-permute-start(bf16[128,1024]{1,0:T(8,128)(2,1)} %pad_maximum_fusion), channel_id=1, source_target_pairs={{0,4},{1,5},{2,6},{3,7},{4,0},{5,1},{6,2},{7,3},{8,12},{9,13},{10,... | collective-permute-start | bytes 786440 | tf_op jit(solution)/shard_map/ppermute | solution.py:31
  21.3 98.1 %collective-permute-start.4 = (bf16[128,1024]{1,0:T(8,128)(2,1)}, bf16[128,1024]{1,0:T(8,128)(2,1)}, u32[]{:S(2)}, u32[]{:S(2)}) collective-permute-start(bf16[128,1024]{1,0:T(8,128)(2,1)} %pad_maximum_fusion), channel_id=1, source_target_pairs={{0,2},{1,3},{2,0},{3,1},{4,6},{5,7},{6,4},{7,5},{8,10},{9,11},{10,... | collective-permute-start | bytes 786440 | tf_op jit(solution)/shard_map/ppermute | solution.py:31
  25.5 4.3 %copy-start.8 = (bf16[1,128,512]{2,1,0:T(8,128)(2,1)S(1)}, bf16[1,128,512]{2,1,0:T(8,128)(2,1)}, u32[]{:S(2)}) copy-start(bf16[1,128,512]{2,1,0:T(8,128)(2,1)} %param.9) | copy-start | bytes 393220
  28.1 93.1 %copy-start.7 = (bf16[128,1024]{0,1:T(8,128)(2,1)S(1)}, bf16[128,1024]{0,1:T(8,128)(2,1)}, u32[]{:S(2)}) copy-start(bf16[128,1024]{0,1:T(8,128)(2,1)} %get-tuple-element.17) | copy-start | bytes 786436
  30.7 93.4 %copy-start.13 = (bf16[128,1024]{0,1:T(8,128)(2,1)S(1)}, bf16[128,1024]{0,1:T(8,128)(2,1)}, u32[]{:S(2)}) copy-start(bf16[128,1024]{0,1:T(8,128)(2,1)} %get-tuple-element.13) | copy-start | bytes 786436
  30.7 249.0 %reduce-scatter.2.cloned.1.call-start = ((), (), s32[]{:S(2)}) async-start(), calls=%async_computation.2 | async-start | bytes 557056 | tf_op jit(solution)/shard_map/reduce_scatter | solution.py:159
  141.1 3.4 %copy-start.3 = (bf16[128,1024]{0,1:T(8,128)(2,1)S(1)}, bf16[128,1024]{0,1:T(8,128)(2,1)}, u32[]{:S(2)}) copy-start(bf16[128,1024]{0,1:T(8,128)(2,1)} %get-tuple-element.18) | copy-start | bytes 786436
  147.4 3.4 %copy-start.5 = (bf16[128,1024]{0,1:T(8,128)(2,1)S(1)}, bf16[128,1024]{0,1:T(8,128)(2,1)}, u32[]{:S(2)}) copy-start(bf16[128,1024]{0,1:T(8,128)(2,1)} %get-tuple-element.19) | copy-start | bytes 786436
  168.1 5.9 %copy-start.16 = (f32[128]{0:T(128)S(1)}, f32[128]{0:T(128)}, u32[]{:S(2)}) copy-start(f32[128]{0:T(128)} %copy-done.15) | copy-start | bytes 1540
  194.2 3.1 %copy-start.19 = (f32[8,128,640]{1,2,0:T(8,128)S(1)}, f32[8,128,640]{1,2,0:T(8,128)}, u32[]{:S(2)}) copy-start(f32[8,128,640]{1,2,0:T(8,128)} %get-tuple-element.30) | copy-start | bytes 7864324
  202.4 11.4 %copy-start = (f32[128,8,128]{2,0,1:T(8,128)S(1)}, f32[128,8,128]{2,0,1:T(8,128)}, u32[]{:S(2)}) copy-start(f32[128,8,128]{2,0,1:T(8,128)} %fusion.73) | copy-start | bytes 1572868
  202.4 11.5 %copy-start.1 = (f32[128,8,128]{2,0,1:T(8,128)S(1)}, f32[128,8,128]{2,0,1:T(8,128)}, u32[]{:S(2)}) copy-start(f32[128,8,128]{2,0,1:T(8,128)} %fusion.70) | copy-start | bytes 1572868
  204.5 15.0 %collective-permute-start.10 = (bf16[128,1024]{1,0:T(8,128)(2,1)S(1)}, bf16[128,1024]{1,0:T(8,128)(2,1)S(1)}, u32[]{:S(2)}, u32[]{:S(2)}) collective-permute-start(bf16[128,1024]{1,0:T(8,128)(2,1)S(1)} %get-tuple-element.10), channel_id=1, source_target_pairs={{0,8},{1,9},{2,10},{3,11},{4,12},{5,13},{6,14},{7,15},{8,0},{9,1},... | collective-permute-start | bytes 786440 | tf_op jit(solution)/shard_map/ppermute | solution.py:31
  207.5 13.5 %collective-permute-start.9 = (bf16[128,1024]{1,0:T(8,128)(2,1)S(1)}, bf16[128,1024]{1,0:T(8,128)(2,1)S(1)}, u32[]{:S(2)}, u32[]{:S(2)}) collective-permute-start(bf16[128,1024]{1,0:T(8,128)(2,1)S(1)} %get-tuple-element.9), channel_id=1, source_target_pairs={{0,4},{1,5},{2,6},{3,7},{4,0},{5,1},{6,2},{7,3},{8,12},{9,13},{10,... | collective-permute-start | bytes 786440 | tf_op jit(solution)/shard_map/ppermute | solution.py:31
  208.9 12.1 %collective-permute-start.8 = (bf16[128,1024]{1,0:T(8,128)(2,1)S(1)}, bf16[128,1024]{1,0:T(8,128)(2,1)S(1)}, u32[]{:S(2)}, u32[]{:S(2)}) collective-permute-start(bf16[128,1024]{1,0:T(8,128)(2,1)S(1)} %get-tuple-element.11), channel_id=1, source_target_pairs={{0,2},{1,3},{2,0},{3,1},{4,6},{5,7},{6,4},{7,5},{8,10},{9,11},{10,... | collective-permute-start | bytes 786440 | tf_op jit(solution)/shard_map/ppermute | solution.py:31
  209.5 11.5 %collective-permute-start.7 = (bf16[128,1024]{1,0:T(8,128)(2,1)S(1)}, bf16[128,1024]{1,0:T(8,128)(2,1)S(1)}, u32[]{:S(2)}, u32[]{:S(2)}) collective-permute-start(bf16[128,1024]{1,0:T(8,128)(2,1)S(1)} %get-tuple-element.12), channel_id=1, source_target_pairs={{1,0},{2,1},{3,2},{4,3},{5,4},{6,5},{7,6},{8,7},{9,8},{10,9},{11,1... | collective-permute-start | bytes 786440 | tf_op jit(solution)/shard_map/ppermute | solution.py:43
  210.8 10.2 %collective-permute-start.6 = (bf16[128,1024]{1,0:T(8,128)(2,1)S(1)}, bf16[128,1024]{1,0:T(8,128)(2,1)S(1)}, u32[]{:S(2)}, u32[]{:S(2)}) collective-permute-start(bf16[128,1024]{1,0:T(8,128)(2,1)S(1)} %get-tuple-element.8), channel_id=1, source_target_pairs={{0,1},{1,2},{2,3},{3,4},{4,5},{5,6},{6,7},{7,8},{8,9},{9,10},{10,1... | collective-permute-start | bytes 786440 | tf_op jit(solution)/shard_map/ppermute | solution.py:43
  219.5 25.3 %collective-permute-start.5 = (bf16[128,4096]{0,1:T(8,128)(2,1)}, bf16[128,4096]{0,1:T(8,128)(2,1)S(1)}, u32[]{:S(2)}, u32[]{:S(2)}) collective-permute-start(bf16[128,4096]{0,1:T(8,128)(2,1)} %fusion.36), channel_id=1, source_target_pairs={{16,0},{0,16},{17,1},{1,17},{18,2},{2,18},{19,3},{3,19},{20,4},{4,... | collective-permute-start | bytes 3145736 | tf_op jit(solution)/shard_map/ppermute | solution.py:37
  (9 other events, 20.5 us)
Sparse Core Ops, SparseCore 0:
  30.8 86.7 all-reduce.1
  223.4 56.1 reduce-scatter.1
where the time goes:
time: 309 us; the launch traced here: 308 us
  waiting for transfers between devices  141 us (46%)
  matrix products  77.2 us (25%)
  starting transfers between devices  23.7 us (8%)
  blocking collectives  20.1 us (7%)
  other arithmetic  16.7 us (5%)
  between operations  14.9 us (5%)
  local copies, waits for them, and re-layouts  14.1 us (5%)
    psum x1, waiting for transfers between devices, broadcast(): return lax.psum(kept, axis)  83.8 us
    reduce_scatter x1, waiting for transfers between devices, on_device(): lax.psum_scatter(combined, 'seq', scatter_dimension=0, tiled=True)  33.5 us
    dot_general x4, matrix products, group_terms(): jnp.einsum('hqk,qhd->kd', grad_low, query_heads, preferred_element_type=j...  23.1 us
    dot_general x4, matrix products, group_terms(): jnp.einsum('hqk,kd->qhd', grad_low, slot_keys, preferred_element_type=jnp...  21.9 us
    ppermute x1, waiting for transfers between devices, from_behind(): return lax.ppermute(block, axis, route)  21.5 us
    all_gather x1, blocking collectives, on_device(): whole = lax.all_gather(share, 'seq', axis=0, tiled=True)  20.1 us
    sub x4, matrix products, group_terms(): raised = jnp.exp(scores - row_peak)  13.6 us
    ppermute x6, starting transfers between devices, swapped(): return lax.ppermute(value, axis, pairs)  13.4 us
  transfers between devices with their start and end apart: 13, of which 4 were waited for; matrix products, arithmetic and copies ran while one was open for 6% of the time, Pallas kernels for 0%

commit v1 on v0

v1 whole, which is shorter than its diff:
```python
import functools
import math

import jax
import jax.numpy as jnp
from jax import lax
from jax.experimental import pallas as pl
from jax.experimental.pallas import tpu as pltpu
from jax.sharding import PartitionSpec as P

HD=128; NT=(((1,),(1,)),((),()))
NN=(((1,),(0,)),((),()))
TN=(((0,),(0,)),((),()))
def dot(a,b,dims): return lax.dot_general(a,b,dims,preferred_element_type=jnp.float32)

def kernel(U, n_partners, heads_per_group, info, stream, cot, gain, own, near, far, glob, *rest):
    partners=rest[:n_partners]
    handed, own_g, near_g, far_g, glob_g = rest[n_partners:n_partners+5]
    partners_g=rest[n_partners+5:2*n_partners+5]
    q, kall, kt, vall, dq, dk, dv = rest[2*n_partners+5:]
    rows, width = stream.shape
    groups=kall.shape[0]
    kvw=groups*HD
    factor=HD**-0.5
    c=factor*math.log2(math.e)
    me, count, want = info[0], info[1], info[2]
    odd = me % 2
    near_at = (1-odd)*2*rows
    far_at = odd*2*rows
    near_at=pl.multiple_of(near_at,rows); far_at=pl.multiple_of(far_at,rows)
    for g in range(groups):
        kc=slice(g*HD,(g+1)*HD); vc=slice(kvw+g*HD,kvw+(g+1)*HD)
        for dst, cols in ((kall,kc),(vall,vc)):
            dst[g, rows:2*rows, :]=own[:,cols]
            dst[g, pl.ds(near_at,rows), :]=near[:,cols]
            dst[g, pl.ds(far_at,rows), :]=far[:,cols]
            dst[g, 3*rows:4*rows, :]=glob[:,cols]
            for b in range(n_partners):
                @pl.when(want == (me ^ (2<<b)))
                def _():
                    dst[g, 4*rows:5*rows, :]=partners[b][:,cols]
        kt[g]=kall[g].astype(jnp.float32).T.astype(jnp.bfloat16)
    CH=512
    ss=jnp.zeros((rows,128),jnp.float32)
    for i in range(width//128):
        x=stream[:,i*128:(i+1)*128].astype(jnp.float32)
        ss=ss+x*x
    inv=lax.rsqrt(jnp.sum(ss,axis=1,keepdims=True)/width+1e-5)
    for i in range(width//CH):
        s=slice(i*CH,(i+1)*CH)
        q[:,s]=(stream[:,s].astype(jnp.float32)*inv*gain[:,s]).astype(jnp.bfloat16)
    dk[...]=jnp.zeros_like(dk); dv[...]=jnp.zeros_like(dv)
    big=jnp.float32(1e30)
    valid=(me>0, None, me<count-1, me>0, None)
    def one(g, off):
        o0=pl.multiple_of(off,2*HD)
        q2=jnp.concatenate([q[:,pl.ds(o0,HD)],q[:,pl.ds(pl.multiple_of(o0+HD,HD),HD)]],axis=0)
        do2=jnp.concatenate([cot[:,pl.ds(o0,HD)],cot[:,pl.ds(pl.multiple_of(o0+HD,HD),HD)]],axis=0)
        s=dot(kall[g],q2,NT)
        gw=dot(vall[g],do2,NT)
        m=None
        for j in range(5):
            mj=jnp.max(s[j*rows:(j+1)*rows],axis=0,keepdims=True)
            if valid[j] is not None: mj=jnp.where(valid[j],mj,-big)
            m = mj if m is None else jnp.maximum(m,mj)
        mc=m*c
        es=[]
        l=0.; t=0.
        for j in range(5):
            mj = mc if valid[j] is None else jnp.where(valid[j],mc,big)
            e=jnp.exp2(s[j*rows:(j+1)*rows]*c-mj)
            l=l+jnp.sum(e,axis=0,keepdims=True)
            t=t+jnp.sum(e*gw[j*rows:(j+1)*rows],axis=0,keepdims=True)
            es.append(e)
        r=1.0/l
        delta=t*r
        e=jnp.concatenate(es,axis=0)
        w=e*r
        wl=w.astype(jnp.bfloat16)
        ds=(w*((gw-delta)*factor)).astype(jnp.bfloat16)
        dv[g]+=dot(wl,do2,NN)
        dk[g]+=dot(ds,q2,NN)
        dqt=dot(kt[g],ds,NN)
        d2=dqt.T
        dq[:,pl.ds(o0,HD)]=d2[:rows]
        dq[:,pl.ds(pl.multiple_of(o0+HD,HD),HD)]=d2[rows:]
    pairs=heads_per_group//2
    per=pairs//U
    def body(i,_):
        g=i//per
        for u in range(U):
            one(g, (i*U+u)*2*HD)
        return 0
    if U==16:
        for i in range(groups*pairs): one(i//pairs, i*2*HD)
    else:
        lax.fori_loop(0,groups*per,body,0)
    for g in range(groups):
        kc=slice(g*HD,(g+1)*HD); vc=slice(kvw+g*HD,kvw+(g+1)*HD)
        for src, cols in ((dk,kc),(dv,vc)):
            own_g[:,cols]=src[g,rows:2*rows]
            near_g[:,cols]=src[g,pl.ds(near_at,rows)].astype(jnp.bfloat16)
            far_g[:,cols]=src[g,pl.ds(far_at,rows)].astype(jnp.bfloat16)
            glob_g[:,cols]=src[g,3*rows:4*rows]
            rt=src[g,4*rows:5*rows].astype(jnp.bfloat16)
            for b in range(n_partners):
                hit=want==(me^(2<<b))
                partners_g[b][:,cols]=jnp.where(hit,rt,jnp.zeros_like(rt))
    acc=jnp.zeros((rows,128),jnp.float32)
    for i in range(width//128):
        s=slice(i*128,(i+1)*128)
        acc=acc+dq[:,s]*gain[:,s]*stream[:,s].astype(jnp.float32)
    mean=jnp.sum(acc,axis=1,keepdims=True)*inv*(1.0/width)
    for i in range(width//CH):
        s=slice(i*CH,(i+1)*CH)
        normed=stream[:,s].astype(jnp.float32)*inv
        gh=inv*(dq[:,s]*gain[:,s]-normed*mean)
        handed[:,s]=(cot[:,s].astype(jnp.float32)+gh).astype(jnp.bfloat16)

def attend(info, stream, cot, gain, own, near, far, glob, partners, U=1):
    rows,width=stream.shape
    kvw=own.shape[1]//2
    groups=kvw//HD
    hpg=width//HD//groups
    npart=len(partners)
    V=pl.BlockSpec(memory_space=pltpu.VMEM)
    blk=jax.ShapeDtypeStruct((rows,2*kvw),jnp.bfloat16)
    blk32=jax.ShapeDtypeStruct((rows,2*kvw),jnp.float32)
    flops=5*2*width*5*rows*rows
    return pl.pallas_call(
        functools.partial(kernel,U,npart,hpg),
        out_shape=[jax.ShapeDtypeStruct((rows,width),jnp.bfloat16),blk32,blk,blk,blk32]+[blk]*npart,
        in_specs=[pl.BlockSpec(memory_space=pltpu.SMEM)]+[V]*(7+npart),
        out_specs=[V]*(5+npart),
        scratch_shapes=[pltpu.VMEM((rows,width),jnp.bfloat16),
            pltpu.VMEM((groups,5*rows,HD),jnp.bfloat16),
            pltpu.VMEM((groups,HD,5*rows),jnp.bfloat16),
            pltpu.VMEM((groups,5*rows,HD),jnp.bfloat16),
            pltpu.VMEM((rows,width),jnp.float32),
            pltpu.VMEM((groups,5*rows,HD),jnp.float32),
            pltpu.VMEM((groups,5*rows,HD),jnp.float32)],
        compiler_params=pltpu.CompilerParams(vmem_limit_bytes=48<<20),
        cost_estimate=pl.CostEstimate(flops=flops,bytes_accessed=8<<20,transcendentals=width*5*rows),
    )(info,stream,cot,gain,own,near,far,glob,*partners)


def permuted(value, pairs, axis="seq"):
    return lax.ppermute(value, axis, pairs)


def global_rounds(count):
    have = [0] + [1 << b for b in range(1, count.bit_length() - 1)]
    missing = [i for i in range(0, count, 2) if i not in have]
    rounds = []
    while missing:
        pairs = []
        for source in sorted(have, reverse=True):
            near = [t for t in missing if t not in [p[1] for p in pairs]]
            if near:
                best = min(near, key=lambda t: (bin(t ^ source).count("1"), abs(t - source)))
                pairs.append((source, best))
        rounds.append(pairs)
        have = have + [t for _, t in pairs]
        missing = [i for i in missing if i not in have]
    return rounds


def among(device, members):
    hit = device == members[0]
    for member in members[1:]:
        hit = hit | (device == member)
    return hit


def on_device(stream, cotangent, keys, values, gain, rand_blocks):
    hidden = stream[0]
    upstream = cotangent[0]
    kv_width = keys.shape[2]
    count = lax.axis_size("seq")
    bits = count.bit_length() - 1
    device = lax.axis_index("seq")
    own = jnp.concatenate([keys[0], values[0]], axis=1)
    swaps = [[(i, i ^ (1 << b)) for i in range(count)] for b in range(bits)]
    across = [(i, i + 1) for i in range(1, count - 1, 2)]
    across = across + [(j, i) for i, j in across]

    partners = [None] * bits
    for b in reversed(range(1, bits)):
        partners[b] = permuted(own, swaps[b])
    far = permuted(own, across)
    near = permuted(own, swaps[0])
    block0 = own
    for b in range(1, bits):
        block0 = jnp.where(device == (1 << b), partners[b], block0)
    for pairs in global_rounds(count):
        got = permuted(block0, pairs)
        block0 = jnp.where(among(device, [t for _, t in pairs]), got, block0)
    got = permuted(block0, [(i, i + 1) for i in range(0, count, 2)])
    block0 = jnp.where(device % 2 == 1, got, block0)

    info = jnp.stack([device, jnp.int32(count), rand_blocks[0, 0]])
    outs = attend(info, hidden, upstream, gain, own, near, far, block0, partners[1:], U=4)
    handed, own_g, near_g, far_g, glob_g = outs[:5]
    partners_g = outs[5:]

    sections = lax.axis_size("section")
    previous = permuted(handed, [((i + 1) % sections, i) for i in range(sections)], "section")
    acc = glob_g
    total = own_g
    for b in range(bits):
        pairs = [(i + (1 << b), i) for i in range(0, count, 2 << b)]
        got = permuted(acc.astype(jnp.bfloat16), pairs)
        acc = acc + got.astype(jnp.float32)
    for b in reversed(range(1, bits)):
        total = total + permuted(partners_g[b - 1], swaps[b]).astype(jnp.float32)
    total = total + permuted(far_g, across).astype(jnp.float32)
    total = total + permuted(near_g, swaps[0]).astype(jnp.float32)
    total = total + jnp.where(device == 0, acc, 0.0)
    total = total.astype(jnp.bfloat16)
    return (previous[None], total[:, :kv_width][None], total[:, kv_width:][None])


def solution(mesh):
    return jax.shard_map(
        on_device,
        mesh=mesh,
        in_specs=(
            P("section", "seq", None),
            P("section", "seq", None),
            P("section", "seq", None),
            P("section", "seq", None),
            P("section", None),
            P("seq", None),
        ),
        out_specs=(P("section", "seq", None), P("section", "seq", None), P("section", "seq", None)),
        check_vma=False,
    )
```

time: 309 us -> 110 us (0.36)
  waiting for transfers between devices: 141 us -> 43.6 us
  matrix products: 77.2 us -> 0 us
  blocking collectives: 20.1 us -> 0 us
  Pallas kernels: 0 us -> 17.9 us
  between operations: 14.9 us -> 1.48 us
  other arithmetic: 16.7 us -> 3.46 us
  starting transfers between devices: 23.7 us -> 35.3 us
  local copies, waits for them, and re-layouts: 14.1 us -> 6.32 us
    psum x1 -> x0, waiting for transfers between devices: 83.8 us -> none  [broadcast(): return lax.psum(kept, axis)]
    dot_general x16 -> x0, matrix products: 63.6 us -> none  [the longest x4 23.1 us: group_terms(): jnp.einsum('hqk,qhd->kd', grad_low, query_heads, preferred_element_type=j...]
    reduce_scatter x1 -> x0, waiting for transfers between devices: 33.5 us -> none  [on_device(): lax.psum_scatter(combined, 'seq', scatter_dimension=0, tiled=True)]
    all_gather x1 -> x0, blocking collectives: 20.1 us -> none  [on_device(): whole = lax.all_gather(share, 'seq', axis=0, tiled=True)]
    ppermute x11 -> x17, waiting for transfers between devices: 24.1 us -> 43.6 us  [permuted(): return lax.ppermute(value, axis, pairs)]
    pallas_call x0 -> x1, Pallas kernels: none -> 17.9 us  [attend(): pl.pallas_call(functools.partial(kernel, U, npart, hpg), out_shape=[jax.S...]
    sub x4 -> x0, matrix products: 13.6 us -> none  [group_terms(): raised = jnp.exp(scores - row_peak)]
    ppermute x11 -> x17, starting transfers between devices: 23.6 us -> 35.3 us  [permuted(): return lax.ppermute(value, axis, pairs)]
  transfers between devices with their start and end apart: 13 -> 17, of which waited for: 4 -> 9; matrix products, arithmetic and copies ran while one was open for 6% -> 3% of each run, Pallas kernels for 0% -> 0%
where the time goes in v1:
time: 110 us; the launch traced here: 108 us
  waiting for transfers between devices  43.6 us (40%)
  starting transfers between devices  35.3 us (32%)
  Pallas kernels  17.9 us (16%)
  local copies, waits for them, and re-layouts  6.32 us (6%)
  other arithmetic  3.46 us (3%)
  between operations  1.48 us (1%)
    ppermute x17, waiting for transfers between devices, permuted(): return lax.ppermute(value, axis, pairs)  43.6 us
    ppermute x17, starting transfers between devices, permuted(): return lax.ppermute(value, axis, pairs)  35.3 us
    pallas_call x1, Pallas kernels, attend(): pl.pallas_call(functools.partial(kernel, U, npart, hpg), out_shape=[jax.S...  17.9 us
    unnamed x17, local copies, waits for them, and re-layouts  5.6 us
  transfers between devices with their start and end apart: 17, of which 9 were waited for; matrix products, arithmetic and copies ran while one was open for 3% of the time, Pallas kernels for 0%

profile of v1, /device:TPU:0, one launch (start us, length us, event | category | flops | bytes accessed | tf_op | source)
XLA Modules:
  0.0 108.1 jit_solution(16225017453986657731)
XLA Ops:
  1.7 3.0 %collective-permute-start.4 = (bf16[128,1024]{1,0:T(8,128)(2,1)S(1)}, bf16[128,1024]{1,0:T(8,128)(2,1)S(1)}, u32[]{:S(2)}, u32[]{:S(2)}) collective-permute-start(bf16[128,1024]{1,0:T(8,128)(2,1)S(1)} %pad_maximum_fusion.own), channel_id=1, source_target_pairs={{0,2},{1,3},{2,0},{3,1},{4,6},{5,7},{6,4},{7,5},{8,10},{9,11},{10,... | collective-permute-start | bytes 786440 | tf_op jit(solution)/shard_map/ppermute | solution.py:148
  4.7 1.6 %collective-permute-start.3 = (bf16[128,1024]{1,0:T(8,128)(2,1)S(1)}, bf16[128,1024]{1,0:T(8,128)(2,1)S(1)}, u32[]{:S(2)}, u32[]{:S(2)}) collective-permute-start(bf16[128,1024]{1,0:T(8,128)(2,1)S(1)} %pad_maximum_fusion.own), channel_id=1, source_target_pairs={{0,4},{1,5},{2,6},{3,7},{4,0},{5,1},{6,2},{7,3},{8,12},{9,13},{10,... | collective-permute-start | bytes 786440 | tf_op jit(solution)/shard_map/ppermute | solution.py:148
  6.3 2.6 %collective-permute-start.2 = (bf16[128,1024]{1,0:T(8,128)(2,1)S(1)}, bf16[128,1024]{1,0:T(8,128)(2,1)S(1)}, u32[]{:S(2)}, u32[]{:S(2)}) collective-permute-start(bf16[128,1024]{1,0:T(8,128)(2,1)S(1)} %pad_maximum_fusion.own), channel_id=1, source_target_pairs={{0,8},{1,9},{2,10},{3,11},{4,12},{5,13},{6,14},{7,15},{8,0},{9,1},... | collective-permute-start | bytes 786440 | tf_op jit(solution)/shard_map/ppermute | solution.py:148
  8.9 2.1 %collective-permute-done.4.rest_0_ = bf16[128,1024]{1,0:T(8,128)(2,1)S(1)} collective-permute-done((bf16[128,1024]{1,0:T(8,128)(2,1)S(1)}, bf16[128,1024]{1,0:T(8,128)(2,1)S(1)}, u32[]{:S(2)}, u32[]{:S(2)}) %collective-permute-start.4) | collective-permute-done | bytes 262176 | tf_op jit(solution)/shard_map/ppermute | solution.py:148
  11.0 7.0 %collective-permute-done.3.rest_1_ = bf16[128,1024]{1,0:T(8,128)(2,1)S(1)} collective-permute-done((bf16[128,1024]{1,0:T(8,128)(2,1)S(1)}, bf16[128,1024]{1,0:T(8,128)(2,1)S(1)}, u32[]{:S(2)}, u32[]{:S(2)}) %collective-permute-start.3) | collective-permute-done | bytes 262176 | tf_op jit(solution)/shard_map/ppermute | solution.py:148
  18.0 2.4 %collective-permute-done.2.rest_2_ = bf16[128,1024]{1,0:T(8,128)(2,1)S(1)} collective-permute-done((bf16[128,1024]{1,0:T(8,128)(2,1)S(1)}, bf16[128,1024]{1,0:T(8,128)(2,1)S(1)}, u32[]{:S(2)}, u32[]{:S(2)}) %collective-permute-start.2) | collective-permute-done | bytes 262176 | tf_op jit(solution)/shard_map/ppermute | solution.py:148
  20.5 4.4 %collective-permute-start.5 = (bf16[128,1024]{1,0:T(8,128)(2,1)S(1)}, bf16[128,1024]{1,0:T(8,128)(2,1)S(1)}, u32[]{:S(2)}, u32[]{:S(2)}) collective-permute-start(bf16[128,1024]{1,0:T(8,128)(2,1)S(1)} %select_select_fusion), channel_id=1, source_target_pairs={{8,10},{4,6},{2,14},{0,12},{24,26},{20,22},{18,30},{16,28}} | collective-permute-start | bytes 786440 | tf_op jit(solution)/shard_map/ppermute | solution.py:148
  24.9 3.8 %collective-permute-done.5 = bf16[128,1024]{1,0:T(8,128)(2,1)S(1)} collective-permute-done((bf16[128,1024]{1,0:T(8,128)(2,1)S(1)}, bf16[128,1024]{1,0:T(8,128)(2,1)S(1)}, u32[]{:S(2)}, u32[]{:S(2)}) %collective-permute-start.5) | collective-permute-done | bytes 262176 | tf_op jit(solution)/shard_map/ppermute | solution.py:148
  28.8 1.3 %collective-permute-start.6 = (bf16[128,1024]{1,0:T(8,128)(2,1)S(1)}, bf16[128,1024]{1,0:T(8,128)(2,1)S(1)}, u32[]{:S(2)}, u32[]{:S(2)}) collective-permute-start(bf16[128,1024]{1,0:T(8,128)(2,1)S(1)} %broadcast_select_fusion), channel_id=1, source_target_pairs={{0,1},{2,3},{4,5},{6,7},{8,9},{10,11},{12,13},{14,15},{16,17},{18,... | collective-permute-start | bytes 786440 | tf_op jit(solution)/shard_map/ppermute | solution.py:148
  30.8 1.9 %collective-permute-start = (bf16[128,1024]{1,0:T(8,128)(2,1)S(1)}, bf16[128,1024]{1,0:T(8,128)(2,1)S(1)}, u32[]{:S(2)}, u32[]{:S(2)}) collective-permute-start(bf16[128,1024]{1,0:T(8,128)(2,1)S(1)} %pad_maximum_fusion.own), channel_id=1, source_target_pairs={{0,1},{1,0},{2,3},{3,2},{4,5},{5,4},{6,7},{7,6},{8,9},{9,8},{10,11... | collective-permute-start | bytes 786440 | tf_op jit(solution)/shard_map/ppermute | solution.py:148
  36.8 17.9 %shard_map.85 = (bf16[128,4096]{1,0:T(8,128)(2,1)S(1)}, f32[128,1024]{1,0:T(8,128)S(1)}, bf16[128,1024]{1,0:T(8,128)(2,1)S(1)}, bf16[128,1024]{1,0:T(8,128)(2,1)...) custom-call(s32[3]{0:T(128)S(1)} %pad_add_fusion.info, ...), custom_call_target="tpu_custom_call" | custom-call | flops 3355443200 | bytes 8388608 | tf_op jit(solution)/shard_map/pallas_call | solution.py:130
  56.0 4.3 %collective-permute-done.13 = bf16[128,1024]{1,0:T(8,128)(2,1)S(1)} collective-permute-done((bf16[128,1024]{1,0:T(8,128)(2,1)S(1)}, bf16[128,1024]{1,0:T(8,128)(2,1)S(1)}, u32[]{:S(2)}, u32[]{:S(2)}) %collective-permute-start.13) | collective-permute-done | bytes 262176 | tf_op jit(solution)/shard_map/ppermute | solution.py:148
  60.4 1.3 %collective-permute-start.14 = (bf16[128,1024]{1,0:T(8,128)(2,1)S(1)}, bf16[128,1024]{1,0:T(8,128)(2,1)S(1)}, u32[]{:S(2)}, u32[]{:S(2)}) collective-permute-start(bf16[128,1024]{1,0:T(8,128)(2,1)S(1)} %fusion), channel_id=1, source_target_pairs={{2,0},{6,4},{10,8},{14,12},{18,16},{22,20},{26,24},{30,28}} | collective-permute-start | bytes 786440 | tf_op jit(solution)/shard_map/ppermute | solution.py:148
  61.7 7.8 %collective-permute-done.14 = bf16[128,1024]{1,0:T(8,128)(2,1)S(1)} collective-permute-done((bf16[128,1024]{1,0:T(8,128)(2,1)S(1)}, bf16[128,1024]{1,0:T(8,128)(2,1)S(1)}, u32[]{:S(2)}, u32[]{:S(2)}) %collective-permute-start.14) | collective-permute-done | bytes 262176 | tf_op jit(solution)/shard_map/ppermute | solution.py:148
  69.6 1.3 %collective-permute-start.15 = (bf16[128,1024]{1,0:T(8,128)(2,1)S(1)}, bf16[128,1024]{1,0:T(8,128)(2,1)S(1)}, u32[]{:S(2)}, u32[]{:S(2)}) collective-permute-start(bf16[128,1024]{1,0:T(8,128)(2,1)S(1)} %fusion.2), channel_id=1, source_target_pairs={{4,0},{12,8},{20,16},{28,24}} | collective-permute-start | bytes 786440 | tf_op jit(solution)/shard_map/ppermute | solution.py:148
  70.9 2.3 %collective-permute-start.8 = (bf16[128,1024]{1,0:T(8,128)(2,1)S(1)}, bf16[128,1024]{1,0:T(8,128)(2,1)S(1)}, u32[]{:S(2)}, u32[]{:S(2)}) collective-permute-start(bf16[128,1024]{1,0:T(8,128)(2,1)S(1)} %get-tuple-element.13), channel_id=1, source_target_pairs={{0,8},{1,9},{2,10},{3,11},{4,12},{5,13},{6,14},{7,15},{8,0},{9,1},... | collective-permute-start | bytes 786440 | tf_op jit(solution)/shard_map/ppermute | solution.py:148
  73.2 6.9 %collective-permute-start.9 = (bf16[128,1024]{1,0:T(8,128)(2,1)S(1)}, bf16[128,1024]{1,0:T(8,128)(2,1)}, u32[]{:S(2)}, u32[]{:S(2)}) collective-permute-start(bf16[128,1024]{1,0:T(8,128)(2,1)S(1)} %get-tuple-element.14), channel_id=1, source_target_pairs={{0,4},{1,5},{2,6},{3,7},{4,0},{5,1},{6,2},{7,3},{8,12},{9,13},{10,... | collective-permute-start | bytes 786440 | tf_op jit(solution)/shard_map/ppermute | solution.py:148
  80.1 1.4 %collective-permute-start.11 = (bf16[128,1024]{1,0:T(8,128)(2,1)}, bf16[128,1024]{1,0:T(8,128)(2,1)}, u32[]{:S(2)}, u32[]{:S(2)}) collective-permute-start(bf16[128,1024]{1,0:T(8,128)(2,1)} %get-tuple-element.16), channel_id=1, source_target_pairs={{1,2},{3,4},{5,6},{7,8},{9,10},{11,12},{13,14},{2,1},{4,3},{6,5},{... | collective-permute-start | bytes 786440 | tf_op jit(solution)/shard_map/ppermute | solution.py:148
  81.5 1.5 %collective-permute-start.7 = (bf16[128,4096]{1,0:T(8,128)(2,1)S(1)}, bf16[128,4096]{1,0:T(8,128)(2,1)}, u32[]{:S(2)}, u32[]{:S(2)}) collective-permute-start(bf16[128,4096]{1,0:T(8,128)(2,1)S(1)} %get-tuple-element.11), channel_id=1, source_target_pairs={{16,0},{0,16},{17,1},{1,17},{18,2},{2,18},{19,3},{3,19},{20,4},{4,... | collective-permute-start | bytes 3145736 | tf_op jit(solution)/shard_map/ppermute | solution.py:148
  83.2 2.5 %collective-permute-start.12 = (bf16[128,1024]{1,0:T(8,128)(2,1)S(1)}, bf16[128,1024]{1,0:T(8,128)(2,1)}, u32[]{:S(2)}, u32[]{:S(2)}) collective-permute-start(bf16[128,1024]{1,0:T(8,128)(2,1)S(1)} %get-tuple-element.17), channel_id=1, source_target_pairs={{0,1},{1,0},{2,3},{3,2},{4,5},{5,4},{6,7},{7,6},{8,9},{9,8},{10,11... | collective-permute-start | bytes 786440 | tf_op jit(solution)/shard_map/ppermute | solution.py:148
  87.8 8.1 %collective-permute-done.16 = bf16[128,1024]{1,0:T(8,128)(2,1)} collective-permute-done((bf16[128,1024]{1,0:T(8,128)(2,1)S(1)}, bf16[128,1024]{1,0:T(8,128)(2,1)}, u32[]{:S(2)}, u32[]{:S(2)}) %collective-permute-start.16) | collective-permute-done | bytes 262176 | tf_op jit(solution)/shard_map/ppermute | solution.py:148
  95.9 1.8 %add_convert_fusion = bf16[128,1024]{1,0:T(8,128)(2,1)S(1)} fusion(bf16[128,1024]{1,0:T(8,128)(2,1)} %collective-permute-done.16, bf16[128,1024]{1,0:T(8,128)(2,1)} %collective-permute-done.12, bf16[128,1024]{1,0:T(8,128)(2,1)} %collective-permute-done.11, bf16[128,1024]{1,0:T(8,128)(2,1)} %collective-permute-done.10, ...), kind=kLoop, calls=%fused_computation | loop fusion | flops 2752512 | bytes 3670017 | tf_op jit(solution)/shard_map/convert_element_type | solution.py:219
  98.4 7.4 %collective-permute-done.7 = bf16[128,4096]{1,0:T(8,128)(2,1)} collective-permute-done((bf16[128,4096]{1,0:T(8,128)(2,1)S(1)}, bf16[128,4096]{1,0:T(8,128)(2,1)}, u32[]{:S(2)}, u32[]{:S(2)}) %collective-permute-start.7) | collective-permute-done | bytes 1048608 | tf_op jit(solution)/shard_map/ppermute | solution.py:148
  105.8 2.3 %copy.11 = bf16[1,128,4096]{2,1,0:T(8,128)(2,1)} copy(bf16[1,128,4096]{2,1,0:T(8,128)(2,1)} %bitcast.6) | data formatting | bytes 2097152
  (39 shorter events, 9.7 us)
Async XLA Ops:
  0.6 19.7 %copy-start.5 = (bf16[1,128,512]{2,1,0:T(8,128)(2,1)S(1)}, bf16[1,128,512]{2,1,0:T(8,128)(2,1)}, u32[]{:S(2)}) copy-start(bf16[1,128,512]{2,1,0:T(8,128)(2,1)} %param.9) | copy-start | bytes 393220
  0.6 19.7 %copy-start.6 = (bf16[1,128,512]{2,1,0:T(8,128)(2,1)S(1)}, bf16[1,128,512]{2,1,0:T(8,128)(2,1)}, u32[]{:S(2)}) copy-start(bf16[1,128,512]{2,1,0:T(8,128)(2,1)} %param.8) | copy-start | bytes 393220
  1.7 9.3 %collective-permute-start.4 = (bf16[128,1024]{1,0:T(8,128)(2,1)S(1)}, bf16[128,1024]{1,0:T(8,128)(2,1)S(1)}, u32[]{:S(2)}, u32[]{:S(2)}) collective-permute-start(bf16[128,1024]{1,0:T(8,128)(2,1)S(1)} %pad_maximum_fusion.own), channel_id=1, source_target_pairs={{0,2},{1,3},{2,0},{3,1},{4,6},{5,7},{6,4},{7,5},{8,10},{9,11},{10,... | collective-permute-start | bytes 786440 | tf_op jit(solution)/shard_map/ppermute | solution.py:148
  4.7 13.3 %collective-permute-start.3 = (bf16[128,1024]{1,0:T(8,128)(2,1)S(1)}, bf16[128,1024]{1,0:T(8,128)(2,1)S(1)}, u32[]{:S(2)}, u32[]{:S(2)}) collective-permute-start(bf16[128,1024]{1,0:T(8,128)(2,1)S(1)} %pad_maximum_fusion.own), channel_id=1, source_target_pairs={{0,4},{1,5},{2,6},{3,7},{4,0},{5,1},{6,2},{7,3},{8,12},{9,13},{10,... | collective-permute-start | bytes 786440 | tf_op jit(solution)/shard_map/ppermute | solution.py:148
  6.3 14.0 %collective-permute-start.2 = (bf16[128,1024]{1,0:T(8,128)(2,1)S(1)}, bf16[128,1024]{1,0:T(8,128)(2,1)S(1)}, u32[]{:S(2)}, u32[]{:S(2)}) collective-permute-start(bf16[128,1024]{1,0:T(8,128)(2,1)S(1)} %pad_maximum_fusion.own), channel_id=1, source_target_pairs={{0,8},{1,9},{2,10},{3,11},{4,12},{5,13},{6,14},{7,15},{8,0},{9,1},... | collective-permute-start | bytes 786440 | tf_op jit(solution)/shard_map/ppermute | solution.py:148
  20.5 8.3 %collective-permute-start.5 = (bf16[128,1024]{1,0:T(8,128)(2,1)S(1)}, bf16[128,1024]{1,0:T(8,128)(2,1)S(1)}, u32[]{:S(2)}, u32[]{:S(2)}) collective-permute-start(bf16[128,1024]{1,0:T(8,128)(2,1)S(1)} %select_select_fusion), channel_id=1, source_target_pairs={{8,10},{4,6},{2,14},{0,12},{24,26},{20,22},{18,30},{16,28}} | collective-permute-start | bytes 786440 | tf_op jit(solution)/shard_map/ppermute | solution.py:148
  28.8 4.7 %collective-permute-start.6 = (bf16[128,1024]{1,0:T(8,128)(2,1)S(1)}, bf16[128,1024]{1,0:T(8,128)(2,1)S(1)}, u32[]{:S(2)}, u32[]{:S(2)}) collective-permute-start(bf16[128,1024]{1,0:T(8,128)(2,1)S(1)} %broadcast_select_fusion), channel_id=1, source_target_pairs={{0,1},{2,3},{4,5},{6,7},{8,9},{10,11},{12,13},{14,15},{16,17},{18,... | collective-permute-start | bytes 786440 | tf_op jit(solution)/shard_map/ppermute | solution.py:148
  30.1 3.4 %collective-permute-start.1 = (bf16[128,1024]{1,0:T(8,128)(2,1)S(1)}, bf16[128,1024]{1,0:T(8,128)(2,1)S(1)}, u32[]{:S(2)}, u32[]{:S(2)}) collective-permute-start(bf16[128,1024]{1,0:T(8,128)(2,1)S(1)} %pad_maximum_fusion.own), channel_id=1, source_target_pairs={{1,2},{3,4},{5,6},{7,8},{9,10},{11,12},{13,14},{2,1},{4,3},{6,5},{... | collective-permute-start | bytes 786440 | tf_op jit(solution)/shard_map/ppermute | solution.py:148
  30.8 3.4 %collective-permute-start = (bf16[128,1024]{1,0:T(8,128)(2,1)S(1)}, bf16[128,1024]{1,0:T(8,128)(2,1)S(1)}, u32[]{:S(2)}, u32[]{:S(2)}) collective-permute-start(bf16[128,1024]{1,0:T(8,128)(2,1)S(1)} %pad_maximum_fusion.own), channel_id=1, source_target_pairs={{0,1},{1,0},{2,3},{3,2},{4,5},{5,4},{6,7},{7,6},{8,9},{9,8},{10,11... | collective-permute-start | bytes 786440 | tf_op jit(solution)/shard_map/ppermute | solution.py:148
  33.4 1.5 %copy-start.4 = (f32[1,4096]{1,0:T(1,128)S(1)}, f32[1,4096]{1,0:T(1,128)}, u32[]{:S(2)}) copy-start(f32[1,4096]{1,0:T(1,128)} %gain.1) | copy-start | bytes 49156
  33.5 0.7 copy-start
  34.9 1.0 copy-start.1
  35.9 0.9 copy-start.3
  54.7 5.6 %collective-permute-start.13 = (bf16[128,1024]{1,0:T(8,128)(2,1)S(1)}, bf16[128,1024]{1,0:T(8,128)(2,1)S(1)}, u32[]{:S(2)}, u32[]{:S(2)}) collective-permute-start(bf16[128,1024]{1,0:T(8,128)(2,1)S(1)} %convert_element_type.47), channel_id=1, source_target_pairs={{1,0},{3,2},{5,4},{7,6},{9,8},{11,10},{13,12},{15,14},{17,16},{19,... | collective-permute-start | bytes 786440 | tf_op jit(solution)/shard_map/ppermute | solution.py:148
  60.4 9.1 %collective-permute-start.14 = (bf16[128,1024]{1,0:T(8,128)(2,1)S(1)}, bf16[128,1024]{1,0:T(8,128)(2,1)S(1)}, u32[]{:S(2)}, u32[]{:S(2)}) collective-permute-start(bf16[128,1024]{1,0:T(8,128)(2,1)S(1)} %fusion), channel_id=1, source_target_pairs={{2,0},{6,4},{10,8},{14,12},{18,16},{22,20},{26,24},{30,28}} | collective-permute-start | bytes 786440 | tf_op jit(solution)/shard_map/ppermute | solution.py:148
  69.6 11.9 %collective-permute-start.15 = (bf16[128,1024]{1,0:T(8,128)(2,1)S(1)}, bf16[128,1024]{1,0:T(8,128)(2,1)S(1)}, u32[]{:S(2)}, u32[]{:S(2)}) collective-permute-start(bf16[128,1024]{1,0:T(8,128)(2,1)S(1)} %fusion.2), channel_id=1, source_target_pairs={{4,0},{12,8},{20,16},{28,24}} | collective-permute-start | bytes 786440 | tf_op jit(solution)/shard_map/ppermute | solution.py:148
  70.9 12.3 %collective-permute-start.8 = (bf16[128,1024]{1,0:T(8,128)(2,1)S(1)}, bf16[128,1024]{1,0:T(8,128)(2,1)S(1)}, u32[]{:S(2)}, u32[]{:S(2)}) collective-permute-start(bf16[128,1024]{1,0:T(8,128)(2,1)S(1)} %get-tuple-element.13), channel_id=1, source_target_pairs={{0,8},{1,9},{2,10},{3,11},{4,12},{5,13},{6,14},{7,15},{8,0},{9,1},... | collective-permute-start | bytes 786440 | tf_op jit(solution)/shard_map/ppermute | solution.py:148
  73.2 12.5 %collective-permute-start.9 = (bf16[128,1024]{1,0:T(8,128)(2,1)S(1)}, bf16[128,1024]{1,0:T(8,128)(2,1)}, u32[]{:S(2)}, u32[]{:S(2)}) collective-permute-start(bf16[128,1024]{1,0:T(8,128)(2,1)S(1)} %get-tuple-element.14), channel_id=1, source_target_pairs={{0,4},{1,5},{2,6},{3,7},{4,0},{5,1},{6,2},{7,3},{8,12},{9,13},{10,... | collective-permute-start | bytes 786440 | tf_op jit(solution)/shard_map/ppermute | solution.py:148
  80.1 7.6 %collective-permute-start.10 = (bf16[128,1024]{1,0:T(8,128)(2,1)}, bf16[128,1024]{1,0:T(8,128)(2,1)}, u32[]{:S(2)}, u32[]{:S(2)}) collective-permute-start(bf16[128,1024]{1,0:T(8,128)(2,1)} %get-tuple-element.15), channel_id=1, source_target_pairs={{0,2},{1,3},{2,0},{3,1},{4,6},{5,7},{6,4},{7,5},{8,10},{9,11},{10,... | collective-permute-start | bytes 786440 | tf_op jit(solution)/shard_map/ppermute | solution.py:148
  80.1 7.6 %collective-permute-start.11 = (bf16[128,1024]{1,0:T(8,128)(2,1)}, bf16[128,1024]{1,0:T(8,128)(2,1)}, u32[]{:S(2)}, u32[]{:S(2)}) collective-permute-start(bf16[128,1024]{1,0:T(8,128)(2,1)} %get-tuple-element.16), channel_id=1, source_target_pairs={{1,2},{3,4},{5,6},{7,8},{9,10},{11,12},{13,14},{2,1},{4,3},{6,5},{... | collective-permute-start | bytes 786440 | tf_op jit(solution)/shard_map/ppermute | solution.py:148
  81.5 24.3 %collective-permute-start.7 = (bf16[128,4096]{1,0:T(8,128)(2,1)S(1)}, bf16[128,4096]{1,0:T(8,128)(2,1)}, u32[]{:S(2)}, u32[]{:S(2)}) collective-permute-start(bf16[128,4096]{1,0:T(8,128)(2,1)S(1)} %get-tuple-element.11), channel_id=1, source_target_pairs={{16,0},{0,16},{17,1},{1,17},{18,2},{2,18},{19,3},{3,19},{20,4},{4,... | collective-permute-start | bytes 3145736 | tf_op jit(solution)/shard_map/ppermute | solution.py:148
  83.2 2.6 %copy-start.7 = (bf16[128,1024]{1,0:T(8,128)(2,1)}, bf16[128,1024]{1,0:T(8,128)(2,1)S(1)}, u32[]{:S(2)}) copy-start(bf16[128,1024]{1,0:T(8,128)(2,1)S(1)} %collective-permute-done.8) | copy-start | bytes 786436
  83.2 4.6 %collective-permute-start.12 = (bf16[128,1024]{1,0:T(8,128)(2,1)S(1)}, bf16[128,1024]{1,0:T(8,128)(2,1)}, u32[]{:S(2)}, u32[]{:S(2)}) collective-permute-start(bf16[128,1024]{1,0:T(8,128)(2,1)S(1)} %get-tuple-element.17), channel_id=1, source_target_pairs={{0,1},{1,0},{2,3},{3,2},{4,5},{5,4},{6,7},{7,6},{8,9},{9,8},{10,11... | collective-permute-start | bytes 786440 | tf_op jit(solution)/shard_map/ppermute | solution.py:148
  85.7 10.2 %collective-permute-start.16 = (bf16[128,1024]{1,0:T(8,128)(2,1)S(1)}, bf16[128,1024]{1,0:T(8,128)(2,1)}, u32[]{:S(2)}, u32[]{:S(2)}) collective-permute-start(bf16[128,1024]{1,0:T(8,128)(2,1)S(1)} %fusion.1), channel_id=1, source_target_pairs={{8,0},{24,16}} | collective-permute-start | bytes 786440 | tf_op jit(solution)/shard_map/ppermute | solution.py:148
  (1 other events, 0.7 us)

commit v2 on v1

v2 whole, which is shorter than its diff:
```python
import functools
import math

import jax
import jax.numpy as jnp
from jax import lax
from jax.experimental import pallas as pl
from jax.experimental.pallas import tpu as pltpu
from jax.sharding import PartitionSpec as P

HD = 128
BIG = 1e30
MEGA = 1 << 20
VM_SMALL = 16
VM_ATTEND = 28

NT = (((1,), (1,)), ((), ()))
NN = (((1,), (0,)), ((), ()))


def dot(a, b, dims):
    return lax.dot_general(a, b, dims, preferred_element_type=jnp.float32)


def cost(micros):
    return pl.CostEstimate(flops=int(micros * 1.15e9), bytes_accessed=MEGA, transcendentals=0)


def params(megas):
    return pltpu.CompilerParams(vmem_limit_bytes=megas * MEGA)


VMEM = pl.BlockSpec(memory_space=pltpu.VMEM)
SMEM = pl.BlockSpec(memory_space=pltpu.SMEM)


def prepare_kernel(partner_count, info, stream, gain, own, near, far, *rest):
    partners = rest[:partner_count]
    queries, inverse, slots, key_cols = rest[partner_count:]
    rows, width = stream.shape
    groups = key_cols.shape[0]
    me, want = info[0], info[2]
    odd = me % 2
    near_at = pl.multiple_of((1 - odd) * 2 * rows, rows)
    far_at = pl.multiple_of(odd * 2 * rows, rows)
    slots[rows : 2 * rows, :] = own[...]
    slots[pl.ds(near_at, rows), :] = near[...]
    slots[pl.ds(far_at, rows), :] = far[...]
    slots[3 * rows : 4 * rows, :] = partners[0][...]
    for b in range(1, partner_count):
        @pl.when(want == (me ^ (2 << b)))
        def _():
            slots[3 * rows : 4 * rows, :] = partners[b][...]
    for g in range(groups):
        key_cols[g] = slots[:, g * HD : (g + 1) * HD].T
    squares = jnp.zeros((rows, HD), jnp.float32)
    for i in range(width // HD):
        x = stream[:, i * HD : (i + 1) * HD].astype(jnp.float32)
        squares = squares + x * x
    inv = lax.rsqrt(jnp.sum(squares, axis=1, keepdims=True) / width + 1e-5)
    inv = jnp.broadcast_to(inv, (rows, HD))
    inverse[...] = inv
    for i in range(width // HD):
        s = slice(i * HD, (i + 1) * HD)
        queries[:, s] = (stream[:, s].astype(jnp.float32) * inv * gain[:, s]).astype(jnp.bfloat16)


def prepare(info, stream, gain, own, near, far, partners):
    rows, width = stream.shape
    kvw = own.shape[1] // 2
    groups = kvw // HD
    return pl.pallas_call(
        functools.partial(prepare_kernel, len(partners)),
        out_shape=[
            jax.ShapeDtypeStruct((rows, width), jnp.bfloat16),
            jax.ShapeDtypeStruct((rows, HD), jnp.float32),
            jax.ShapeDtypeStruct((4 * rows, 2 * kvw), jnp.bfloat16),
            jax.ShapeDtypeStruct((groups, HD, 4 * rows), jnp.bfloat16),
        ],
        in_specs=[SMEM] + [VMEM] * (5 + len(partners)),
        out_specs=[VMEM] * 4,
        compiler_params=params(VM_SMALL),
        cost_estimate=cost(6.0),
    )(info, stream, gain, own, near, far, *partners)


def attend_kernel(partner_count, info, stream, cot, gain, queries, inverse, slots, key_cols,
                  even_block, odd_block, *rest):
    handed, own_g, near_g, far_g, glob_g = rest[:5]
    partners_g = rest[5 : 5 + partner_count]
    dq, dk, dv, block, block_t, w0, d0, w1, d1 = rest[5 + partner_count :]
    rows, width = stream.shape
    groups = key_cols.shape[0]
    kvw = groups * HD
    heads = width // HD
    pairs = heads // groups // 2
    count = groups * pairs
    factor = HD**-0.5
    scale = factor * math.log2(math.e)
    me, devices, want = info[0], info[1], info[2]
    odd = me % 2
    valid = (me > 0, None, me < devices - 1, None, me > 0)
    block[...] = jnp.where(odd == 1, odd_block[...], even_block[...])
    for g in range(groups):
        block_t[g] = block[:, g * HD : (g + 1) * HD].T

    def stack(ref, i):
        at = 2 * i * HD
        return jnp.concatenate([ref[:, at : at + HD], ref[:, at + HD : at + 2 * HD]], axis=0)

    def weigh(i, low, grad):
        g = i // pairs
        kc = slice(g * HD, (g + 1) * HD)
        vc = slice(kvw + g * HD, kvw + (g + 1) * HD)
        q2, do2 = stack(queries, i), stack(cot, i)
        s4, g4 = dot(slots[:, kc], q2, NT), dot(slots[:, vc], do2, NT)
        s1, g1 = dot(block[:, kc], q2, NT), dot(block[:, vc], do2, NT)
        scores = [s4[j * rows : (j + 1) * rows] for j in range(4)] + [s1]
        gws = [g4[j * rows : (j + 1) * rows] for j in range(4)] + [g1]
        peak = jnp.max(scores[1], axis=0, keepdims=True)
        for j in (0, 2, 3, 4):
            top = jnp.max(scores[j], axis=0, keepdims=True)
            if valid[j] is not None:
                top = jnp.where(valid[j], top, -BIG)
            peak = jnp.maximum(peak, top)
        peak = peak * scale
        raised = []
        total = 0.0
        weighted = 0.0
        for j in range(5):
            shift = peak if valid[j] is None else jnp.where(valid[j], peak, BIG)
            e = jnp.exp2(scores[j] * scale - shift)
            total = total + jnp.sum(e, axis=0, keepdims=True)
            weighted = weighted + jnp.sum(e * gws[j], axis=0, keepdims=True)
            raised.append(e)
        share = 1.0 / total
        centre = weighted * share
        for j in range(5):
            w = raised[j] * share
            low[j * rows : (j + 1) * rows] = w.astype(jnp.bfloat16)
            grad[j * rows : (j + 1) * rows] = (w * ((gws[j] - centre) * factor)).astype(jnp.bfloat16)

    def spread(i, low, grad):
        g = i // pairs
        q2, do2 = stack(queries, i), stack(cot, i)
        value_part = dot(low[...], do2, NN)
        key_part = dot(grad[...], q2, NN)
        if i % pairs == 0:
            dv[g] = value_part
            dk[g] = key_part
        else:
            dv[g] += value_part
            dk[g] += key_part
        cols = dot(key_cols[g], grad[: 4 * rows], NN) + dot(block_t[g], grad[4 * rows :], NN)
        back = cols.T
        at = 2 * i * HD
        dq[:, at : at + HD] = back[:rows]
        dq[:, at + HD : at + 2 * HD] = back[rows:]

    buffers = ((w0, d0), (w1, d1))
    weigh(0, *buffers[0])
    for i in range(1, count):
        weigh(i, *buffers[i % 2])
        spread(i - 1, *buffers[(i - 1) % 2])
    spread(count - 1, *buffers[(count - 1) % 2])

    inv = inverse[...]
    products = jnp.zeros((rows, HD), jnp.float32)
    for i in range(width // HD):
        s = slice(i * HD, (i + 1) * HD)
        products = products + dq[:, s] * gain[:, s] * stream[:, s].astype(jnp.float32)
    mean = jnp.sum(products, axis=1, keepdims=True) * (1.0 / width) * inv
    pull = inv * inv * mean
    for i in range(width // HD):
        s = slice(i * HD, (i + 1) * HD)
        x = stream[:, s].astype(jnp.float32)
        grad_hidden = dq[:, s] * gain[:, s] * inv - x * pull
        handed[:, s] = (cot[:, s].astype(jnp.float32) + grad_hidden).astype(jnp.bfloat16)

    near_at = pl.multiple_of((1 - odd) * 2 * rows, rows)
    far_at = pl.multiple_of(odd * 2 * rows, rows)
    for g in range(groups):
        kc = slice(g * HD, (g + 1) * HD)
        vc = slice(kvw + g * HD, kvw + (g + 1) * HD)
        for source, cols in ((dk, kc), (dv, vc)):
            own_g[:, cols] = source[g, rows : 2 * rows]
            near_g[:, cols] = source[g, pl.ds(near_at, rows)].astype(jnp.bfloat16)
            far_g[:, cols] = source[g, pl.ds(far_at, rows)].astype(jnp.bfloat16)
            glob_g[:, cols] = source[g, 4 * rows : 5 * rows]
            term = source[g, 3 * rows : 4 * rows].astype(jnp.bfloat16)
            for b in range(partner_count):
                hit = want == (me ^ (2 << b))
                partners_g[b][:, cols] = jnp.where(hit, term, jnp.zeros_like(term))


def attend(info, stream, cot, gain, queries, inverse, slots, key_cols, even_block, odd_block, partner_count):
    rows, width = stream.shape
    groups = key_cols.shape[0]
    kvw = groups * HD
    low = jax.ShapeDtypeStruct((rows, 2 * kvw), jnp.bfloat16)
    wide = jax.ShapeDtypeStruct((rows, 2 * kvw), jnp.float32)
    return pl.pallas_call(
        functools.partial(attend_kernel, partner_count),
        out_shape=[jax.ShapeDtypeStruct((rows, width), jnp.bfloat16), wide, low, low, wide] + [low] * partner_count,
        in_specs=[SMEM] + [VMEM] * 9,
        out_specs=[VMEM] * (5 + partner_count),
        scratch_shapes=[
            pltpu.VMEM((rows, width), jnp.float32),
            pltpu.VMEM((groups, 5 * rows, HD), jnp.float32),
            pltpu.VMEM((groups, 5 * rows, HD), jnp.float32),
            pltpu.VMEM((rows, 2 * kvw), jnp.bfloat16),
            pltpu.VMEM((groups, HD, rows), jnp.bfloat16),
        ]
        + [pltpu.VMEM((5 * rows, 2 * rows), jnp.bfloat16)] * 4,
        compiler_params=params(VM_ATTEND),
        cost_estimate=cost(12.0),
    )(info, stream, cot, gain, queries, inverse, slots, key_cols, even_block, odd_block)


def collect_kernel(own, *rest):
    total = own[...]
    for ref in rest[:-1]:
        total = total + ref[...].astype(jnp.float32)
    rest[-1][...] = total


def collect(own, parts):
    return pl.pallas_call(
        collect_kernel,
        out_shape=jax.ShapeDtypeStruct(own.shape, jnp.float32),
        in_specs=[VMEM] * (1 + len(parts)),
        out_specs=VMEM,
        compiler_params=params(VM_SMALL),
        cost_estimate=cost(0.5),
    )(own, *parts)


def land_kernel(source, target):
    target[...] = source[...]


def land(rows):
    return pl.pallas_call(
        land_kernel,
        out_shape=jax.ShapeDtypeStruct(rows.shape, rows.dtype),
        in_specs=[VMEM],
        out_specs=VMEM,
        compiler_params=params(VM_SMALL),
        cost_estimate=cost(1.0),
    )(rows)


def finish_kernel(info, total, acc, got, keys, values):
    kvw = keys.shape[1]
    last = acc[...] + got[...].astype(jnp.float32)
    result = (total[...] + jnp.where(info[0] == 0, last, 0.0)).astype(jnp.bfloat16)
    keys[...] = result[:, :kvw]
    values[...] = result[:, kvw:]


def finish(info, total, acc, got):
    half = jax.ShapeDtypeStruct((total.shape[0], total.shape[1] // 2), jnp.bfloat16)
    return pl.pallas_call(
        finish_kernel,
        out_shape=[half, half],
        in_specs=[SMEM] + [VMEM] * 3,
        out_specs=[VMEM] * 2,
        compiler_params=params(VM_SMALL),
        cost_estimate=cost(0.5),
    )(info, total, acc, got)


def permuted(value, pairs, axis="seq"):
    return lax.ppermute(value, axis, pairs)


def global_rounds(count, have):
    missing = [i for i in range(0, count, 2) if i not in have]
    rounds = []
    while missing:
        pairs = []
        for source in sorted(have, reverse=True):
            free = [t for t in missing if t not in [p[1] for p in pairs]]
            if free:
                best = min(free, key=lambda t: (bin(t ^ source).count("1"), abs(t - source)))
                pairs.append((source, best))
        rounds.append(pairs)
        have = have + [t for _, t in pairs]
        missing = [i for i in missing if i not in have]
    return rounds


def among(device, members):
    hit = device == members[0]
    for member in members[1:]:
        hit = hit | (device == member)
    return hit


def on_device(stream, cotangent, keys, values, gain, rand_blocks):
    hidden = stream[0]
    upstream = cotangent[0]
    count = lax.axis_size("seq")
    bits = count.bit_length() - 1
    device = lax.axis_index("seq")
    own = jnp.concatenate([keys[0], values[0]], axis=1)
    swaps = [[(i, i ^ (1 << b)) for i in range(count)] for b in range(bits)]
    across = [(i, i + 1) for i in range(1, count - 1, 2)]
    across = across + [(j, i) for i, j in across]
    info = jnp.stack([device, jnp.int32(count), rand_blocks[0, 0]])

    top = count // 4 * 3
    partners = [None] * bits
    for b in reversed(range(2, bits)):
        partners[b] = permuted(own, swaps[b])
    block_top = permuted(own, [(0, top)])
    partners[1] = permuted(own, swaps[1])
    far = permuted(own, across)
    near = permuted(own, swaps[0])

    block0 = jnp.where(device == top, block_top, own)
    for b in range(1, bits):
        block0 = jnp.where(device == (1 << b), partners[b], block0)
    block0, far = lax.optimization_barrier((block0, far))
    for pairs in global_rounds(count, [0, top] + [1 << b for b in range(1, bits)]):
        moved = permuted(block0, pairs)
        block0 = jnp.where(among(device, [t for _, t in pairs]), moved, block0)
    odd_block = permuted(block0, [(i, i + 1) for i in range(0, count, 2)])
    queries, inverse, slots, key_cols = prepare(info, hidden, gain, own, near, far, partners[1:])
    outs = attend(info, hidden, upstream, gain, queries, inverse, slots, key_cols, block0, odd_block, bits - 1)
    handed, own_g, near_g, far_g, glob_g = outs[:5]
    partners_g = outs[5:]

    sections = lax.axis_size("section")
    back = [((i + 1) % sections, i) for i in range(sections)]
    previous = land(permuted(handed, back, "section"))
    parts = [permuted(near_g, swaps[0]), permuted(far_g, across)]
    parts = parts + [permuted(partners_g[b - 1], swaps[b]) for b in range(1, bits)]
    acc = glob_g
    for b in range(bits):
        pairs = [(i + (1 << b), i) for i in range(0, count, 2 << b)]
        last = permuted(acc.astype(jnp.bfloat16), pairs)
        if b < bits - 1:
            acc = acc + last.astype(jnp.float32)
    total = collect(own_g, parts)
    key_grads, value_grads = finish(info, total, acc, last)
    return (previous[None], key_grads[None], value_grads[None])


def solution(mesh):
    return jax.shard_map(
        on_device,
        mesh=mesh,
        in_specs=(
            P("section", "seq", None),
            P("section", "seq", None),
            P("section", "seq", None),
            P("section", "seq", None),
            P("section", None),
            P("seq", None),
        ),
        out_specs=(P("section", "seq", None), P("section", "seq", None), P("section", "seq", None)),
        check_vma=False,
    )
```

time: 110 us -> 81.6 us (0.74); the launches traced: 108 us -> 81.3 us
  waiting for transfers between devices: 43.6 us -> 33.5 us
  local copies, waits for them, and re-layouts: 6.32 us -> 0.02 us
  starting transfers between devices: 35.3 us -> 29.3 us
  Pallas kernels: 17.9 us -> 15.3 us
  other arithmetic: 3.46 us -> 1.7 us
    ppermute x17 -> x18, waiting for transfers between devices: 43.6 us -> 33.5 us  [permuted(): return lax.ppermute(value, axis, pairs)]
    ppermute x17 -> x18, starting transfers between devices: 35.3 us -> 29.3 us  [permuted(): return lax.ppermute(value, axis, pairs)]
    unnamed x17 -> x10, local copies, waits for them, and re-layouts: 5.6 us -> 0.02 us
    pallas_call x1 -> x5, Pallas kernels: 17.9 us -> 15.3 us  [the longest x1 11.4 us: attend(): pl.pallas_call(functools.partial(attend_kernel, partner_count), out_shape...]
    convert_element_type x5 -> x4, other arithmetic: 2.15 us -> 0.36 us  [on_device(): last = permuted(acc.astype(jnp.bfloat16), pairs)]
  transfers between devices with their start and end apart: 17 -> 18, of which waited for: 9 -> 8; matrix products, arithmetic and copies ran while one was open for 3% -> 1% of each run, Pallas kernels for 0% -> 3%
where the time goes in v2:
time: 81.6 us; the launch traced here: 81.3 us
  waiting for transfers between devices  33.5 us (41%)
  starting transfers between devices  29.3 us (36%)
  Pallas kernels  15.3 us (19%)
  other arithmetic  1.7 us (2%)
  between operations  1.56 us (2%)
    ppermute x18, waiting for transfers between devices, permuted(): return lax.ppermute(value, axis, pairs)  33.5 us
    ppermute x18, starting transfers between devices, permuted(): return lax.ppermute(value, axis, pairs)  29.3 us
    pallas_call x1, Pallas kernels, attend(): pl.pallas_call(functools.partial(attend_kernel, partner_count), out_shape...  11.4 us
  transfers between devices with their start and end apart: 18, of which 8 were waited for; matrix products, arithmetic and copies ran while one was open for 1% of the time, Pallas kernels for 3%

profile of v2, /device:TPU:0, one launch (start us, length us, event | category | flops | bytes accessed | tf_op | source)
XLA Modules:
  0.0 81.3 jit_solution(4373912255835991035)
XLA Ops:
  0.7 1.0 %pad_maximum_fusion.own = bf16[128,1024]{1,0:T(8,128)(2,1)S(1)} fusion(bf16[128,512]{1,0:T(8,128)(2,1)} %bitcast.13, bf16[128,512]{1,0:T(8,128)(2,1)} %bitcast.15), kind=kLoop, calls=%fused_computation.4 | loop fusion | flops 524288 | bytes 524288 | tf_op jit(solution)/shard_map/concatenate | solution.py:306
  1.7 7.0 %collective-permute-start.4 = (bf16[128,1024]{1,0:T(8,128)(2,1)S(1)}, bf16[128,1024]{1,0:T(8,128)(2,1)S(1)}, u32[]{:S(2)}, u32[]{:S(2)}) collective-permute-start(bf16[128,1024]{1,0:T(8,128)(2,1)S(1)} %pad_maximum_fusion.own), channel_id=1, source_target_pairs={{0,12},{16,28}} | collective-permute-start | bytes 786440 | tf_op jit(solution)/shard_map/ppermute | solution.py:274
  8.8 0.7 collective-permute-start.1
  10.3 4.9 %collective-permute-done.4 = bf16[128,1024]{1,0:T(8,128)(2,1)S(1)} collective-permute-done((bf16[128,1024]{1,0:T(8,128)(2,1)S(1)}, bf16[128,1024]{1,0:T(8,128)(2,1)S(1)}, u32[]{:S(2)}, u32[]{:S(2)}) %collective-permute-start.4) | collective-permute-done | bytes 262176 | tf_op jit(solution)/shard_map/ppermute | solution.py:274
  15.1 2.8 %collective-permute-done.2.rest_1_ = bf16[128,1024]{1,0:T(8,128)(2,1)S(1)} collective-permute-done((bf16[128,1024]{1,0:T(8,128)(2,1)S(1)}, bf16[128,1024]{1,0:T(8,128)(2,1)S(1)}, u32[]{:S(2)}, u32[]{:S(2)}) %collective-permute-start.2) | collective-permute-done | bytes 262176 | tf_op jit(solution)/shard_map/ppermute | solution.py:274
  17.9 3.8 %collective-permute-done.1.rest_2_ = bf16[128,1024]{1,0:T(8,128)(2,1)S(1)} collective-permute-done((bf16[128,1024]{1,0:T(8,128)(2,1)S(1)}, bf16[128,1024]{1,0:T(8,128)(2,1)S(1)}, u32[]{:S(2)}, u32[]{:S(2)}) %collective-permute-start.1) | collective-permute-done | bytes 262176 | tf_op jit(solution)/shard_map/ppermute | solution.py:274
  22.0 0.7 collective-permute-start.6
  23.5 2.4 %collective-permute-start.7 = (bf16[128,1024]{1,0:T(8,128)(2,1)S(1)}, bf16[128,1024]{1,0:T(8,128)(2,1)S(1)}, u32[]{:S(2)}, u32[]{:S(2)}) collective-permute-start(bf16[128,1024]{1,0:T(8,128)(2,1)S(1)} %broadcast_select_fusion.even_block), channel_id=1, source_target_pairs={{0,1},{2,3},{4,5},{6,7},{8,9},{10,11},{12,13},{14,15},{16,17},{18,... | collective-permute-start | bytes 786440 | tf_op jit(solution)/shard_map/ppermute | solution.py:274
  26.0 1.3 %shard_map.85 = (bf16[128,4096]{1,0:T(8,128)(2,1)S(1)}, f32[128,128]{1,0:T(8,128)S(1)}, bf16[512,1024]{1,0:T(8,128)(2,1)S(1)}, bf16[4,128,512]{2,1,0:T(8,128)(2,1)S(1)}) custom-call(s32[3]{0:T(128)S(1)} %pad_add_fusion.info, bf16[128,4096]{1,0:T(8,128)(2,1)S(1)} %bitcast.10, f32[1,4096]{1,0:T(1,128)S(1)} %copy-done.2, ...), custom_call_target="tpu_custom_call" | custom-call | flops 6899999744 | bytes 1048576 | tf_op jit(solution)/shard_map/pallas_call | solution.py:72
  27.3 11.4 %shard_map.86 = (bf16[128,4096]{1,0:T(8,128)(2,1)S(1)}, f32[128,1024]{1,0:T(8,128)S(1)}, bf16[128,1024]{1,0:T(8,128)(2,1)S(1)}, bf16[128,1024]{1,0:T(8,128)(2,1)...) custom-call(s32[3]{0:T(128)S(1)} %pad_add_fusion.info, ...), custom_call_target="tpu_custom_call" | custom-call | flops 13799999488 | bytes 1048576 | tf_op jit(solution)/shard_map/pallas_call | solution.py:202
  38.8 1.3 %collective-permute-start.14 = (bf16[128,1024]{1,0:T(8,128)(2,1)S(1)}, bf16[128,1024]{1,0:T(8,128)(2,1)S(1)}, u32[]{:S(2)}, u32[]{:S(2)}) collective-permute-start(bf16[128,1024]{1,0:T(8,128)(2,1)S(1)} %convert_element_type.21), channel_id=1, source_target_pairs={{1,0},{3,2},{5,4},{7,6},{9,8},{11,10},{13,12},{15,14},{17,16},{19,... | collective-permute-start | bytes 786440 | tf_op jit(solution)/shard_map/ppermute | solution.py:274
  40.1 2.1 %collective-permute-done.14 = bf16[128,1024]{1,0:T(8,128)(2,1)S(1)} collective-permute-done((bf16[128,1024]{1,0:T(8,128)(2,1)S(1)}, bf16[128,1024]{1,0:T(8,128)(2,1)S(1)}, u32[]{:S(2)}, u32[]{:S(2)}) %collective-permute-start.14) | collective-permute-done | bytes 262176 | tf_op jit(solution)/shard_map/ppermute | solution.py:274
  42.3 1.3 %collective-permute-start.15 = (bf16[128,1024]{1,0:T(8,128)(2,1)S(1)}, bf16[128,1024]{1,0:T(8,128)(2,1)S(1)}, u32[]{:S(2)}, u32[]{:S(2)}) collective-permute-start(bf16[128,1024]{1,0:T(8,128)(2,1)S(1)} %fusion), channel_id=1, source_target_pairs={{2,0},{6,4},{10,8},{14,12},{18,16},{22,20},{26,24},{30,28}} | collective-permute-start | bytes 786440 | tf_op jit(solution)/shard_map/ppermute | solution.py:274
  43.6 1.6 %collective-permute-start.8 = (bf16[128,4096]{1,0:T(8,128)(2,1)S(1)}, bf16[128,4096]{1,0:T(8,128)(2,1)S(1)}, u32[]{:S(2)}, u32[]{:S(2)}) collective-permute-start(bf16[128,4096]{1,0:T(8,128)(2,1)S(1)} %get-tuple-element.25), channel_id=1, source_target_pairs={{16,0},{0,16},{17,1},{1,17},{18,2},{2,18},{19,3},{3,19},{20,4},{4,... | collective-permute-start | bytes 3145736 | tf_op jit(solution)/shard_map/ppermute | solution.py:274
  45.1 5.4 %collective-permute-done.15 = bf16[128,1024]{1,0:T(8,128)(2,1)S(1)} collective-permute-done((bf16[128,1024]{1,0:T(8,128)(2,1)S(1)}, bf16[128,1024]{1,0:T(8,128)(2,1)S(1)}, u32[]{:S(2)}, u32[]{:S(2)}) %collective-permute-start.15) | collective-permute-done | bytes 262176 | tf_op jit(solution)/shard_map/ppermute | solution.py:274
  50.7 1.3 %collective-permute-start.16 = (bf16[128,1024]{1,0:T(8,128)(2,1)S(1)}, bf16[128,1024]{1,0:T(8,128)(2,1)S(1)}, u32[]{:S(2)}, u32[]{:S(2)}) collective-permute-start(bf16[128,1024]{1,0:T(8,128)(2,1)S(1)} %fusion.1), channel_id=1, source_target_pairs={{4,0},{12,8},{20,16},{28,24}} | collective-permute-start | bytes 786440 | tf_op jit(solution)/shard_map/ppermute | solution.py:274
  52.9 5.5 %collective-permute-start.12 = (bf16[128,1024]{1,0:T(8,128)(2,1)S(1)}, bf16[128,1024]{1,0:T(8,128)(2,1)S(1)}, u32[]{:S(2)}, u32[]{:S(2)}) collective-permute-start(bf16[128,1024]{1,0:T(8,128)(2,1)S(1)} %get-tuple-element.30), channel_id=1, source_target_pairs={{0,4},{1,5},{2,6},{3,7},{4,0},{5,1},{6,2},{7,3},{8,12},{9,13},{10,... | collective-permute-start | bytes 786440 | tf_op jit(solution)/shard_map/ppermute | solution.py:274
  58.3 2.2 %collective-permute-done.16 = bf16[128,1024]{1,0:T(8,128)(2,1)S(1)} collective-permute-done((bf16[128,1024]{1,0:T(8,128)(2,1)S(1)}, bf16[128,1024]{1,0:T(8,128)(2,1)S(1)}, u32[]{:S(2)}, u32[]{:S(2)}) %collective-permute-start.16) | collective-permute-done | bytes 262176 | tf_op jit(solution)/shard_map/ppermute | solution.py:274
  60.6 4.5 %collective-permute-start.13 = (bf16[128,1024]{1,0:T(8,128)(2,1)S(1)}, bf16[128,1024]{1,0:T(8,128)(2,1)S(1)}, u32[]{:S(2)}, u32[]{:S(2)}) collective-permute-start(bf16[128,1024]{1,0:T(8,128)(2,1)S(1)} %get-tuple-element.31), channel_id=1, source_target_pairs={{0,8},{1,9},{2,10},{3,11},{4,12},{5,13},{6,14},{7,15},{8,0},{9,1},... | collective-permute-start | bytes 786440 | tf_op jit(solution)/shard_map/ppermute | solution.py:274
  65.2 1.3 %collective-permute-start.17 = (bf16[128,1024]{1,0:T(8,128)(2,1)S(1)}, bf16[128,1024]{1,0:T(8,128)(2,1)S(1)}, u32[]{:S(2)}, u32[]{:S(2)}) collective-permute-start(bf16[128,1024]{1,0:T(8,128)(2,1)S(1)} %get-tuple-element.35), channel_id=1, source_target_pairs={{8,0},{24,16}} | collective-permute-start | bytes 786440 | tf_op jit(solution)/shard_map/ppermute | solution.py:274
  66.5 9.6 %collective-permute-done.12.rest_3_ = bf16[128,1024]{1,0:T(8,128)(2,1)S(1)} collective-permute-done((bf16[128,1024]{1,0:T(8,128)(2,1)S(1)}, bf16[128,1024]{1,0:T(8,128)(2,1)S(1)}, u32[]{:S(2)}, u32[]{:S(2)}) %collective-permute-start.12) | collective-permute-done | bytes 262176 | tf_op jit(solution)/shard_map/ppermute | solution.py:274
  76.3 1.0 %shard_map.87 = bf16[128,4096]{1,0:T(8,128)(2,1)} custom-call(bf16[128,4096]{1,0:T(8,128)(2,1)S(1)} %collective-permute-done.8.source), custom_call_target="tpu_custom_call" | custom-call | flops 1150000000 | bytes 1048576 | tf_op jit(solution)/shard_map/pallas_call | solution.py:243
  77.4 2.6 %collective-permute-done.17.got = bf16[128,1024]{1,0:T(8,128)(2,1)S(1)} collective-permute-done((bf16[128,1024]{1,0:T(8,128)(2,1)S(1)}, bf16[128,1024]{1,0:T(8,128)(2,1)S(1)}, u32[]{:S(2)}, u32[]{:S(2)}) %collective-permute-start.17) | collective-permute-done | bytes 262176 | tf_op jit(solution)/shard_map/ppermute | solution.py:274
  80.0 1.3 %shard_map.89 = (bf16[128,512]{1,0:T(8,128)(2,1)}, bf16[128,512]{1,0:T(8,128)(2,1)}) custom-call(s32[3]{0:T(128)S(1)} %pad_add_fusion.info, f32[128,1024]{1,0:T(8,128)S(1)} %shard_map.88.total, f32[128,1024]{1,0:T(8,128)S(1)} %get-tuple-element.36.acc, bf16[128,1024]{1,0:T(8,128)(2,1)S(1)} %collective-permute-done.17.got), custom_call_target="tpu_custom_call" | custom-call | flops 575000000 | bytes 1048576 | tf_op jit(solution)/shard_map/pallas_call | solution.py:263
  (35 shorter events, 2.7 us)
Async XLA Ops:
  0.6 21.1 %copy-start.3 = (bf16[1,128,512]{2,1,0:T(8,128)(2,1)S(1)}, bf16[1,128,512]{2,1,0:T(8,128)(2,1)}, u32[]{:S(2)}) copy-start(bf16[1,128,512]{2,1,0:T(8,128)(2,1)} %param.9) | copy-start | bytes 393220
  0.6 21.1 %copy-start.4 = (bf16[1,128,512]{2,1,0:T(8,128)(2,1)S(1)}, bf16[1,128,512]{2,1,0:T(8,128)(2,1)}, u32[]{:S(2)}) copy-start(bf16[1,128,512]{2,1,0:T(8,128)(2,1)} %param.8) | copy-start | bytes 393220
  1.7 13.4 %collective-permute-start.4 = (bf16[128,1024]{1,0:T(8,128)(2,1)S(1)}, bf16[128,1024]{1,0:T(8,128)(2,1)S(1)}, u32[]{:S(2)}, u32[]{:S(2)}) collective-permute-start(bf16[128,1024]{1,0:T(8,128)(2,1)S(1)} %pad_maximum_fusion.own), channel_id=1, source_target_pairs={{0,12},{16,28}} | collective-permute-start | bytes 786440 | tf_op jit(solution)/shard_map/ppermute | solution.py:274
  8.7 6.5 %collective-permute-start.3 = (bf16[128,1024]{1,0:T(8,128)(2,1)S(1)}, bf16[128,1024]{1,0:T(8,128)(2,1)S(1)}, u32[]{:S(2)}, u32[]{:S(2)}) collective-permute-start(bf16[128,1024]{1,0:T(8,128)(2,1)S(1)} %pad_maximum_fusion.own), channel_id=1, source_target_pairs={{0,2},{1,3},{2,0},{3,1},{4,6},{5,7},{6,4},{7,5},{8,10},{9,11},{10,... | collective-permute-start | bytes 786440 | tf_op jit(solution)/shard_map/ppermute | solution.py:274
  8.7 9.2 %collective-permute-start.2 = (bf16[128,1024]{1,0:T(8,128)(2,1)S(1)}, bf16[128,1024]{1,0:T(8,128)(2,1)S(1)}, u32[]{:S(2)}, u32[]{:S(2)}) collective-permute-start(bf16[128,1024]{1,0:T(8,128)(2,1)S(1)} %pad_maximum_fusion.own), channel_id=1, source_target_pairs={{0,4},{1,5},{2,6},{3,7},{4,0},{5,1},{6,2},{7,3},{8,12},{9,13},{10,... | collective-permute-start | bytes 786440 | tf_op jit(solution)/shard_map/ppermute | solution.py:274
  8.8 13.0 %collective-permute-start.1 = (bf16[128,1024]{1,0:T(8,128)(2,1)S(1)}, bf16[128,1024]{1,0:T(8,128)(2,1)S(1)}, u32[]{:S(2)}, u32[]{:S(2)}) collective-permute-start(bf16[128,1024]{1,0:T(8,128)(2,1)S(1)} %pad_maximum_fusion.own), channel_id=1, source_target_pairs={{0,8},{1,9},{2,10},{3,11},{4,12},{5,13},{6,14},{7,15},{8,0},{9,1},... | collective-permute-start | bytes 786440 | tf_op jit(solution)/shard_map/ppermute | solution.py:274
  9.6 12.4 %collective-permute-start.5 = (bf16[128,1024]{1,0:T(8,128)(2,1)S(1)}, bf16[128,1024]{1,0:T(8,128)(2,1)S(1)}, u32[]{:S(2)}, u32[]{:S(2)}) collective-permute-start(bf16[128,1024]{1,0:T(8,128)(2,1)S(1)} %pad_maximum_fusion.own), channel_id=1, source_target_pairs={{1,2},{3,4},{5,6},{7,8},{9,10},{11,12},{13,14},{2,1},{4,3},{6,5},{... | collective-permute-start | bytes 786440 | tf_op jit(solution)/shard_map/ppermute | solution.py:274
  10.3 15.7 %copy-start = (bf16[1,128,4096]{2,1,0:T(8,128)(2,1)S(1)}, bf16[1,128,4096]{2,1,0:T(8,128)(2,1)}, u32[]{:S(2)}) copy-start(bf16[1,128,4096]{2,1,0:T(8,128)(2,1)} %param.6) | copy-start | bytes 3145732
  22.0 1.5 %collective-permute-start.6 = (bf16[128,1024]{1,0:T(8,128)(2,1)S(1)}, bf16[128,1024]{1,0:T(8,128)(2,1)S(1)}, u32[]{:S(2)}, u32[]{:S(2)}) collective-permute-start(bf16[128,1024]{1,0:T(8,128)(2,1)S(1)} %select_select_fusion), channel_id=1, source_target_pairs={{12,14},{8,10},{4,6},{28,30},{24,26},{20,22}} | collective-permute-start | bytes 786440 | tf_op jit(solution)/shard_map/ppermute | solution.py:274
  22.7 3.3 %collective-permute-start = (bf16[128,1024]{1,0:T(8,128)(2,1)S(1)}, bf16[128,1024]{1,0:T(8,128)(2,1)S(1)}, u32[]{:S(2)}, u32[]{:S(2)}) collective-permute-start(bf16[128,1024]{1,0:T(8,128)(2,1)S(1)} %pad_maximum_fusion.own), channel_id=1, source_target_pairs={{0,1},{1,0},{2,3},{3,2},{4,5},{5,4},{6,7},{7,6},{8,9},{9,8},{10,11... | collective-permute-start | bytes 786440 | tf_op jit(solution)/shard_map/ppermute | solution.py:274
  23.5 2.5 %copy-start.2 = (f32[1,4096]{1,0:T(1,128)S(1)}, f32[1,4096]{1,0:T(1,128)}, u32[]{:S(2)}) copy-start(f32[1,4096]{1,0:T(1,128)} %gain.3) | copy-start | bytes 49156
  23.5 3.8 %collective-permute-start.7 = (bf16[128,1024]{1,0:T(8,128)(2,1)S(1)}, bf16[128,1024]{1,0:T(8,128)(2,1)S(1)}, u32[]{:S(2)}, u32[]{:S(2)}) collective-permute-start(bf16[128,1024]{1,0:T(8,128)(2,1)S(1)} %broadcast_select_fusion.even_block), channel_id=1, source_target_pairs={{0,1},{2,3},{4,5},{6,7},{8,9},{10,11},{12,13},{14,15},{16,17},{18,... | collective-permute-start | bytes 786440 | tf_op jit(solution)/shard_map/ppermute | solution.py:274
  26.0 1.3 %copy-start.1 = (bf16[1,128,4096]{2,1,0:T(8,128)(2,1)S(1)}, bf16[1,128,4096]{2,1,0:T(8,128)(2,1)}, u32[]{:S(2)}) copy-start(bf16[1,128,4096]{2,1,0:T(8,128)(2,1)} %param.7) | copy-start | bytes 3145732
  38.8 3.4 %collective-permute-start.14 = (bf16[128,1024]{1,0:T(8,128)(2,1)S(1)}, bf16[128,1024]{1,0:T(8,128)(2,1)S(1)}, u32[]{:S(2)}, u32[]{:S(2)}) collective-permute-start(bf16[128,1024]{1,0:T(8,128)(2,1)S(1)} %convert_element_type.21), channel_id=1, source_target_pairs={{1,0},{3,2},{5,4},{7,6},{9,8},{11,10},{13,12},{15,14},{17,16},{19,... | collective-permute-start | bytes 786440 | tf_op jit(solution)/shard_map/ppermute | solution.py:274
  42.3 8.3 %collective-permute-start.15 = (bf16[128,1024]{1,0:T(8,128)(2,1)S(1)}, bf16[128,1024]{1,0:T(8,128)(2,1)S(1)}, u32[]{:S(2)}, u32[]{:S(2)}) collective-permute-start(bf16[128,1024]{1,0:T(8,128)(2,1)S(1)} %fusion), channel_id=1, source_target_pairs={{2,0},{6,4},{10,8},{14,12},{18,16},{22,20},{26,24},{30,28}} | collective-permute-start | bytes 786440 | tf_op jit(solution)/shard_map/ppermute | solution.py:274
  43.6 32.8 %collective-permute-start.8 = (bf16[128,4096]{1,0:T(8,128)(2,1)S(1)}, bf16[128,4096]{1,0:T(8,128)(2,1)S(1)}, u32[]{:S(2)}, u32[]{:S(2)}) collective-permute-start(bf16[128,4096]{1,0:T(8,128)(2,1)S(1)} %get-tuple-element.25), channel_id=1, source_target_pairs={{16,0},{0,16},{17,1},{1,17},{18,2},{2,18},{19,3},{3,19},{20,4},{4,... | collective-permute-start | bytes 3145736 | tf_op jit(solution)/shard_map/ppermute | solution.py:274
  45.1 7.7 %collective-permute-start.9 = (bf16[128,1024]{1,0:T(8,128)(2,1)S(1)}, bf16[128,1024]{1,0:T(8,128)(2,1)S(1)}, u32[]{:S(2)}, u32[]{:S(2)}) collective-permute-start(bf16[128,1024]{1,0:T(8,128)(2,1)S(1)} %get-tuple-element.27), channel_id=1, source_target_pairs={{0,1},{1,0},{2,3},{3,2},{4,5},{5,4},{6,7},{7,6},{8,9},{9,8},{10,11... | collective-permute-start | bytes 786440 | tf_op jit(solution)/shard_map/ppermute | solution.py:274
  50.7 9.9 %collective-permute-start.16 = (bf16[128,1024]{1,0:T(8,128)(2,1)S(1)}, bf16[128,1024]{1,0:T(8,128)(2,1)S(1)}, u32[]{:S(2)}, u32[]{:S(2)}) collective-permute-start(bf16[128,1024]{1,0:T(8,128)(2,1)S(1)} %fusion.1), channel_id=1, source_target_pairs={{4,0},{12,8},{20,16},{28,24}} | collective-permute-start | bytes 786440 | tf_op jit(solution)/shard_map/ppermute | solution.py:274
  52.0 13.3 %collective-permute-start.10 = (bf16[128,1024]{1,0:T(8,128)(2,1)S(1)}, bf16[128,1024]{1,0:T(8,128)(2,1)S(1)}, u32[]{:S(2)}, u32[]{:S(2)}) collective-permute-start(bf16[128,1024]{1,0:T(8,128)(2,1)S(1)} %get-tuple-element.28), channel_id=1, source_target_pairs={{1,2},{3,4},{5,6},{7,8},{9,10},{11,12},{13,14},{2,1},{4,3},{6,5},{... | collective-permute-start | bytes 786440 | tf_op jit(solution)/shard_map/ppermute | solution.py:274
  52.6 13.9 %collective-permute-start.11 = (bf16[128,1024]{1,0:T(8,128)(2,1)S(1)}, bf16[128,1024]{1,0:T(8,128)(2,1)S(1)}, u32[]{:S(2)}, u32[]{:S(2)}) collective-permute-start(bf16[128,1024]{1,0:T(8,128)(2,1)S(1)} %get-tuple-element.29), channel_id=1, source_target_pairs={{0,2},{1,3},{2,0},{3,1},{4,6},{5,7},{6,4},{7,5},{8,10},{9,11},{10,... | collective-permute-start | bytes 786440 | tf_op jit(solution)/shard_map/ppermute | solution.py:274
  52.9 23.2 %collective-permute-start.12 = (bf16[128,1024]{1,0:T(8,128)(2,1)S(1)}, bf16[128,1024]{1,0:T(8,128)(2,1)S(1)}, u32[]{:S(2)}, u32[]{:S(2)}) collective-permute-start(bf16[128,1024]{1,0:T(8,128)(2,1)S(1)} %get-tuple-element.30), channel_id=1, source_target_pairs={{0,4},{1,5},{2,6},{3,7},{4,0},{5,1},{6,2},{7,3},{8,12},{9,13},{10,... | collective-permute-start | bytes 786440 | tf_op jit(solution)/shard_map/ppermute | solution.py:274
  60.6 15.6 %collective-permute-start.13 = (bf16[128,1024]{1,0:T(8,128)(2,1)S(1)}, bf16[128,1024]{1,0:T(8,128)(2,1)S(1)}, u32[]{:S(2)}, u32[]{:S(2)}) collective-permute-start(bf16[128,1024]{1,0:T(8,128)(2,1)S(1)} %get-tuple-element.31), channel_id=1, source_target_pairs={{0,8},{1,9},{2,10},{3,11},{4,12},{5,13},{6,14},{7,15},{8,0},{9,1},... | collective-permute-start | bytes 786440 | tf_op jit(solution)/shard_map/ppermute | solution.py:274
  65.2 14.8 %collective-permute-start.17 = (bf16[128,1024]{1,0:T(8,128)(2,1)S(1)}, bf16[128,1024]{1,0:T(8,128)(2,1)S(1)}, u32[]{:S(2)}, u32[]{:S(2)}) collective-permute-start(bf16[128,1024]{1,0:T(8,128)(2,1)S(1)} %get-tuple-element.35), channel_id=1, source_target_pairs={{8,0},{24,16}} | collective-permute-start | bytes 786440 | tf_op jit(solution)/shard_map/ppermute | solution.py:274

commit v3 on v2

--- a/solution.py
+++ b/solution.py
@@ -11,8 +11,8 @@
 HD = 128
 BIG = 1e30
 MEGA = 1 << 20
-VM_SMALL = 16
-VM_ATTEND = 28
+VM_SMALL = 8
+VM_ATTEND = 20
 
 NT = (((1,), (1,)), ((), ()))
 NN = (((1,), (0,)), ((), ()))
@@ -86,9 +86,9 @@
 
 def attend_kernel(partner_count, info, stream, cot, gain, queries, inverse, slots, key_cols,
                   even_block, odd_block, *rest):
-    handed, own_g, near_g, far_g, glob_g = rest[:5]
-    partners_g = rest[5 : 5 + partner_count]
-    dq, dk, dv, block, block_t, w0, d0, w1, d1 = rest[5 + partner_count :]
+    handed, own_g, near_g, far_g, keep_g, across_g, corner_g = rest[:7]
+    partners_g = rest[7 : 7 + partner_count]
+    dq, products, dk, dv, block, block_t, w0, d0, w1, d1 = rest[7 + partner_count :]
     rows, width = stream.shape
     groups = key_cols.shape[0]
     kvw = groups * HD
@@ -138,7 +138,7 @@
         for j in range(5):
             w = raised[j] * share
             low[j * rows : (j + 1) * rows] = w.astype(jnp.bfloat16)
-            grad[j * rows : (j + 1) * rows] = (w * ((gws[j] - centre) * factor)).astype(jnp.bfloat16)
+            grad[j * rows : (j + 1) * rows] = (w * (gws[j] - centre)).astype(jnp.bfloat16)
 
     def spread(i, low, grad):
         g = i // pairs
@@ -153,10 +153,13 @@
             dk[g] += key_part
         cols = dot(key_cols[g], grad[: 4 * rows], NN) + dot(block_t[g], grad[4 * rows :], NN)
         back = cols.T
-        at = 2 * i * HD
-        dq[:, at : at + HD] = back[:rows]
-        dq[:, at + HD : at + 2 * HD] = back[rows:]
-
+        for h in range(2):
+            s = slice((2 * i + h) * HD, (2 * i + h + 1) * HD)
+            part = back[h * rows : (h + 1) * rows] * (gain[:, s] * factor)
+            dq[:, s] = part
+            products[...] += part * stream[:, s].astype(jnp.float32)
+
+    products[...] = jnp.zeros_like(products)
     buffers = ((w0, d0), (w1, d1))
     weigh(0, *buffers[0])
     for i in range(1, count):
@@ -165,28 +168,33 @@
     spread(count - 1, *buffers[(count - 1) % 2])
 
     inv = inverse[...]
-    products = jnp.zeros((rows, HD), jnp.float32)
-    for i in range(width // HD):
-        s = slice(i * HD, (i + 1) * HD)
-        products = products + dq[:, s] * gain[:, s] * stream[:, s].astype(jnp.float32)
-    mean = jnp.sum(products, axis=1, keepdims=True) * (1.0 / width) * inv
+    mean = jnp.sum(products[...], axis=1, keepdims=True) * (1.0 / width) * inv
     pull = inv * inv * mean
     for i in range(width // HD):
         s = slice(i * HD, (i + 1) * HD)
         x = stream[:, s].astype(jnp.float32)
-        grad_hidden = dq[:, s] * gain[:, s] * inv - x * pull
+        grad_hidden = dq[:, s] * inv - x * pull
         handed[:, s] = (cot[:, s].astype(jnp.float32) + grad_hidden).astype(jnp.bfloat16)
+
+    share = rows // 4
+
+    def share_at(mask):
+        return pl.multiple_of(4 * rows + ((me % 4) ^ mask) * share, share)
 
     near_at = pl.multiple_of((1 - odd) * 2 * rows, rows)
     far_at = pl.multiple_of(odd * 2 * rows, rows)
     for g in range(groups):
         kc = slice(g * HD, (g + 1) * HD)
         vc = slice(kvw + g * HD, kvw + (g + 1) * HD)
+        dk[g] = dk[g] * factor
         for source, cols in ((dk, kc), (dv, vc)):
             own_g[:, cols] = source[g, rows : 2 * rows]
-            near_g[:, cols] = source[g, pl.ds(near_at, rows)].astype(jnp.bfloat16)
+            near_g[:rows, cols] = source[g, pl.ds(near_at, rows)].astype(jnp.bfloat16)
             far_g[:, cols] = source[g, pl.ds(far_at, rows)].astype(jnp.bfloat16)
-            glob_g[:, cols] = source[g, 4 * rows : 5 * rows]
+            keep_g[:, cols] = source[g, pl.ds(share_at(0), share)]
+            near_g[rows:, cols] = source[g, pl.ds(share_at(1), share)].astype(jnp.bfloat16)
+            across_g[:, cols] = source[g, pl.ds(share_at(2), share)].astype(jnp.bfloat16)
+            corner_g[:, cols] = source[g, pl.ds(share_at(3), share)].astype(jnp.bfloat16)
             term = source[g, 3 * rows : 4 * rows].astype(jnp.bfloat16)
             for b in range(partner_count):
                 hit = want == (me ^ (2 << b))
@@ -199,13 +207,17 @@
     kvw = groups * HD
     low = jax.ShapeDtypeStruct((rows, 2 * kvw), jnp.bfloat16)
     wide = jax.ShapeDtypeStruct((rows, 2 * kvw), jnp.float32)
+    longer = jax.ShapeDtypeStruct((rows + rows // 4, 2 * kvw), jnp.bfloat16)
+    kept = jax.ShapeDtypeStruct((rows // 4, 2 * kvw), jnp.float32)
+    share = jax.ShapeDtypeStruct((rows // 4, 2 * kvw), jnp.bfloat16)
     return pl.pallas_call(
         functools.partial(attend_kernel, partner_count),
-        out_shape=[jax.ShapeDtypeStruct((rows, width), jnp.bfloat16), wide, low, low, wide] + [low] * partner_count,
+        out_shape=[jax.ShapeDtypeStruct((rows, width), jnp.bfloat16), wide, longer, low, kept, share, share] + [low] * partner_count,
         in_specs=[SMEM] + [VMEM] * 9,
-        out_specs=[VMEM] * (5 + partner_count),
+        out_specs=[VMEM] * (7 + partner_count),
         scratch_shapes=[
             pltpu.VMEM((rows, width), jnp.float32),
+            pltpu.VMEM((rows, HD), jnp.float32),
             pltpu.VMEM((groups, 5 * rows, HD), jnp.float32),
             pltpu.VMEM((groups, 5 * rows, HD), jnp.float32),
             pltpu.VMEM((rows, 2 * kvw), jnp.bfloat16),
@@ -220,7 +232,7 @@
 def collect_kernel(own, *rest):
     total = own[...]
     for ref in rest[:-1]:
-        total = total + ref[...].astype(jnp.float32)
+        total = total + ref[: own.shape[0], :].astype(jnp.float32)
     rest[-1][...] = total
 
 
@@ -235,39 +247,34 @@
     )(own, *parts)
 
 
-def land_kernel(source, target):
-    target[...] = source[...]
-
-
-def land(rows):
-    return pl.pallas_call(
-        land_kernel,
-        out_shape=jax.ShapeDtypeStruct(rows.shape, rows.dtype),
-        in_specs=[VMEM],
-        out_specs=VMEM,
-        compiler_params=params(VM_SMALL),
-        cost_estimate=cost(1.0),
-    )(rows)
-
-
-def finish_kernel(info, total, acc, got, keys, values):
+def finish_kernel(info, total, received, acc, *rest):
+    previous, keys, values = rest[-3:]
+    others = rest[-6:-3]
+    previous[...] = received[...]
     kvw = keys.shape[1]
-    last = acc[...] + got[...].astype(jnp.float32)
-    result = (total[...] + jnp.where(info[0] == 0, last, 0.0)).astype(jnp.bfloat16)
-    keys[...] = result[:, :kvw]
-    values[...] = result[:, kvw:]
-
-
-def finish(info, total, acc, got):
-    half = jax.ShapeDtypeStruct((total.shape[0], total.shape[1] // 2), jnp.bfloat16)
+    rows = acc.shape[0]
+    first = info[0] == 0
+    last = acc[...]
+    for ref in rest[:-6]:
+        last = last + ref[...].astype(jnp.float32)
+    for k in range(4):
+        part = last if k == 0 else others[k - 1][...].astype(jnp.float32)
+        part = jnp.where(first, part, 0.0)
+        result = (total[k * rows : (k + 1) * rows, :] + part).astype(jnp.bfloat16)
+        keys[k * rows : (k + 1) * rows, :] = result[:, :kvw]
+        values[k * rows : (k + 1) * rows, :] = result[:, kvw:]
+
+
+def finish(info, total, received, acc, terms, others):
+    shape = jax.ShapeDtypeStruct((total.shape[0], total.shape[1] // 2), jnp.bfloat16)
     return pl.pallas_call(
         finish_kernel,
-        out_shape=[half, half],
-        in_specs=[SMEM] + [VMEM] * 3,
-        out_specs=[VMEM] * 2,
+        out_shape=[jax.ShapeDtypeStruct(received.shape, received.dtype), shape, shape],
+        in_specs=[SMEM] + [VMEM] * (3 + len(terms) + len(others)),
+        out_specs=[VMEM] * 3,
         compiler_params=params(VM_SMALL),
         cost_estimate=cost(0.5),
-    )(info, total, acc, got)
+    )(info, total, received, acc, *terms, *others)
 
 
 def permuted(value, pairs, axis="seq"):
@@ -323,27 +330,43 @@
         block0 = jnp.where(device == (1 << b), partners[b], block0)
     block0, far = lax.optimization_barrier((block0, far))
     for pairs in global_rounds(count, [0, top] + [1 << b for b in range(1, bits)]):
-        moved = permuted(block0, pairs)
+        masks = {i ^ j for i, j in pairs}
+        if len(masks) == 1:
+            route = swaps[masks.pop().bit_length() - 1]
+        else:
+            route = pairs
+        moved = permuted(block0, route)
         block0 = jnp.where(among(device, [t for _, t in pairs]), moved, block0)
-    odd_block = permuted(block0, [(i, i + 1) for i in range(0, count, 2)])
+    odd_block = permuted(block0, swaps[0])
     queries, inverse, slots, key_cols = prepare(info, hidden, gain, own, near, far, partners[1:])
     outs = attend(info, hidden, upstream, gain, queries, inverse, slots, key_cols, block0, odd_block, bits - 1)
-    handed, own_g, near_g, far_g, glob_g = outs[:5]
-    partners_g = outs[5:]
+    handed, own_g, near_g, far_g, keep_g, across_g, corner_g = outs[:7]
+    partners_g = outs[7:]
 
     sections = lax.axis_size("section")
     back = [((i + 1) % sections, i) for i in range(sections)]
-    previous = land(permuted(handed, back, "section"))
-    parts = [permuted(near_g, swaps[0]), permuted(far_g, across)]
-    parts = parts + [permuted(partners_g[b - 1], swaps[b]) for b in range(1, bits)]
-    acc = glob_g
-    for b in range(bits):
-        pairs = [(i + (1 << b), i) for i in range(0, count, 2 << b)]
-        last = permuted(acc.astype(jnp.bfloat16), pairs)
-        if b < bits - 1:
-            acc = acc + last.astype(jnp.float32)
+    rows = own.shape[0]
+
+    def swapped(value, mask):
+        return permuted(value, [(i, i ^ mask) for i in range(count)])
+
+    received = permuted(handed, back, "section")
+    near_r = permuted(near_g, swaps[0])
+    parts = [near_r, permuted(partners_g[0], swaps[1])]
+    for b in reversed(range(2, bits)):
+        parts.append(permuted(partners_g[b - 1], swaps[b]))
+    parts.append(permuted(far_g, across))
+
+    terms = [near_r[rows:], swapped(across_g, 2), swapped(corner_g, 3)]
+    acc = keep_g
+    for b in range(2, bits, 2):
+        acc = acc + sum(t.astype(jnp.float32) for t in terms)
+        low = acc.astype(jnp.bfloat16)
+        terms = [swapped(low, k << b) for k in range(1, 1 << min(2, bits - b))]
+    mine = (acc + sum(t.astype(jnp.float32) for t in terms)).astype(jnp.bfloat16)
+    others = [swapped(mine, mask) for mask in (1, 2, 3)]
     total = collect(own_g, parts)
-    key_grads, value_grads = finish(info, total, acc, last)
+    previous, key_grads, value_grads = finish(info, total, received, acc, terms, others)
     return (previous[None], key_grads[None], value_grads[None])
 
 

time: 81.6 us -> 77.4 us (0.949)
  waiting for transfers between devices: 33.5 us -> 31.2 us
  Pallas kernels: 15.3 us -> 14.3 us
    ppermute x18 -> x22, waiting for transfers between devices: 33.5 us -> 31.2 us  [permuted(): return lax.ppermute(value, axis, pairs)]
    pallas_call x2 -> x1, Pallas kernels: 2.34 us -> 1.69 us  [finish(): pl.pallas_call(finish_kernel, out_shape=[jax.ShapeDtypeStruct(received.sh...]
    ppermute x18 -> x22, starting transfers between devices: 29.3 us -> 28.8 us  [permuted(): return lax.ppermute(value, axis, pairs)]
  transfers between devices with their start and end apart: 18 -> 22, of which waited for: 8 -> 12; matrix products, arithmetic and copies ran while one was open for 1% -> 0% of each run, Pallas kernels for 3% -> 2%
where the time goes in v3:
time: 77.4 us; the launch traced here: 77.2 us
  waiting for transfers between devices  31.2 us (40%)
  starting transfers between devices  28.8 us (37%)
  Pallas kernels  14.3 us (18%)
  between operations  1.48 us (2%)
  other arithmetic  1.4 us (2%)
    ppermute x22, waiting for transfers between devices, permuted(): return lax.ppermute(value, axis, pairs)  31.2 us
    ppermute x22, starting transfers between devices, permuted(): return lax.ppermute(value, axis, pairs)  28.8 us
    pallas_call x1, Pallas kernels, attend(): pl.pallas_call(functools.partial(attend_kernel, partner_count), out_shape...  11.1 us
    pallas_call x1, Pallas kernels, finish(): pl.pallas_call(finish_kernel, out_shape=[jax.ShapeDtypeStruct(received.sh...  1.69 us
  transfers between devices with their start and end apart: 22, of which 12 were waited for; matrix products, arithmetic and copies ran while one was open for 0% of the time, Pallas kernels for 2%

profile of v3, /device:TPU:0, one launch (start us, length us, event | category | flops | bytes accessed | tf_op | source)
XLA Modules:
  0.0 77.2 jit_solution(16003693047889887402)
XLA Ops:
  0.7 1.0 %pad_maximum_fusion.own = bf16[128,1024]{1,0:T(8,128)(2,1)S(1)} fusion(bf16[128,512]{1,0:T(8,128)(2,1)} %bitcast.13, bf16[128,512]{1,0:T(8,128)(2,1)} %bitcast.15), kind=kLoop, calls=%fused_computation | loop fusion | flops 524288 | bytes 524288 | tf_op jit(solution)/shard_map/concatenate | solution.py:313
  1.7 7.0 %collective-permute-start.4 = (bf16[128,1024]{1,0:T(8,128)(2,1)S(1)}, bf16[128,1024]{1,0:T(8,128)(2,1)S(1)}, u32[]{:S(2)}, u32[]{:S(2)}) collective-permute-start(bf16[128,1024]{1,0:T(8,128)(2,1)S(1)} %pad_maximum_fusion.own), channel_id=1, source_target_pairs={{0,12},{16,28}} | collective-permute-start | bytes 786440 | tf_op jit(solution)/shard_map/ppermute | solution.py:281
  8.8 0.7 collective-permute-start.1
  10.3 4.9 %collective-permute-done.4 = bf16[128,1024]{1,0:T(8,128)(2,1)S(1)} collective-permute-done((bf16[128,1024]{1,0:T(8,128)(2,1)S(1)}, bf16[128,1024]{1,0:T(8,128)(2,1)S(1)}, u32[]{:S(2)}, u32[]{:S(2)}) %collective-permute-start.4) | collective-permute-done | bytes 262176 | tf_op jit(solution)/shard_map/ppermute | solution.py:281
  15.1 2.8 %collective-permute-done.2.rest_1_ = bf16[128,1024]{1,0:T(8,128)(2,1)S(1)} collective-permute-done((bf16[128,1024]{1,0:T(8,128)(2,1)S(1)}, bf16[128,1024]{1,0:T(8,128)(2,1)S(1)}, u32[]{:S(2)}, u32[]{:S(2)}) %collective-permute-start.2) | collective-permute-done | bytes 262176 | tf_op jit(solution)/shard_map/ppermute | solution.py:281
  17.9 3.8 %collective-permute-done.1.rest_2_ = bf16[128,1024]{1,0:T(8,128)(2,1)S(1)} collective-permute-done((bf16[128,1024]{1,0:T(8,128)(2,1)S(1)}, bf16[128,1024]{1,0:T(8,128)(2,1)S(1)}, u32[]{:S(2)}, u32[]{:S(2)}) %collective-permute-start.1) | collective-permute-done | bytes 262176 | tf_op jit(solution)/shard_map/ppermute | solution.py:281
  22.0 1.4 %collective-permute-start.6 = (bf16[128,1024]{1,0:T(8,128)(2,1)S(1)}, bf16[128,1024]{1,0:T(8,128)(2,1)S(1)}, u32[]{:S(2)}, u32[]{:S(2)}) collective-permute-start(bf16[128,1024]{1,0:T(8,128)(2,1)S(1)} %select_select_fusion), channel_id=1, source_target_pairs={{0,2},{1,3},{2,0},{3,1},{4,6},{5,7},{6,4},{7,5},{8,10},{9,11},{10,... | collective-permute-start | bytes 786440 | tf_op jit(solution)/shard_map/ppermute | solution.py:281
  24.1 4.7 %collective-permute-done.6 = bf16[128,1024]{1,0:T(8,128)(2,1)S(1)} collective-permute-done((bf16[128,1024]{1,0:T(8,128)(2,1)S(1)}, bf16[128,1024]{1,0:T(8,128)(2,1)S(1)}, u32[]{:S(2)}, u32[]{:S(2)}) %collective-permute-start.6) | collective-permute-done | bytes 262176 | tf_op jit(solution)/shard_map/ppermute | solution.py:281
  28.9 1.3 %shard_map.85 = (bf16[128,4096]{1,0:T(8,128)(2,1)S(1)}, f32[128,128]{1,0:T(8,128)S(1)}, bf16[512,1024]{1,0:T(8,128)(2,1)S(1)}, bf16[4,128,512]{2,1,0:T(8,128)(2,1)S(1)}) custom-call(s32[3]{0:T(128)S(1)} %pad_add_fusion.info, bf16[128,4096]{1,0:T(8,128)(2,1)S(1)} %bitcast.10, f32[1,4096]{1,0:T(1,128)S(1)} %copy-done.2, ...), custom_call_target="tpu_custom_call" | custom-call | flops 6899999744 | bytes 1048576 | tf_op jit(solution)/shard_map/pallas_call | solution.py:72
  30.4 11.1 %shard_map.86 = (bf16[128,4096]{1,0:T(8,128)(2,1)S(1)}, f32[128,1024]{1,0:T(8,128)S(1)}, bf16[160,1024]{1,0:T(8,128)(2,1)S(1)}, bf16[128,1024]{1,0:T(8,128)(2,1)...) custom-call(s32[3]{0:T(128)S(1)} %pad_add_fusion.info, ...), custom_call_target="tpu_custom_call" | custom-call | flops 13799999488 | bytes 1048576 | tf_op jit(solution)/shard_map/pallas_call | solution.py:213
  41.6 1.6 %collective-permute-start.13 = (bf16[128,4096]{1,0:T(8,128)(2,1)S(1)}, bf16[128,4096]{1,0:T(8,128)(2,1)S(1)}, u32[]{:S(2)}, u32[]{:S(2)}) collective-permute-start(bf16[128,4096]{1,0:T(8,128)(2,1)S(1)} %get-tuple-element.34), channel_id=1, source_target_pairs={{16,0},{0,16},{17,1},{1,17},{18,2},{2,18},{19,3},{3,19},{20,4},{4,... | collective-permute-start | bytes 3145736 | tf_op jit(solution)/shard_map/ppermute | solution.py:281
  43.2 1.7 %collective-permute-start.14 = (bf16[32,1024]{1,0:T(8,128)(2,1)S(1)}, bf16[32,1024]{1,0:T(8,128)(2,1)S(1)}, u32[]{:S(2)}, u32[]{:S(2)}) collective-permute-start(bf16[32,1024]{1,0:T(8,128)(2,1)S(1)} %get-tuple-element.36), channel_id=1, source_target_pairs={{0,2},{1,3},{2,0},{3,1},{4,6},{5,7},{6,4},{7,5},{8,10},{9,11},{10,... | collective-permute-start | bytes 196616 | tf_op jit(solution)/shard_map/ppermute | solution.py:281
  45.0 2.6 %collective-permute-done.14 = bf16[32,1024]{1,0:T(8,128)(2,1)S(1)} collective-permute-done((bf16[32,1024]{1,0:T(8,128)(2,1)S(1)}, bf16[32,1024]{1,0:T(8,128)(2,1)S(1)}, u32[]{:S(2)}, u32[]{:S(2)}) %collective-permute-start.14) | collective-permute-done | bytes 65568 | tf_op jit(solution)/shard_map/ppermute | solution.py:281
  47.6 1.4 %collective-permute-done.15 = bf16[32,1024]{1,0:T(8,128)(2,1)S(1)} collective-permute-done((bf16[32,1024]{1,0:T(8,128)(2,1)S(1)}, bf16[32,1024]{1,0:T(8,128)(2,1)S(1)}, u32[]{:S(2)}, u32[]{:S(2)}) %collective-permute-start.15) | collective-permute-done | bytes 65568 | tf_op jit(solution)/shard_map/ppermute | solution.py:281
  49.0 3.9 %collective-permute-start.18 = (bf16[32,1024]{1,0:T(8,128)(2,1)S(1)}, bf16[32,1024]{1,0:T(8,128)(2,1)S(1)}, u32[]{:S(2)}, u32[]{:S(2)}) collective-permute-start(bf16[32,1024]{1,0:T(8,128)(2,1)S(1)} %get-tuple-element.41), channel_id=1, source_target_pairs={{0,12},{1,13},{2,14},{3,15},{4,8},{5,9},{6,10},{7,11},{8,4},{9,5},... | collective-permute-start | bytes 196616 | tf_op jit(solution)/shard_map/ppermute | solution.py:281
  52.9 1.4 %collective-permute-start.17 = (bf16[32,1024]{1,0:T(8,128)(2,1)S(1)}, bf16[32,1024]{1,0:T(8,128)(2,1)S(1)}, u32[]{:S(2)}, u32[]{:S(2)}) collective-permute-start(bf16[32,1024]{1,0:T(8,128)(2,1)S(1)} %get-tuple-element.41), channel_id=1, source_target_pairs={{0,8},{1,9},{2,10},{3,11},{4,12},{5,13},{6,14},{7,15},{8,0},{9,1},... | collective-permute-start | bytes 196616 | tf_op jit(solution)/shard_map/ppermute | solution.py:281
  54.3 0.8 collective-permute-start.9
  55.8 4.2 %collective-permute-start.10 = (bf16[128,1024]{1,0:T(8,128)(2,1)S(1)}, bf16[128,1024]{1,0:T(8,128)(2,1)S(1)}, u32[]{:S(2)}, u32[]{:S(2)}) collective-permute-start(bf16[128,1024]{1,0:T(8,128)(2,1)S(1)} %get-tuple-element.31), channel_id=1, source_target_pairs={{0,8},{1,9},{2,10},{3,11},{4,12},{5,13},{6,14},{7,15},{8,0},{9,1},... | collective-permute-start | bytes 786440 | tf_op jit(solution)/shard_map/ppermute | solution.py:281
  61.0 1.5 %collective-permute-done.9.rest_1_ = bf16[128,1024]{1,0:T(8,128)(2,1)S(1)} collective-permute-done((bf16[128,1024]{1,0:T(8,128)(2,1)S(1)}, bf16[128,1024]{1,0:T(8,128)(2,1)S(1)}, u32[]{:S(2)}, u32[]{:S(2)}) %collective-permute-start.9) | collective-permute-done | bytes 262176 | tf_op jit(solution)/shard_map/ppermute | solution.py:281
  62.5 2.8 %collective-permute-start.21 = (bf16[32,1024]{1,0:T(8,128)(2,1)S(1)}, bf16[32,1024]{1,0:T(8,128)(2,1)S(1)}, u32[]{:S(2)}, u32[]{:S(2)}) collective-permute-start(bf16[32,1024]{1,0:T(8,128)(2,1)S(1)} %add_convert_fusion), channel_id=1, source_target_pairs={{0,3},{1,2},{2,1},{3,0},{4,7},{5,6},{6,5},{7,4},{8,11},{9,10},{10,... | collective-permute-start | bytes 196616 | tf_op jit(solution)/shard_map/ppermute | solution.py:281
  65.3 6.0 %collective-permute-done.10.rest_2_ = bf16[128,1024]{1,0:T(8,128)(2,1)S(1)} collective-permute-done((bf16[128,1024]{1,0:T(8,128)(2,1)S(1)}, bf16[128,1024]{1,0:T(8,128)(2,1)S(1)}, u32[]{:S(2)}, u32[]{:S(2)}) %collective-permute-start.10) | collective-permute-done | bytes 262176 | tf_op jit(solution)/shard_map/ppermute | solution.py:281
  71.3 1.6 %collective-permute-start.20 = (bf16[32,1024]{1,0:T(8,128)(2,1)S(1)}, bf16[32,1024]{1,0:T(8,128)(2,1)S(1)}, u32[]{:S(2)}, u32[]{:S(2)}) collective-permute-start(bf16[32,1024]{1,0:T(8,128)(2,1)S(1)} %add_convert_fusion), channel_id=1, source_target_pairs={{0,2},{1,3},{2,0},{3,1},{4,6},{5,7},{6,4},{7,5},{8,10},{9,11},{10,... | collective-permute-start | bytes 196616 | tf_op jit(solution)/shard_map/ppermute | solution.py:281
  73.0 2.5 %collective-permute-done.20.rest_4_ = bf16[32,1024]{1,0:T(8,128)(2,1)S(1)} collective-permute-done((bf16[32,1024]{1,0:T(8,128)(2,1)S(1)}, bf16[32,1024]{1,0:T(8,128)(2,1)S(1)}, u32[]{:S(2)}, u32[]{:S(2)}) %collective-permute-start.20) | collective-permute-done | bytes 65568 | tf_op jit(solution)/shard_map/ppermute | solution.py:281
  75.5 1.7 %shard_map.88 = (bf16[128,4096]{1,0:T(8,128)(2,1)}, bf16[128,512]{1,0:T(8,128)(2,1)}, bf16[128,512]{1,0:T(8,128)(2,1)}) custom-call(s32[3]{0:T(128)S(1)} %pad_add_fusion.info, f32[128,1024]{1,0:T(8,128)S(1)} %shard_map.87.total, bf16[128,4096]{1,0:T(8,128)(2,1)S(1)} %collective-permute-done.13.received, f32[32,1024]{1,0:T(8,128)S(1)} %get-tuple-element.42.acc, ...), custom_call_target="tpu_custom_call" | custom-call | flops 575000000 | bytes 1048576 | tf_op jit(solution)/shard_map/pallas_call | solution.py:270
  (40 shorter events, 3.5 us)
Async XLA Ops:
  0.6 21.1 %copy-start.3 = (bf16[1,128,512]{2,1,0:T(8,128)(2,1)S(1)}, bf16[1,128,512]{2,1,0:T(8,128)(2,1)}, u32[]{:S(2)}) copy-start(bf16[1,128,512]{2,1,0:T(8,128)(2,1)} %param.9) | copy-start | bytes 393220
  0.6 21.1 %copy-start.4 = (bf16[1,128,512]{2,1,0:T(8,128)(2,1)S(1)}, bf16[1,128,512]{2,1,0:T(8,128)(2,1)}, u32[]{:S(2)}) copy-start(bf16[1,128,512]{2,1,0:T(8,128)(2,1)} %param.8) | copy-start | bytes 393220
  1.7 13.4 %collective-permute-start.4 = (bf16[128,1024]{1,0:T(8,128)(2,1)S(1)}, bf16[128,1024]{1,0:T(8,128)(2,1)S(1)}, u32[]{:S(2)}, u32[]{:S(2)}) collective-permute-start(bf16[128,1024]{1,0:T(8,128)(2,1)S(1)} %pad_maximum_fusion.own), channel_id=1, source_target_pairs={{0,12},{16,28}} | collective-permute-start | bytes 786440 | tf_op jit(solution)/shard_map/ppermute | solution.py:281
  8.7 6.5 %collective-permute-start.3 = (bf16[128,1024]{1,0:T(8,128)(2,1)S(1)}, bf16[128,1024]{1,0:T(8,128)(2,1)S(1)}, u32[]{:S(2)}, u32[]{:S(2)}) collective-permute-start(bf16[128,1024]{1,0:T(8,128)(2,1)S(1)} %pad_maximum_fusion.own), channel_id=1, source_target_pairs={{0,2},{1,3},{2,0},{3,1},{4,6},{5,7},{6,4},{7,5},{8,10},{9,11},{10,... | collective-permute-start | bytes 786440 | tf_op jit(solution)/shard_map/ppermute | solution.py:281
  8.7 9.2 %collective-permute-start.2 = (bf16[128,1024]{1,0:T(8,128)(2,1)S(1)}, bf16[128,1024]{1,0:T(8,128)(2,1)S(1)}, u32[]{:S(2)}, u32[]{:S(2)}) collective-permute-start(bf16[128,1024]{1,0:T(8,128)(2,1)S(1)} %pad_maximum_fusion.own), channel_id=1, source_target_pairs={{0,4},{1,5},{2,6},{3,7},{4,0},{5,1},{6,2},{7,3},{8,12},{9,13},{10,... | collective-permute-start | bytes 786440 | tf_op jit(solution)/shard_map/ppermute | solution.py:281
  8.8 13.0 %collective-permute-start.1 = (bf16[128,1024]{1,0:T(8,128)(2,1)S(1)}, bf16[128,1024]{1,0:T(8,128)(2,1)S(1)}, u32[]{:S(2)}, u32[]{:S(2)}) collective-permute-start(bf16[128,1024]{1,0:T(8,128)(2,1)S(1)} %pad_maximum_fusion.own), channel_id=1, source_target_pairs={{0,8},{1,9},{2,10},{3,11},{4,12},{5,13},{6,14},{7,15},{8,0},{9,1},... | collective-permute-start | bytes 786440 | tf_op jit(solution)/shard_map/ppermute | solution.py:281
  9.6 12.4 %collective-permute-start.5 = (bf16[128,1024]{1,0:T(8,128)(2,1)S(1)}, bf16[128,1024]{1,0:T(8,128)(2,1)S(1)}, u32[]{:S(2)}, u32[]{:S(2)}) collective-permute-start(bf16[128,1024]{1,0:T(8,128)(2,1)S(1)} %pad_maximum_fusion.own), channel_id=1, source_target_pairs={{1,2},{3,4},{5,6},{7,8},{9,10},{11,12},{13,14},{2,1},{4,3},{6,5},{... | collective-permute-start | bytes 786440 | tf_op jit(solution)/shard_map/ppermute | solution.py:281
  22.0 6.8 %collective-permute-start.6 = (bf16[128,1024]{1,0:T(8,128)(2,1)S(1)}, bf16[128,1024]{1,0:T(8,128)(2,1)S(1)}, u32[]{:S(2)}, u32[]{:S(2)}) collective-permute-start(bf16[128,1024]{1,0:T(8,128)(2,1)S(1)} %select_select_fusion), channel_id=1, source_target_pairs={{0,2},{1,3},{2,0},{3,1},{4,6},{5,7},{6,4},{7,5},{8,10},{9,11},{10,... | collective-permute-start | bytes 786440 | tf_op jit(solution)/shard_map/ppermute | solution.py:281
  23.4 5.5 %collective-permute-start = (bf16[128,1024]{1,0:T(8,128)(2,1)S(1)}, bf16[128,1024]{1,0:T(8,128)(2,1)S(1)}, u32[]{:S(2)}, u32[]{:S(2)}) collective-permute-start(bf16[128,1024]{1,0:T(8,128)(2,1)S(1)} %pad_maximum_fusion.own), channel_id=1, source_target_pairs={{0,1},{1,0},{2,3},{3,2},{4,5},{5,4},{6,7},{7,6},{8,9},{9,8},{10,11... | collective-permute-start | bytes 786440 | tf_op jit(solution)/shard_map/ppermute | solution.py:281
  28.8 1.6 %collective-permute-start.7 = (bf16[128,1024]{1,0:T(8,128)(2,1)S(1)}, bf16[128,1024]{1,0:T(8,128)(2,1)S(1)}, u32[]{:S(2)}, u32[]{:S(2)}) collective-permute-start(bf16[128,1024]{1,0:T(8,128)(2,1)S(1)} %broadcast_select_fusion.even_block), channel_id=1, source_target_pairs={{0,1},{1,0},{2,3},{3,2},{4,5},{5,4},{6,7},{7,6},{8,9},{9,8},{10,11... | collective-permute-start | bytes 786440 | tf_op jit(solution)/shard_map/ppermute | solution.py:281
  41.6 34.0 %collective-permute-start.13 = (bf16[128,4096]{1,0:T(8,128)(2,1)S(1)}, bf16[128,4096]{1,0:T(8,128)(2,1)S(1)}, u32[]{:S(2)}, u32[]{:S(2)}) collective-permute-start(bf16[128,4096]{1,0:T(8,128)(2,1)S(1)} %get-tuple-element.34), channel_id=1, source_target_pairs={{16,0},{0,16},{17,1},{1,17},{18,2},{2,18},{19,3},{3,19},{20,4},{4,... | collective-permute-start | bytes 3145736 | tf_op jit(solution)/shard_map/ppermute | solution.py:281
  43.1 5.9 %collective-permute-start.8 = (bf16[160,1024]{1,0:T(8,128)(2,1)S(1)}, bf16[160,1024]{1,0:T(8,128)(2,1)S(1)}, u32[]{:S(2)}, u32[]{:S(2)}) collective-permute-start(bf16[160,1024]{1,0:T(8,128)(2,1)S(1)} %get-tuple-element.29), channel_id=1, source_target_pairs={{0,1},{1,0},{2,3},{3,2},{4,5},{5,4},{6,7},{7,6},{8,9},{9,8},{10,11... | collective-permute-start | bytes 983048 | tf_op jit(solution)/shard_map/ppermute | solution.py:281
  43.2 4.4 %collective-permute-start.14 = (bf16[32,1024]{1,0:T(8,128)(2,1)S(1)}, bf16[32,1024]{1,0:T(8,128)(2,1)S(1)}, u32[]{:S(2)}, u32[]{:S(2)}) collective-permute-start(bf16[32,1024]{1,0:T(8,128)(2,1)S(1)} %get-tuple-element.36), channel_id=1, source_target_pairs={{0,2},{1,3},{2,0},{3,1},{4,6},{5,7},{6,4},{7,5},{8,10},{9,11},{10,... | collective-permute-start | bytes 196616 | tf_op jit(solution)/shard_map/ppermute | solution.py:281
  44.9 4.1 %collective-permute-start.15 = (bf16[32,1024]{1,0:T(8,128)(2,1)S(1)}, bf16[32,1024]{1,0:T(8,128)(2,1)S(1)}, u32[]{:S(2)}, u32[]{:S(2)}) collective-permute-start(bf16[32,1024]{1,0:T(8,128)(2,1)S(1)} %get-tuple-element.37), channel_id=1, source_target_pairs={{0,3},{1,2},{2,1},{3,0},{4,7},{5,6},{6,5},{7,4},{8,11},{9,10},{10,... | collective-permute-start | bytes 196616 | tf_op jit(solution)/shard_map/ppermute | solution.py:281
  49.0 6.7 %collective-permute-start.18 = (bf16[32,1024]{1,0:T(8,128)(2,1)S(1)}, bf16[32,1024]{1,0:T(8,128)(2,1)S(1)}, u32[]{:S(2)}, u32[]{:S(2)}) collective-permute-start(bf16[32,1024]{1,0:T(8,128)(2,1)S(1)} %get-tuple-element.41), channel_id=1, source_target_pairs={{0,12},{1,13},{2,14},{3,15},{4,8},{5,9},{6,10},{7,11},{8,4},{9,5},... | collective-permute-start | bytes 196616 | tf_op jit(solution)/shard_map/ppermute | solution.py:281
  52.9 7.2 %collective-permute-start.17 = (bf16[32,1024]{1,0:T(8,128)(2,1)S(1)}, bf16[32,1024]{1,0:T(8,128)(2,1)S(1)}, u32[]{:S(2)}, u32[]{:S(2)}) collective-permute-start(bf16[32,1024]{1,0:T(8,128)(2,1)S(1)} %get-tuple-element.41), channel_id=1, source_target_pairs={{0,8},{1,9},{2,10},{3,11},{4,12},{5,13},{6,14},{7,15},{8,0},{9,1},... | collective-permute-start | bytes 196616 | tf_op jit(solution)/shard_map/ppermute | solution.py:281
  54.3 6.0 %collective-permute-start.16 = (bf16[32,1024]{1,0:T(8,128)(2,1)S(1)}, bf16[32,1024]{1,0:T(8,128)(2,1)S(1)}, u32[]{:S(2)}, u32[]{:S(2)}) collective-permute-start(bf16[32,1024]{1,0:T(8,128)(2,1)S(1)} %get-tuple-element.41), channel_id=1, source_target_pairs={{0,4},{1,5},{2,6},{3,7},{4,0},{5,1},{6,2},{7,3},{8,12},{9,13},{10,... | collective-permute-start | bytes 196616 | tf_op jit(solution)/shard_map/ppermute | solution.py:281
  54.3 8.2 %collective-permute-start.9 = (bf16[128,1024]{1,0:T(8,128)(2,1)S(1)}, bf16[128,1024]{1,0:T(8,128)(2,1)S(1)}, u32[]{:S(2)}, u32[]{:S(2)}) collective-permute-start(bf16[128,1024]{1,0:T(8,128)(2,1)S(1)} %get-tuple-element.30), channel_id=1, source_target_pairs={{0,2},{1,3},{2,0},{3,1},{4,6},{5,7},{6,4},{7,5},{8,10},{9,11},{10,... | collective-permute-start | bytes 786440 | tf_op jit(solution)/shard_map/ppermute | solution.py:281
  55.8 15.5 %collective-permute-start.10 = (bf16[128,1024]{1,0:T(8,128)(2,1)S(1)}, bf16[128,1024]{1,0:T(8,128)(2,1)S(1)}, u32[]{:S(2)}, u32[]{:S(2)}) collective-permute-start(bf16[128,1024]{1,0:T(8,128)(2,1)S(1)} %get-tuple-element.31), channel_id=1, source_target_pairs={{0,8},{1,9},{2,10},{3,11},{4,12},{5,13},{6,14},{7,15},{8,0},{9,1},... | collective-permute-start | bytes 786440 | tf_op jit(solution)/shard_map/ppermute | solution.py:281
  60.1 12.8 %collective-permute-start.11 = (bf16[128,1024]{1,0:T(8,128)(2,1)S(1)}, bf16[128,1024]{1,0:T(8,128)(2,1)S(1)}, u32[]{:S(2)}, u32[]{:S(2)}) collective-permute-start(bf16[128,1024]{1,0:T(8,128)(2,1)S(1)} %get-tuple-element.32), channel_id=1, source_target_pairs={{0,4},{1,5},{2,6},{3,7},{4,0},{5,1},{6,2},{7,3},{8,12},{9,13},{10,... | collective-permute-start | bytes 786440 | tf_op jit(solution)/shard_map/ppermute | solution.py:281
  60.3 12.6 %collective-permute-start.12 = (bf16[128,1024]{1,0:T(8,128)(2,1)S(1)}, bf16[128,1024]{1,0:T(8,128)(2,1)S(1)}, u32[]{:S(2)}, u32[]{:S(2)}) collective-permute-start(bf16[128,1024]{1,0:T(8,128)(2,1)S(1)} %get-tuple-element.33), channel_id=1, source_target_pairs={{1,2},{3,4},{5,6},{7,8},{9,10},{11,12},{13,14},{2,1},{4,3},{6,5},{... | collective-permute-start | bytes 786440 | tf_op jit(solution)/shard_map/ppermute | solution.py:281
  62.5 10.5 %collective-permute-start.21 = (bf16[32,1024]{1,0:T(8,128)(2,1)S(1)}, bf16[32,1024]{1,0:T(8,128)(2,1)S(1)}, u32[]{:S(2)}, u32[]{:S(2)}) collective-permute-start(bf16[32,1024]{1,0:T(8,128)(2,1)S(1)} %add_convert_fusion), channel_id=1, source_target_pairs={{0,3},{1,2},{2,1},{3,0},{4,7},{5,6},{6,5},{7,4},{8,11},{9,10},{10,... | collective-permute-start | bytes 196616 | tf_op jit(solution)/shard_map/ppermute | solution.py:281
  71.3 4.3 %collective-permute-start.20 = (bf16[32,1024]{1,0:T(8,128)(2,1)S(1)}, bf16[32,1024]{1,0:T(8,128)(2,1)S(1)}, u32[]{:S(2)}, u32[]{:S(2)}) collective-permute-start(bf16[32,1024]{1,0:T(8,128)(2,1)S(1)} %add_convert_fusion), channel_id=1, source_target_pairs={{0,2},{1,3},{2,0},{3,1},{4,6},{5,7},{6,4},{7,5},{8,10},{9,11},{10,... | collective-permute-start | bytes 196616 | tf_op jit(solution)/shard_map/ppermute | solution.py:281
  72.8 2.7 %collective-permute-start.19 = (bf16[32,1024]{1,0:T(8,128)(2,1)S(1)}, bf16[32,1024]{1,0:T(8,128)(2,1)S(1)}, u32[]{:S(2)}, u32[]{:S(2)}) collective-permute-start(bf16[32,1024]{1,0:T(8,128)(2,1)S(1)} %add_convert_fusion), channel_id=1, source_target_pairs={{0,1},{1,0},{2,3},{3,2},{4,5},{5,4},{6,7},{7,6},{8,9},{9,8},{10,11... | collective-permute-start | bytes 196616 | tf_op jit(solution)/shard_map/ppermute | solution.py:281
  (3 other events, 25.0 us)

commit v4 on v3

--- a/solution.py
+++ b/solution.py
@@ -11,8 +11,10 @@
 HD = 128
 BIG = 1e30
 MEGA = 1 << 20
-VM_SMALL = 8
-VM_ATTEND = 20
+VM_SMALL = 6
+VM_LOCAL = 6
+VM_TERMS = 6
+VM_ATTEND = 8
 
 NT = (((1,), (1,)), ((), ()))
 NN = (((1,), (0,)), ((), ()))
@@ -84,11 +86,63 @@
     )(info, stream, gain, own, near, far, *partners)
 
 
-def attend_kernel(partner_count, info, stream, cot, gain, queries, inverse, slots, key_cols,
-                  even_block, odd_block, *rest):
-    handed, own_g, near_g, far_g, keep_g, across_g, corner_g = rest[:7]
-    partners_g = rest[7 : 7 + partner_count]
-    dq, products, dk, dv, block, block_t, w0, d0, w1, d1 = rest[7 + partner_count :]
+def local_kernel(info, cot, queries, slots, raised_all, gws_all, peaks, totals, weighted):
+    rows, width = cot.shape
+    kvw = slots.shape[1] // 2
+    count = raised_all.shape[0]
+    pairs = count // (kvw // HD)
+    scale = HD**-0.5 * math.log2(math.e)
+    me, devices = info[0], info[1]
+    valid = (me > 0, None, me < devices - 1, None)
+
+    def stack(ref, i):
+        at = 2 * i * HD
+        return jnp.concatenate([ref[:, at : at + HD], ref[:, at + HD : at + 2 * HD]], axis=0)
+
+    for i in range(count):
+        g = i // pairs
+        scores = dot(slots[:, g * HD : (g + 1) * HD], stack(queries, i), NT)
+        gws = dot(slots[:, kvw + g * HD : kvw + (g + 1) * HD], stack(cot, i), NT)
+        gws_all[i] = gws
+        peak = None
+        for j in range(4):
+            top = jnp.max(scores[j * rows : (j + 1) * rows], axis=0, keepdims=True)
+            if valid[j] is not None:
+                top = jnp.where(valid[j], top, -BIG)
+            peak = top if peak is None else jnp.maximum(peak, top)
+        peak = peak * scale
+        total = 0.0
+        product = 0.0
+        for j in range(4):
+            s = slice(j * rows, (j + 1) * rows)
+            shift = peak if valid[j] is None else jnp.where(valid[j], peak, BIG)
+            e = jnp.exp2(scores[s] * scale - shift)
+            total = total + jnp.sum(e, axis=0, keepdims=True)
+            product = product + jnp.sum(e * gws[s], axis=0, keepdims=True)
+            raised_all[i, s] = e
+        peaks[i] = peak
+        totals[i] = total
+        weighted[i] = product
+
+
+def local(info, cot, queries, slots):
+    rows, width = cot.shape
+    count = width // HD // 2
+    tall = jax.ShapeDtypeStruct((count, 4 * rows, 2 * rows), jnp.float32)
+    flat = jax.ShapeDtypeStruct((count, 1, 2 * rows), jnp.float32)
+    return pl.pallas_call(
+        local_kernel,
+        out_shape=[tall, tall, flat, flat, flat],
+        in_specs=[SMEM] + [VMEM] * 3,
+        out_specs=[VMEM] * 5,
+        compiler_params=params(VM_LOCAL),
+        cost_estimate=cost(6.0),
+    )(info, cot, queries, slots)
+
+
+def attend_kernel(info, stream, cot, gain, queries, inverse, key_cols, raised_all, gws_all, peaks, totals,
+                  weighted_all, even_block, odd_block, handed, keep_g, beside_g, across_g, corner_g,
+                  low_all, grad_all, dq, products, dk, dv, block, block_t, w0, d0, w1, d1):
     rows, width = stream.shape
     groups = key_cols.shape[0]
     kvw = groups * HD
@@ -97,61 +151,53 @@
     count = groups * pairs
     factor = HD**-0.5
     scale = factor * math.log2(math.e)
-    me, devices, want = info[0], info[1], info[2]
-    odd = me % 2
-    valid = (me > 0, None, me < devices - 1, None, me > 0)
-    block[...] = jnp.where(odd == 1, odd_block[...], even_block[...])
+    me = info[0]
+    valid = me > 0
+    block[...] = jnp.where(me % 2 == 1, odd_block[...], even_block[...])
     for g in range(groups):
         block_t[g] = block[:, g * HD : (g + 1) * HD].T
 
     def stack(ref, i):
         at = 2 * i * HD
         return jnp.concatenate([ref[:, at : at + HD], ref[:, at + HD : at + 2 * HD]], axis=0)
+
+    def columns(i):
+        return slice((i % pairs) * 2 * rows, (i % pairs + 1) * 2 * rows)
 
     def weigh(i, low, grad):
         g = i // pairs
         kc = slice(g * HD, (g + 1) * HD)
         vc = slice(kvw + g * HD, kvw + (g + 1) * HD)
-        q2, do2 = stack(queries, i), stack(cot, i)
-        s4, g4 = dot(slots[:, kc], q2, NT), dot(slots[:, vc], do2, NT)
-        s1, g1 = dot(block[:, kc], q2, NT), dot(block[:, vc], do2, NT)
-        scores = [s4[j * rows : (j + 1) * rows] for j in range(4)] + [s1]
-        gws = [g4[j * rows : (j + 1) * rows] for j in range(4)] + [g1]
-        peak = jnp.max(scores[1], axis=0, keepdims=True)
-        for j in (0, 2, 3, 4):
-            top = jnp.max(scores[j], axis=0, keepdims=True)
-            if valid[j] is not None:
-                top = jnp.where(valid[j], top, -BIG)
-            peak = jnp.maximum(peak, top)
-        peak = peak * scale
-        raised = []
-        total = 0.0
-        weighted = 0.0
-        for j in range(5):
-            shift = peak if valid[j] is None else jnp.where(valid[j], peak, BIG)
-            e = jnp.exp2(scores[j] * scale - shift)
-            total = total + jnp.sum(e, axis=0, keepdims=True)
-            weighted = weighted + jnp.sum(e * gws[j], axis=0, keepdims=True)
-            raised.append(e)
+        s1, g1 = dot(block[:, kc], stack(queries, i), NT), dot(block[:, vc], stack(cot, i), NT)
+        top = jnp.where(valid, jnp.max(s1, axis=0, keepdims=True) * scale, -BIG)
+        peak = jnp.maximum(peaks[i], top)
+        fade = jnp.exp2(peaks[i] - peak)
+        e = jnp.exp2(s1 * scale - jnp.where(valid, peak, BIG))
+        total = totals[i] * fade + jnp.sum(e, axis=0, keepdims=True)
+        weighted = weighted_all[i] * fade + jnp.sum(e * g1, axis=0, keepdims=True)
         share = 1.0 / total
         centre = weighted * share
-        for j in range(5):
-            w = raised[j] * share
-            low[j * rows : (j + 1) * rows] = w.astype(jnp.bfloat16)
-            grad[j * rows : (j + 1) * rows] = (w * (gws[j] - centre)).astype(jnp.bfloat16)
+        fade = fade * share
+        for j in range(4):
+            at = slice(j * rows, (j + 1) * rows)
+            w = raised_all[i, at] * fade
+            low_all[g, at, columns(i)] = w.astype(jnp.bfloat16)
+            grad_all[g, at, columns(i)] = (w * (gws_all[i, at] - centre)).astype(jnp.bfloat16)
+        w = e * share
+        low[...] = w.astype(jnp.bfloat16)
+        grad[...] = (w * (g1 - centre)).astype(jnp.bfloat16)
 
     def spread(i, low, grad):
         g = i // pairs
-        q2, do2 = stack(queries, i), stack(cot, i)
-        value_part = dot(low[...], do2, NN)
-        key_part = dot(grad[...], q2, NN)
+        value_part = dot(low[...], stack(cot, i), NN)
+        key_part = dot(grad[...], stack(queries, i), NN)
         if i % pairs == 0:
             dv[g] = value_part
             dk[g] = key_part
         else:
             dv[g] += value_part
             dk[g] += key_part
-        cols = dot(key_cols[g], grad[: 4 * rows], NN) + dot(block_t[g], grad[4 * rows :], NN)
+        cols = dot(key_cols[g], grad_all[g, :, columns(i)], NN) + dot(block_t[g], grad[...], NN)
         back = cols.T
         for h in range(2):
             s = slice((2 * i + h) * HD, (2 * i + h + 1) * HD)
@@ -179,60 +225,95 @@
     share = rows // 4
 
     def share_at(mask):
-        return pl.multiple_of(4 * rows + ((me % 4) ^ mask) * share, share)
-
-    near_at = pl.multiple_of((1 - odd) * 2 * rows, rows)
-    far_at = pl.multiple_of(odd * 2 * rows, rows)
+        return pl.ds(pl.multiple_of(((me % 4) ^ mask) * share, share), share)
+
     for g in range(groups):
         kc = slice(g * HD, (g + 1) * HD)
         vc = slice(kvw + g * HD, kvw + (g + 1) * HD)
         dk[g] = dk[g] * factor
         for source, cols in ((dk, kc), (dv, vc)):
-            own_g[:, cols] = source[g, rows : 2 * rows]
-            near_g[:rows, cols] = source[g, pl.ds(near_at, rows)].astype(jnp.bfloat16)
-            far_g[:, cols] = source[g, pl.ds(far_at, rows)].astype(jnp.bfloat16)
-            keep_g[:, cols] = source[g, pl.ds(share_at(0), share)]
-            near_g[rows:, cols] = source[g, pl.ds(share_at(1), share)].astype(jnp.bfloat16)
-            across_g[:, cols] = source[g, pl.ds(share_at(2), share)].astype(jnp.bfloat16)
-            corner_g[:, cols] = source[g, pl.ds(share_at(3), share)].astype(jnp.bfloat16)
-            term = source[g, 3 * rows : 4 * rows].astype(jnp.bfloat16)
-            for b in range(partner_count):
-                hit = want == (me ^ (2 << b))
-                partners_g[b][:, cols] = jnp.where(hit, term, jnp.zeros_like(term))
-
-
-def attend(info, stream, cot, gain, queries, inverse, slots, key_cols, even_block, odd_block, partner_count):
+            keep_g[:, cols] = source[g, share_at(0)]
+            beside_g[:, cols] = source[g, share_at(1)].astype(jnp.bfloat16)
+            across_g[:, cols] = source[g, share_at(2)].astype(jnp.bfloat16)
+            corner_g[:, cols] = source[g, share_at(3)].astype(jnp.bfloat16)
+
+
+def attend(info, stream, cot, gain, queries, inverse, key_cols, locals_, even_block, odd_block):
     rows, width = stream.shape
     groups = key_cols.shape[0]
     kvw = groups * HD
-    low = jax.ShapeDtypeStruct((rows, 2 * kvw), jnp.bfloat16)
-    wide = jax.ShapeDtypeStruct((rows, 2 * kvw), jnp.float32)
-    longer = jax.ShapeDtypeStruct((rows + rows // 4, 2 * kvw), jnp.bfloat16)
     kept = jax.ShapeDtypeStruct((rows // 4, 2 * kvw), jnp.float32)
     share = jax.ShapeDtypeStruct((rows // 4, 2 * kvw), jnp.bfloat16)
-    return pl.pallas_call(
-        functools.partial(attend_kernel, partner_count),
-        out_shape=[jax.ShapeDtypeStruct((rows, width), jnp.bfloat16), wide, longer, low, kept, share, share] + [low] * partner_count,
-        in_specs=[SMEM] + [VMEM] * 9,
-        out_specs=[VMEM] * (7 + partner_count),
+    tall = jax.ShapeDtypeStruct((groups, 4 * rows, rows * width // (HD * groups)), jnp.bfloat16)
+    return pl.pallas_call(
+        attend_kernel,
+        out_shape=[jax.ShapeDtypeStruct((rows, width), jnp.bfloat16), kept, share, share, share, tall, tall],
+        in_specs=[SMEM] + [VMEM] * 13,
+        out_specs=[VMEM] * 7,
         scratch_shapes=[
             pltpu.VMEM((rows, width), jnp.float32),
             pltpu.VMEM((rows, HD), jnp.float32),
-            pltpu.VMEM((groups, 5 * rows, HD), jnp.float32),
-            pltpu.VMEM((groups, 5 * rows, HD), jnp.float32),
+            pltpu.VMEM((groups, rows, HD), jnp.float32),
+            pltpu.VMEM((groups, rows, HD), jnp.float32),
             pltpu.VMEM((rows, 2 * kvw), jnp.bfloat16),
             pltpu.VMEM((groups, HD, rows), jnp.bfloat16),
         ]
-        + [pltpu.VMEM((5 * rows, 2 * rows), jnp.bfloat16)] * 4,
+        + [pltpu.VMEM((rows, 2 * rows), jnp.bfloat16)] * 4,
         compiler_params=params(VM_ATTEND),
         cost_estimate=cost(12.0),
-    )(info, stream, cot, gain, queries, inverse, slots, key_cols, even_block, odd_block)
+    )(info, stream, cot, gain, queries, inverse, key_cols, *locals_, even_block, odd_block)
+
+
+def terms_kernel(partner_count, info, cot, queries, low_all, grad_all, *outs):
+    own_g, near_g, far_g = outs[:3]
+    partners_g = outs[3 : 3 + partner_count]
+    term = outs[3 + partner_count]
+    rows, width = cot.shape
+    groups = low_all.shape[0]
+    kvw = groups * HD
+    each = width // groups // HD
+    factor = HD**-0.5
+    me, want = info[0], info[2]
+    odd = me % 2
+    near_at = pl.multiple_of((1 - odd) * 2 * rows, rows)
+    far_at = pl.multiple_of(odd * 2 * rows, rows)
+    for g in range(groups):
+        for part, (weights, ref, base) in enumerate(((grad_all, queries, 0), (low_all, cot, kvw))):
+            heads = [ref[:, (g * each + h) * HD : (g * each + h + 1) * HD] for h in range(each)]
+            n = 2 * g + part
+            cols = slice(base + g * HD, base + (g + 1) * HD)
+            sums = dot(weights[g], jnp.concatenate(heads, axis=0), NN)
+            term[n] = sums * factor if part == 0 else sums
+            own_g[:, cols] = term[n, rows : 2 * rows]
+            near_g[:, cols] = term[n, pl.ds(near_at, rows)].astype(jnp.bfloat16)
+            far_g[:, cols] = term[n, pl.ds(far_at, rows)].astype(jnp.bfloat16)
+            picked = term[n, 3 * rows : 4 * rows].astype(jnp.bfloat16)
+            for b in range(partner_count):
+                hit = want == (me ^ (2 << b))
+                partners_g[b][:, cols] = jnp.where(hit, picked, jnp.zeros_like(picked))
+
+
+def terms_of(info, cot, queries, low_all, grad_all, partner_count):
+    rows = cot.shape[0]
+    groups = low_all.shape[0]
+    kvw = groups * HD
+    low = jax.ShapeDtypeStruct((rows, 2 * kvw), jnp.bfloat16)
+    wide = jax.ShapeDtypeStruct((rows, 2 * kvw), jnp.float32)
+    return pl.pallas_call(
+        functools.partial(terms_kernel, partner_count),
+        out_shape=[wide, low, low] + [low] * partner_count,
+        in_specs=[SMEM] + [VMEM] * 4,
+        out_specs=[VMEM] * (3 + partner_count),
+        scratch_shapes=[pltpu.VMEM((2 * groups, 4 * rows, HD), jnp.float32)],
+        compiler_params=params(VM_TERMS),
+        cost_estimate=cost(5.0),
+    )(info, cot, queries, low_all, grad_all)
 
 
 def collect_kernel(own, *rest):
     total = own[...]
     for ref in rest[:-1]:
-        total = total + ref[: own.shape[0], :].astype(jnp.float32)
+        total = total + ref[...].astype(jnp.float32)
     rest[-1][...] = total
 
 
@@ -247,34 +328,39 @@
     )(own, *parts)
 
 
-def finish_kernel(info, total, received, acc, *rest):
+def finish_kernel(part_count, info, received, own, acc, *rest):
     previous, keys, values = rest[-3:]
+    parts = rest[:part_count]
+    terms = rest[part_count:-6]
     others = rest[-6:-3]
     previous[...] = received[...]
     kvw = keys.shape[1]
     rows = acc.shape[0]
     first = info[0] == 0
     last = acc[...]
-    for ref in rest[:-6]:
+    for ref in terms:
         last = last + ref[...].astype(jnp.float32)
     for k in range(4):
+        at = slice(k * rows, (k + 1) * rows)
+        total = own[at, :]
+        for ref in parts:
+            total = total + ref[at, :].astype(jnp.float32)
         part = last if k == 0 else others[k - 1][...].astype(jnp.float32)
-        part = jnp.where(first, part, 0.0)
-        result = (total[k * rows : (k + 1) * rows, :] + part).astype(jnp.bfloat16)
-        keys[k * rows : (k + 1) * rows, :] = result[:, :kvw]
-        values[k * rows : (k + 1) * rows, :] = result[:, kvw:]
-
-
-def finish(info, total, received, acc, terms, others):
-    shape = jax.ShapeDtypeStruct((total.shape[0], total.shape[1] // 2), jnp.bfloat16)
-    return pl.pallas_call(
-        finish_kernel,
+        result = (total + jnp.where(first, part, 0.0)).astype(jnp.bfloat16)
+        keys[at, :] = result[:, :kvw]
+        values[at, :] = result[:, kvw:]
+
+
+def finish(info, received, own, parts, acc, terms, others):
+    shape = jax.ShapeDtypeStruct((own.shape[0], own.shape[1] // 2), jnp.bfloat16)
+    return pl.pallas_call(
+        functools.partial(finish_kernel, len(parts)),
         out_shape=[jax.ShapeDtypeStruct(received.shape, received.dtype), shape, shape],
-        in_specs=[SMEM] + [VMEM] * (3 + len(terms) + len(others)),
+        in_specs=[SMEM] + [VMEM] * (3 + len(parts) + len(terms) + len(others)),
         out_specs=[VMEM] * 3,
         compiler_params=params(VM_SMALL),
         cost_estimate=cost(0.5),
-    )(info, total, received, acc, *terms, *others)
+    )(info, received, own, acc, *parts, *terms, *others)
 
 
 def permuted(value, pairs, axis="seq"):
@@ -337,11 +423,16 @@
             route = pairs
         moved = permuted(block0, route)
         block0 = jnp.where(among(device, [t for _, t in pairs]), moved, block0)
+    queries, inverse, slots, key_cols = prepare(info, hidden, gain, own, near, far, partners[1:])
+    locals_ = list(local(info, upstream, queries, slots))
+    block0, locals_[2] = lax.optimization_barrier((block0, locals_[2]))
     odd_block = permuted(block0, swaps[0])
-    queries, inverse, slots, key_cols = prepare(info, hidden, gain, own, near, far, partners[1:])
-    outs = attend(info, hidden, upstream, gain, queries, inverse, slots, key_cols, block0, odd_block, bits - 1)
-    handed, own_g, near_g, far_g, keep_g, across_g, corner_g = outs[:7]
-    partners_g = outs[7:]
+    handed, keep_g, beside_g, across_g, corner_g, low_all, grad_all = attend(
+        info, hidden, upstream, gain, queries, inverse, key_cols, locals_, block0, odd_block
+    )
+    outs = terms_of(info, upstream, queries, low_all, grad_all, bits - 1)
+    own_g, near_g, far_g = outs[:3]
+    partners_g = outs[3:]
 
     sections = lax.axis_size("section")
     back = [((i + 1) % sections, i) for i in range(sections)]
@@ -352,12 +443,11 @@
 
     received = permuted(handed, back, "section")
     near_r = permuted(near_g, swaps[0])
-    parts = [near_r, permuted(partners_g[0], swaps[1])]
-    for b in reversed(range(2, bits)):
-        parts.append(permuted(partners_g[b - 1], swaps[b]))
-    parts.append(permuted(far_g, across))
-
-    terms = [near_r[rows:], swapped(across_g, 2), swapped(corner_g, 3)]
+    y_r = permuted(partners_g[0], swaps[1])
+    far_r = permuted(far_g, across)
+    z_r = [permuted(partners_g[b - 1], swaps[b]) for b in range(2, bits)]
+
+    terms = [swapped(beside_g, 1), swapped(across_g, 2), swapped(corner_g, 3)]
     acc = keep_g
     for b in range(2, bits, 2):
         acc = acc + sum(t.astype(jnp.float32) for t in terms)
@@ -365,8 +455,9 @@
         terms = [swapped(low, k << b) for k in range(1, 1 << min(2, bits - b))]
     mine = (acc + sum(t.astype(jnp.float32) for t in terms)).astype(jnp.bfloat16)
     others = [swapped(mine, mask) for mask in (1, 2, 3)]
-    total = collect(own_g, parts)
-    previous, key_grads, value_grads = finish(info, total, received, acc, terms, others)
+    own_g = collect(own_g, z_r)
+    parts = [near_r, y_r, far_r]
+    previous, key_grads, value_grads = finish(info, received, own_g, parts, acc, terms, others)
     return (previous[None], key_grads[None], value_grads[None])
 
 

time: 77.4 us -> 75.3 us (0.973)
  waiting for transfers between devices: 31.2 us -> 27.1 us
  starting transfers between devices: 28.8 us -> 25.5 us
  Pallas kernels: 14.3 us -> 16.7 us
  local copies, waits for them, and re-layouts: 0.02 us -> 1.96 us
  other arithmetic: 1.4 us -> 2.34 us
    ppermute x22 -> x23, waiting for transfers between devices: 31.2 us -> 27.1 us  [permuted(): return lax.ppermute(value, axis, pairs)]
    ppermute x22 -> x23, starting transfers between devices: 28.8 us -> 25.5 us  [permuted(): return lax.ppermute(value, axis, pairs)]
    pallas_call x2 -> x4, Pallas kernels: 12.8 us -> 15.3 us  [the longest x1 5.38 us: attend(): pl.pallas_call(attend_kernel, out_shape=[jax.ShapeDtypeStruct((rows, widt...]
    unnamed x10, local copies, waits for them, and re-layouts: 0.02 us -> 1.96 us
    select_n x1, other arithmetic: 0.2 us -> 1.18 us  [on_device(): block0 = jnp.where(device == 1 << b, partners[b], block0)]
  transfers between devices with their start and end apart: 22 -> 23, of which waited for: 12 -> 12; matrix products, arithmetic and copies ran while one was open for 0% -> 2% of each run, Pallas kernels for 2% -> 13%
where the time goes in v4:
time: 75.3 us; the launch traced here: 75 us
  waiting for transfers between devices  27.1 us (36%)
  starting transfers between devices  25.5 us (34%)
  Pallas kernels  16.7 us (22%)
  other arithmetic  2.34 us (3%)
  local copies, waits for them, and re-layouts  1.96 us (3%)
  between operations  1.46 us (2%)
    ppermute x23, waiting for transfers between devices, permuted(): return lax.ppermute(value, axis, pairs)  27.1 us
    ppermute x23, starting transfers between devices, permuted(): return lax.ppermute(value, axis, pairs)  25.5 us
    pallas_call x1, Pallas kernels, attend(): pl.pallas_call(attend_kernel, out_shape=[jax.ShapeDtypeStruct((rows, widt...  5.38 us
    pallas_call x1, Pallas kernels, local(): pl.pallas_call(local_kernel, out_shape=[tall, tall, flat, flat, flat], in...  5.06 us
    pallas_call x1, Pallas kernels, terms_of(): pl.pallas_call(functools.partial(terms_kernel, partner_count), out_shape=...  3.08 us
    unnamed x10, local copies, waits for them, and re-layouts  1.96 us
    pallas_call x1, Pallas kernels, finish(): pl.pallas_call(functools.partial(finish_kernel, len(parts)), out_shape=[j...  1.76 us
  transfers between devices with their start and end apart: 23, of which 12 were waited for; matrix products, arithmetic and copies ran while one was open for 2% of the time, Pallas kernels for 13%

profile of v4, /device:TPU:0, one launch (start us, length us, event | category | flops | bytes accessed | tf_op | source)
XLA Modules:
  0.0 75.0 jit_solution(4796824678461027933)
XLA Ops:
  0.6 1.0 %pad_maximum_fusion.own = bf16[128,1024]{1,0:T(8,128)(2,1)S(1)} fusion(bf16[128,512]{1,0:T(8,128)(2,1)} %bitcast.15, bf16[128,512]{1,0:T(8,128)(2,1)} %bitcast.17), kind=kLoop, calls=%fused_computation | loop fusion | flops 524288 | bytes 524288 | tf_op jit(solution)/shard_map/concatenate | solution.py:399
  1.6 7.0 %collective-permute-start.4 = (bf16[128,1024]{1,0:T(8,128)(2,1)S(1)}, bf16[128,1024]{1,0:T(8,128)(2,1)S(1)}, u32[]{:S(2)}, u32[]{:S(2)}) collective-permute-start(bf16[128,1024]{1,0:T(8,128)(2,1)S(1)} %pad_maximum_fusion.own), channel_id=1, source_target_pairs={{0,12},{16,28}} | collective-permute-start | bytes 786440 | tf_op jit(solution)/shard_map/ppermute | solution.py:367
  10.8 4.2 %collective-permute-done.4 = bf16[128,1024]{1,0:T(8,128)(2,1)S(1)} collective-permute-done((bf16[128,1024]{1,0:T(8,128)(2,1)S(1)}, bf16[128,1024]{1,0:T(8,128)(2,1)S(1)}, u32[]{:S(2)}, u32[]{:S(2)}) %collective-permute-start.4) | collective-permute-done | bytes 262176 | tf_op jit(solution)/shard_map/ppermute | solution.py:367
  15.1 2.7 %collective-permute-done.2.rest_1_ = bf16[128,1024]{1,0:T(8,128)(2,1)S(1)} collective-permute-done((bf16[128,1024]{1,0:T(8,128)(2,1)S(1)}, bf16[128,1024]{1,0:T(8,128)(2,1)S(1)}, u32[]{:S(2)}, u32[]{:S(2)}) %collective-permute-start.2) | collective-permute-done | bytes 262176 | tf_op jit(solution)/shard_map/ppermute | solution.py:367
  17.9 3.8 %collective-permute-done.1.rest_2_ = bf16[128,1024]{1,0:T(8,128)(2,1)S(1)} collective-permute-done((bf16[128,1024]{1,0:T(8,128)(2,1)S(1)}, bf16[128,1024]{1,0:T(8,128)(2,1)S(1)}, u32[]{:S(2)}, u32[]{:S(2)}) %collective-permute-start.1) | collective-permute-done | bytes 262176 | tf_op jit(solution)/shard_map/ppermute | solution.py:367
  21.7 1.2 %select_select_fusion = bf16[128,1024]{1,0:T(8,128)(2,1)S(1)} fusion(bf16[128,1024]{1,0:T(8,128)(2,1)S(1)} %collective-permute-done.1.rest_2_, bf16[128,1024]{1,0:T(8,128)(2,1)S(1)} %collective-permute-done.2.rest_1_, bf16[128,1024]{1,0:T(8,128)(2,1)S(1)} %collective-permute-done.3.rest_0_, bf16[128,1024]{1,0:T(8,128)(2,1)S(1)} %collective-permute-done.4, ...), kind=kLoop, calls=%fused_computation.1 | loop fusion | flops 1048576 | bytes 1572868 | tf_op jit(solution)/shard_map/jit(_where)/select_n | solution.py:416
  22.9 1.4 %collective-permute-start.6 = (bf16[128,1024]{1,0:T(8,128)(2,1)S(1)}, bf16[128,1024]{1,0:T(8,128)(2,1)S(1)}, u32[]{:S(2)}, u32[]{:S(2)}) collective-permute-start(bf16[128,1024]{1,0:T(8,128)(2,1)S(1)} %select_select_fusion), channel_id=1, source_target_pairs={{0,2},{1,3},{2,0},{3,1},{4,6},{5,7},{6,4},{7,5},{8,10},{9,11},{10,... | collective-permute-start | bytes 786440 | tf_op jit(solution)/shard_map/ppermute | solution.py:367
  24.3 1.2 %copy-done = bf16[1,128,4096]{2,1,0:T(8,128)(2,1)S(1)} copy-done((bf16[1,128,4096]{2,1,0:T(8,128)(2,1)S(1)}, bf16[1,128,4096]{2,1,0:T(8,128)(2,1)}, u32[]{:S(2)}) %copy-start) | copy-done | bytes 1048600
  26.2 1.3 %shard_map.85 = (bf16[128,4096]{1,0:T(8,128)(2,1)S(1)}, f32[128,128]{1,0:T(8,128)S(1)}, bf16[512,1024]{1,0:T(8,128)(2,1)S(1)}, bf16[4,128,512]{2,1,0:T(8,128)(2,1)S(1)}) custom-call(s32[3]{0:T(128)S(1)} %pad_add_fusion.info, bf16[128,4096]{1,0:T(8,128)(2,1)S(1)} %bitcast.10, f32[1,4096]{1,0:T(1,128)S(1)} %copy-done.3, ...), custom_call_target="tpu_custom_call" | custom-call | flops 6899999744 | bytes 1048576 | tf_op jit(solution)/shard_map/pallas_call | solution.py:74
  27.6 5.1 %shard_map.86 = (f32[16,512,256]{2,1,0:T(8,128)S(1)}, f32[16,512,256]{2,1,0:T(8,128)S(1)}, f32[16,1,256]{2,1,0:T(1,128)S(1)}, f32[16,1,256]{2,1,0:T(1,128)S(1)}, f32[16,1,256]{2,1,0:T(1,128)S(1)}) custom-call(s32[3]{0:T(128)S(1)} %pad_add_fusion.info, bf16[128,4096]{1,0:T(8,128)(2,1)S(1)} %bitcast.12, bf16[128,4096]{1,0:T(8,128)(2,1)S(1)} %get-tuple-element.33.queries, ...), custom_call_target="tpu_custom_call" | custom-call | flops 6899999744 | bytes 1048576 | tf_op jit(solution)/shard_map/pallas_call | solution.py:133
  32.8 1.5 %collective-permute-done.7.odd_block = bf16[128,1024]{1,0:T(8,128)(2,1)S(1)} collective-permute-done((bf16[128,1024]{1,0:T(8,128)(2,1)S(1)}, bf16[128,1024]{1,0:T(8,128)(2,1)S(1)}, u32[]{:S(2)}, u32[]{:S(2)}) %collective-permute-start.7) | collective-permute-done | bytes 262176 | tf_op jit(solution)/shard_map/ppermute | solution.py:367
  34.3 5.4 %shard_map.87 = (bf16[128,4096]{1,0:T(8,128)(2,1)S(1)}, f32[32,1024]{1,0:T(8,128)S(1)}, bf16[32,1024]{1,0:T(8,128)(2,1)S(1)}, bf16[32,1024]{1,0:T(8,128)(2,1)S(1...) custom-call(s32[3]{0:T(128)S(1)} %pad_add_fusion.info, ...), custom_call_target="tpu_custom_call" | custom-call | flops 13799999488 | bytes 1048576 | tf_op jit(solution)/shard_map/pallas_call | solution.py:248
  40.6 1.0 %collective-permute-start.13 = (bf16[32,1024]{1,0:T(8,128)(2,1)S(1)}, bf16[32,1024]{1,0:T(8,128)(2,1)S(1)}, u32[]{:S(2)}, u32[]{:S(2)}) collective-permute-start(bf16[32,1024]{1,0:T(8,128)(2,1)S(1)} %get-tuple-element.54), channel_id=1, source_target_pairs={{0,3},{1,2},{2,1},{3,0},{4,7},{5,6},{6,5},{7,4},{8,11},{9,10},{10,... | collective-permute-start | bytes 196616 | tf_op jit(solution)/shard_map/ppermute | solution.py:367
  41.6 1.5 %collective-permute-start.8 = (bf16[128,4096]{1,0:T(8,128)(2,1)S(1)}, bf16[128,4096]{1,0:T(8,128)(2,1)S(1)}, u32[]{:S(2)}, u32[]{:S(2)}) collective-permute-start(bf16[128,4096]{1,0:T(8,128)(2,1)S(1)} %get-tuple-element.45), channel_id=1, source_target_pairs={{16,0},{0,16},{17,1},{1,17},{18,2},{2,18},{19,3},{3,19},{20,4},{4,... | collective-permute-start | bytes 3145736 | tf_op jit(solution)/shard_map/ppermute | solution.py:367
  43.1 1.7 %collective-permute-done.12 = bf16[32,1024]{1,0:T(8,128)(2,1)S(1)} collective-permute-done((bf16[32,1024]{1,0:T(8,128)(2,1)S(1)}, bf16[32,1024]{1,0:T(8,128)(2,1)S(1)}, u32[]{:S(2)}, u32[]{:S(2)}) %collective-permute-start.12) | collective-permute-done | bytes 65568 | tf_op jit(solution)/shard_map/ppermute | solution.py:367
  45.1 4.3 %collective-permute-start.19 = (bf16[32,1024]{1,0:T(8,128)(2,1)S(1)}, bf16[32,1024]{1,0:T(8,128)(2,1)S(1)}, u32[]{:S(2)}, u32[]{:S(2)}) collective-permute-start(bf16[32,1024]{1,0:T(8,128)(2,1)S(1)} %get-tuple-element.61), channel_id=1, source_target_pairs={{0,12},{1,13},{2,14},{3,15},{4,8},{5,9},{6,10},{7,11},{8,4},{9,5},... | collective-permute-start | bytes 196616 | tf_op jit(solution)/shard_map/ppermute | solution.py:367
  50.1 3.1 %shard_map.88 = (f32[128,1024]{1,0:T(8,128)S(1)}, bf16[128,1024]{1,0:T(8,128)(2,1)S(1)}, bf16[128,1024]{1,0:T(8,128)(2,1)S(1)}, bf16[128,1024]{1,0:T(8,128)(2,1)...) custom-call(s32[3]{0:T(128)S(1)} %pad_add_fusion.info, bf16[128,4096]{1,0:T(8,128)(2,1)S(1)} %bitcast.14, ...), custom_call_target="tpu_custom_call" | custom-call | flops 5750000128 | bytes 1048576 | tf_op jit(solution)/shard_map/pallas_call | solution.py:302
  53.2 1.5 %collective-permute-start.9 = (bf16[128,1024]{1,0:T(8,128)(2,1)S(1)}, bf16[128,1024]{1,0:T(8,128)(2,1)S(1)}, u32[]{:S(2)}, u32[]{:S(2)}) collective-permute-start(bf16[128,1024]{1,0:T(8,128)(2,1)S(1)} %get-tuple-element.49), channel_id=1, source_target_pairs={{0,4},{1,5},{2,6},{3,7},{4,0},{5,1},{6,2},{7,3},{8,12},{9,13},{10,... | collective-permute-start | bytes 786440 | tf_op jit(solution)/shard_map/ppermute | solution.py:367
  56.7 2.0 %collective-permute-start.10 = (bf16[128,1024]{1,0:T(8,128)(2,1)S(1)}, bf16[128,1024]{1,0:T(8,128)(2,1)S(1)}, u32[]{:S(2)}, u32[]{:S(2)}) collective-permute-start(bf16[128,1024]{1,0:T(8,128)(2,1)S(1)} %get-tuple-element.50), channel_id=1, source_target_pairs={{0,8},{1,9},{2,10},{3,11},{4,12},{5,13},{6,14},{7,15},{8,0},{9,1},... | collective-permute-start | bytes 786440 | tf_op jit(solution)/shard_map/ppermute | solution.py:367
  59.8 1.2 %collective-permute-done.21.rest_7_ = bf16[32,1024]{1,0:T(8,128)(2,1)S(1)} collective-permute-done((bf16[32,1024]{1,0:T(8,128)(2,1)S(1)}, bf16[32,1024]{1,0:T(8,128)(2,1)S(1)}, u32[]{:S(2)}, u32[]{:S(2)}) %collective-permute-start.21) | collective-permute-done | bytes 65568 | tf_op jit(solution)/shard_map/ppermute | solution.py:367
  61.0 1.2 %collective-permute-start.15 = (bf16[128,1024]{1,0:T(8,128)(2,1)S(1)}, bf16[128,1024]{1,0:T(8,128)(2,1)S(1)}, u32[]{:S(2)}, u32[]{:S(2)}) collective-permute-start(bf16[128,1024]{1,0:T(8,128)(2,1)S(1)} %get-tuple-element.56), channel_id=1, source_target_pairs={{0,2},{1,3},{2,0},{3,1},{4,6},{5,7},{6,4},{7,5},{8,10},{9,11},{10,... | collective-permute-start | bytes 786440 | tf_op jit(solution)/shard_map/ppermute | solution.py:367
  63.7 8.3 %collective-permute-done.10.rest_1_ = bf16[128,1024]{1,0:T(8,128)(2,1)S(1)} collective-permute-done((bf16[128,1024]{1,0:T(8,128)(2,1)S(1)}, bf16[128,1024]{1,0:T(8,128)(2,1)S(1)}, u32[]{:S(2)}, u32[]{:S(2)}) %collective-permute-start.10) | collective-permute-done | bytes 262176 | tf_op jit(solution)/shard_map/ppermute | solution.py:367
  72.0 1.2 %collective-permute-done.20.rest_6_ = bf16[32,1024]{1,0:T(8,128)(2,1)S(1)} collective-permute-done((bf16[32,1024]{1,0:T(8,128)(2,1)S(1)}, bf16[32,1024]{1,0:T(8,128)(2,1)S(1)}, u32[]{:S(2)}, u32[]{:S(2)}) %collective-permute-start.20) | collective-permute-done | bytes 65568 | tf_op jit(solution)/shard_map/ppermute | solution.py:367
  73.2 1.8 %shard_map.90 = (bf16[128,4096]{1,0:T(8,128)(2,1)}, bf16[128,512]{1,0:T(8,128)(2,1)}, bf16[128,512]{1,0:T(8,128)(2,1)}) custom-call(s32[3]{0:T(128)S(1)} %pad_add_fusion.info, bf16[128,4096]{1,0:T(8,128)(2,1)S(1)} %collective-permute-done.8.received, f32[128,1024]{1,0:T(8,128)S(1)} %shard_map.89.own, f32[32,1024]{1,0:T(8,128)S(1)} %get-tuple-element.62.acc, ...), custom_call_target="tpu_custom_call" | custom-call | flops 575000000 | bytes 1048576 | tf_op jit(solution)/shard_map/pallas_call | solution.py:356
  (44 shorter events, 9.1 us)
Async XLA Ops:
  1.6 13.4 %collective-permute-start.4 = (bf16[128,1024]{1,0:T(8,128)(2,1)S(1)}, bf16[128,1024]{1,0:T(8,128)(2,1)S(1)}, u32[]{:S(2)}, u32[]{:S(2)}) collective-permute-start(bf16[128,1024]{1,0:T(8,128)(2,1)S(1)} %pad_maximum_fusion.own), channel_id=1, source_target_pairs={{0,12},{16,28}} | collective-permute-start | bytes 786440 | tf_op jit(solution)/shard_map/ppermute | solution.py:367
  8.6 6.5 %collective-permute-start.3 = (bf16[128,1024]{1,0:T(8,128)(2,1)S(1)}, bf16[128,1024]{1,0:T(8,128)(2,1)S(1)}, u32[]{:S(2)}, u32[]{:S(2)}) collective-permute-start(bf16[128,1024]{1,0:T(8,128)(2,1)S(1)} %pad_maximum_fusion.own), channel_id=1, source_target_pairs={{0,2},{1,3},{2,0},{3,1},{4,6},{5,7},{6,4},{7,5},{8,10},{9,11},{10,... | collective-permute-start | bytes 786440 | tf_op jit(solution)/shard_map/ppermute | solution.py:367
  8.7 9.2 %collective-permute-start.2 = (bf16[128,1024]{1,0:T(8,128)(2,1)S(1)}, bf16[128,1024]{1,0:T(8,128)(2,1)S(1)}, u32[]{:S(2)}, u32[]{:S(2)}) collective-permute-start(bf16[128,1024]{1,0:T(8,128)(2,1)S(1)} %pad_maximum_fusion.own), channel_id=1, source_target_pairs={{0,4},{1,5},{2,6},{3,7},{4,0},{5,1},{6,2},{7,3},{8,12},{9,13},{10,... | collective-permute-start | bytes 786440 | tf_op jit(solution)/shard_map/ppermute | solution.py:367
  8.8 13.0 %collective-permute-start.1 = (bf16[128,1024]{1,0:T(8,128)(2,1)S(1)}, bf16[128,1024]{1,0:T(8,128)(2,1)S(1)}, u32[]{:S(2)}, u32[]{:S(2)}) collective-permute-start(bf16[128,1024]{1,0:T(8,128)(2,1)S(1)} %pad_maximum_fusion.own), channel_id=1, source_target_pairs={{0,8},{1,9},{2,10},{3,11},{4,12},{5,13},{6,14},{7,15},{8,0},{9,1},... | collective-permute-start | bytes 786440 | tf_op jit(solution)/shard_map/ppermute | solution.py:367
  9.5 13.4 %collective-permute-start.5 = (bf16[128,1024]{1,0:T(8,128)(2,1)S(1)}, bf16[128,1024]{1,0:T(8,128)(2,1)S(1)}, u32[]{:S(2)}, u32[]{:S(2)}) collective-permute-start(bf16[128,1024]{1,0:T(8,128)(2,1)S(1)} %pad_maximum_fusion.own), channel_id=1, source_target_pairs={{1,2},{3,4},{5,6},{7,8},{9,10},{11,12},{13,14},{2,1},{4,3},{6,5},{... | collective-permute-start | bytes 786440 | tf_op jit(solution)/shard_map/ppermute | solution.py:367
  15.1 9.2 %collective-permute-start = (bf16[128,1024]{1,0:T(8,128)(2,1)S(1)}, bf16[128,1024]{1,0:T(8,128)(2,1)S(1)}, u32[]{:S(2)}, u32[]{:S(2)}) collective-permute-start(bf16[128,1024]{1,0:T(8,128)(2,1)S(1)} %pad_maximum_fusion.own), channel_id=1, source_target_pairs={{0,1},{1,0},{2,3},{3,2},{4,5},{5,4},{6,7},{7,6},{8,9},{9,8},{10,11... | collective-permute-start | bytes 786440 | tf_op jit(solution)/shard_map/ppermute | solution.py:367
  22.9 9.7 %collective-permute-start.6 = (bf16[128,1024]{1,0:T(8,128)(2,1)S(1)}, bf16[128,1024]{1,0:T(8,128)(2,1)S(1)}, u32[]{:S(2)}, u32[]{:S(2)}) collective-permute-start(bf16[128,1024]{1,0:T(8,128)(2,1)S(1)} %select_select_fusion), channel_id=1, source_target_pairs={{0,2},{1,3},{2,0},{3,1},{4,6},{5,7},{6,4},{7,5},{8,10},{9,11},{10,... | collective-permute-start | bytes 786440 | tf_op jit(solution)/shard_map/ppermute | solution.py:367
  27.5 6.7 %copy-start.1 = (bf16[1,128,4096]{2,1,0:T(8,128)(2,1)S(1)}, bf16[1,128,4096]{2,1,0:T(8,128)(2,1)}, u32[]{:S(2)}) copy-start(bf16[1,128,4096]{2,1,0:T(8,128)(2,1)} %param.6) | copy-start | bytes 3145732
  32.7 1.6 %collective-permute-start.7 = (bf16[128,1024]{1,0:T(8,128)(2,1)S(1)}, bf16[128,1024]{1,0:T(8,128)(2,1)S(1)}, u32[]{:S(2)}, u32[]{:S(2)}) collective-permute-start(bf16[128,1024]{1,0:T(8,128)(2,1)S(1)} %broadcast_select_fusion.even_block), channel_id=1, source_target_pairs={{0,1},{1,0},{2,3},{3,2},{4,5},{5,4},{6,7},{7,6},{8,9},{9,8},{10,11... | collective-permute-start | bytes 786440 | tf_op jit(solution)/shard_map/ppermute | solution.py:367
  39.7 3.4 %collective-permute-start.11 = (bf16[32,1024]{1,0:T(8,128)(2,1)S(1)}, bf16[32,1024]{1,0:T(8,128)(2,1)S(1)}, u32[]{:S(2)}, u32[]{:S(2)}) collective-permute-start(bf16[32,1024]{1,0:T(8,128)(2,1)S(1)} %get-tuple-element.52), channel_id=1, source_target_pairs={{0,1},{1,0},{2,3},{3,2},{4,5},{5,4},{6,7},{7,6},{8,9},{9,8},{10,11... | collective-permute-start | bytes 196616 | tf_op jit(solution)/shard_map/ppermute | solution.py:367
  39.9 4.9 %collective-permute-start.12 = (bf16[32,1024]{1,0:T(8,128)(2,1)S(1)}, bf16[32,1024]{1,0:T(8,128)(2,1)S(1)}, u32[]{:S(2)}, u32[]{:S(2)}) collective-permute-start(bf16[32,1024]{1,0:T(8,128)(2,1)S(1)} %get-tuple-element.53), channel_id=1, source_target_pairs={{0,2},{1,3},{2,0},{3,1},{4,6},{5,7},{6,4},{7,5},{8,10},{9,11},{10,... | collective-permute-start | bytes 196616 | tf_op jit(solution)/shard_map/ppermute | solution.py:367
  40.6 4.5 %collective-permute-start.13 = (bf16[32,1024]{1,0:T(8,128)(2,1)S(1)}, bf16[32,1024]{1,0:T(8,128)(2,1)S(1)}, u32[]{:S(2)}, u32[]{:S(2)}) collective-permute-start(bf16[32,1024]{1,0:T(8,128)(2,1)S(1)} %get-tuple-element.54), channel_id=1, source_target_pairs={{0,3},{1,2},{2,1},{3,0},{4,7},{5,6},{6,5},{7,4},{8,11},{9,10},{10,... | collective-permute-start | bytes 196616 | tf_op jit(solution)/shard_map/ppermute | solution.py:367
  41.6 31.6 %collective-permute-start.8 = (bf16[128,4096]{1,0:T(8,128)(2,1)S(1)}, bf16[128,4096]{1,0:T(8,128)(2,1)S(1)}, u32[]{:S(2)}, u32[]{:S(2)}) collective-permute-start(bf16[128,4096]{1,0:T(8,128)(2,1)S(1)} %get-tuple-element.45), channel_id=1, source_target_pairs={{16,0},{0,16},{17,1},{1,17},{18,2},{2,18},{19,3},{3,19},{20,4},{4,... | collective-permute-start | bytes 3145736 | tf_op jit(solution)/shard_map/ppermute | solution.py:367
  45.1 9.5 %collective-permute-start.19 = (bf16[32,1024]{1,0:T(8,128)(2,1)S(1)}, bf16[32,1024]{1,0:T(8,128)(2,1)S(1)}, u32[]{:S(2)}, u32[]{:S(2)}) collective-permute-start(bf16[32,1024]{1,0:T(8,128)(2,1)S(1)} %get-tuple-element.61), channel_id=1, source_target_pairs={{0,12},{1,13},{2,14},{3,15},{4,8},{5,9},{6,10},{7,11},{8,4},{9,5},... | collective-permute-start | bytes 196616 | tf_op jit(solution)/shard_map/ppermute | solution.py:367
  49.4 5.7 %collective-permute-start.18 = (bf16[32,1024]{1,0:T(8,128)(2,1)S(1)}, bf16[32,1024]{1,0:T(8,128)(2,1)S(1)}, u32[]{:S(2)}, u32[]{:S(2)}) collective-permute-start(bf16[32,1024]{1,0:T(8,128)(2,1)S(1)} %get-tuple-element.61), channel_id=1, source_target_pairs={{0,8},{1,9},{2,10},{3,11},{4,12},{5,13},{6,14},{7,15},{8,0},{9,1},... | collective-permute-start | bytes 196616 | tf_op jit(solution)/shard_map/ppermute | solution.py:367
  49.4 5.7 %collective-permute-start.17 = (bf16[32,1024]{1,0:T(8,128)(2,1)S(1)}, bf16[32,1024]{1,0:T(8,128)(2,1)S(1)}, u32[]{:S(2)}, u32[]{:S(2)}) collective-permute-start(bf16[32,1024]{1,0:T(8,128)(2,1)S(1)} %get-tuple-element.61), channel_id=1, source_target_pairs={{0,4},{1,5},{2,6},{3,7},{4,0},{5,1},{6,2},{7,3},{8,12},{9,13},{10,... | collective-permute-start | bytes 196616 | tf_op jit(solution)/shard_map/ppermute | solution.py:367
  53.2 9.8 %collective-permute-start.9 = (bf16[128,1024]{1,0:T(8,128)(2,1)S(1)}, bf16[128,1024]{1,0:T(8,128)(2,1)S(1)}, u32[]{:S(2)}, u32[]{:S(2)}) collective-permute-start(bf16[128,1024]{1,0:T(8,128)(2,1)S(1)} %get-tuple-element.49), channel_id=1, source_target_pairs={{0,4},{1,5},{2,6},{3,7},{4,0},{5,1},{6,2},{7,3},{8,12},{9,13},{10,... | collective-permute-start | bytes 786440 | tf_op jit(solution)/shard_map/ppermute | solution.py:367
  55.2 4.4 %collective-permute-start.22 = (bf16[32,1024]{1,0:T(8,128)(2,1)S(1)}, bf16[32,1024]{1,0:T(8,128)(2,1)S(1)}, u32[]{:S(2)}, u32[]{:S(2)}) collective-permute-start(bf16[32,1024]{1,0:T(8,128)(2,1)S(1)} %add_convert_fusion), channel_id=1, source_target_pairs={{0,3},{1,2},{2,1},{3,0},{4,7},{5,6},{6,5},{7,4},{8,11},{9,10},{10,... | collective-permute-start | bytes 196616 | tf_op jit(solution)/shard_map/ppermute | solution.py:367
  55.9 5.1 %collective-permute-start.21 = (bf16[32,1024]{1,0:T(8,128)(2,1)S(1)}, bf16[32,1024]{1,0:T(8,128)(2,1)S(1)}, u32[]{:S(2)}, u32[]{:S(2)}) collective-permute-start(bf16[32,1024]{1,0:T(8,128)(2,1)S(1)} %add_convert_fusion), channel_id=1, source_target_pairs={{0,2},{1,3},{2,0},{3,1},{4,6},{5,7},{6,4},{7,5},{8,10},{9,11},{10,... | collective-permute-start | bytes 196616 | tf_op jit(solution)/shard_map/ppermute | solution.py:367
  56.7 15.2 %collective-permute-start.10 = (bf16[128,1024]{1,0:T(8,128)(2,1)S(1)}, bf16[128,1024]{1,0:T(8,128)(2,1)S(1)}, u32[]{:S(2)}, u32[]{:S(2)}) collective-permute-start(bf16[128,1024]{1,0:T(8,128)(2,1)S(1)} %get-tuple-element.50), channel_id=1, source_target_pairs={{0,8},{1,9},{2,10},{3,11},{4,12},{5,13},{6,14},{7,15},{8,0},{9,1},... | collective-permute-start | bytes 786440 | tf_op jit(solution)/shard_map/ppermute | solution.py:367
  59.5 13.7 %collective-permute-start.14 = (bf16[128,1024]{1,0:T(8,128)(2,1)S(1)}, bf16[128,1024]{1,0:T(8,128)(2,1)S(1)}, u32[]{:S(2)}, u32[]{:S(2)}) collective-permute-start(bf16[128,1024]{1,0:T(8,128)(2,1)S(1)} %get-tuple-element.55), channel_id=1, source_target_pairs={{0,1},{1,0},{2,3},{3,2},{4,5},{5,4},{6,7},{7,6},{8,9},{9,8},{10,11... | collective-permute-start | bytes 786440 | tf_op jit(solution)/shard_map/ppermute | solution.py:367
  61.0 12.2 %collective-permute-start.15 = (bf16[128,1024]{1,0:T(8,128)(2,1)S(1)}, bf16[128,1024]{1,0:T(8,128)(2,1)S(1)}, u32[]{:S(2)}, u32[]{:S(2)}) collective-permute-start(bf16[128,1024]{1,0:T(8,128)(2,1)S(1)} %get-tuple-element.56), channel_id=1, source_target_pairs={{0,2},{1,3},{2,0},{3,1},{4,6},{5,7},{6,4},{7,5},{8,10},{9,11},{10,... | collective-permute-start | bytes 786440 | tf_op jit(solution)/shard_map/ppermute | solution.py:367
  63.0 10.2 %collective-permute-start.16 = (bf16[128,1024]{1,0:T(8,128)(2,1)S(1)}, bf16[128,1024]{1,0:T(8,128)(2,1)S(1)}, u32[]{:S(2)}, u32[]{:S(2)}) collective-permute-start(bf16[128,1024]{1,0:T(8,128)(2,1)S(1)} %get-tuple-element.57), channel_id=1, source_target_pairs={{1,2},{3,4},{5,6},{7,8},{9,10},{11,12},{13,14},{2,1},{4,3},{6,5},{... | collective-permute-start | bytes 786440 | tf_op jit(solution)/shard_map/ppermute | solution.py:367
  72.0 1.3 %collective-permute-start.20 = (bf16[32,1024]{1,0:T(8,128)(2,1)S(1)}, bf16[32,1024]{1,0:T(8,128)(2,1)S(1)}, u32[]{:S(2)}, u32[]{:S(2)}) collective-permute-start(bf16[32,1024]{1,0:T(8,128)(2,1)S(1)} %add_convert_fusion), channel_id=1, source_target_pairs={{0,1},{1,0},{2,3},{3,2},{4,5},{5,4},{6,7},{7,6},{8,9},{9,8},{10,11... | collective-permute-start | bytes 196616 | tf_op jit(solution)/shard_map/ppermute | solution.py:367
  (4 other events, 10.0 us)

commit v5 on v4

--- a/solution.py
+++ b/solution.py
@@ -36,11 +36,36 @@
 SMEM = pl.BlockSpec(memory_space=pltpu.SMEM)
 
 
-def prepare_kernel(partner_count, info, stream, gain, own, near, far, *rest):
+def norm_kernel(stream, gain, queries, inverse):
+    rows, width = stream.shape
+    squares = jnp.zeros((rows, HD), jnp.float32)
+    for i in range(width // HD):
+        x = stream[:, i * HD : (i + 1) * HD].astype(jnp.float32)
+        squares = squares + x * x
+    inv = lax.rsqrt(jnp.sum(squares, axis=1, keepdims=True) / width + 1e-5)
+    inv = jnp.broadcast_to(inv, (rows, HD))
+    inverse[...] = inv
+    for i in range(width // HD):
+        s = slice(i * HD, (i + 1) * HD)
+        queries[:, s] = (stream[:, s].astype(jnp.float32) * inv * gain[:, s]).astype(jnp.bfloat16)
+
+
+def norm(stream, gain):
+    rows, width = stream.shape
+    return pl.pallas_call(
+        norm_kernel,
+        out_shape=[jax.ShapeDtypeStruct((rows, width), jnp.bfloat16), jax.ShapeDtypeStruct((rows, HD), jnp.float32)],
+        in_specs=[VMEM] * 2,
+        out_specs=[VMEM] * 2,
+        compiler_params=params(VM_SMALL),
+        cost_estimate=cost(2.0),
+    )(stream, gain)
+
+
+def arrange_kernel(partner_count, info, own, near, far, *rest):
     partners = rest[:partner_count]
-    queries, inverse, slots, key_cols = rest[partner_count:]
-    rows, width = stream.shape
-    groups = key_cols.shape[0]
+    slots, key_cols = rest[partner_count:]
+    rows = own.shape[0]
     me, want = info[0], info[2]
     odd = me % 2
     near_at = pl.multiple_of((1 - odd) * 2 * rows, rows)
@@ -53,37 +78,24 @@
         @pl.when(want == (me ^ (2 << b)))
         def _():
             slots[3 * rows : 4 * rows, :] = partners[b][...]
-    for g in range(groups):
+    for g in range(key_cols.shape[0]):
         key_cols[g] = slots[:, g * HD : (g + 1) * HD].T
-    squares = jnp.zeros((rows, HD), jnp.float32)
-    for i in range(width // HD):
-        x = stream[:, i * HD : (i + 1) * HD].astype(jnp.float32)
-        squares = squares + x * x
-    inv = lax.rsqrt(jnp.sum(squares, axis=1, keepdims=True) / width + 1e-5)
-    inv = jnp.broadcast_to(inv, (rows, HD))
-    inverse[...] = inv
-    for i in range(width // HD):
-        s = slice(i * HD, (i + 1) * HD)
-        queries[:, s] = (stream[:, s].astype(jnp.float32) * inv * gain[:, s]).astype(jnp.bfloat16)
-
-
-def prepare(info, stream, gain, own, near, far, partners):
-    rows, width = stream.shape
+
+
+def arrange(info, own, near, far, partners):
+    rows = own.shape[0]
     kvw = own.shape[1] // 2
-    groups = kvw // HD
-    return pl.pallas_call(
-        functools.partial(prepare_kernel, len(partners)),
+    return pl.pallas_call(
+        functools.partial(arrange_kernel, len(partners)),
         out_shape=[
-            jax.ShapeDtypeStruct((rows, width), jnp.bfloat16),
-            jax.ShapeDtypeStruct((rows, HD), jnp.float32),
             jax.ShapeDtypeStruct((4 * rows, 2 * kvw), jnp.bfloat16),
-            jax.ShapeDtypeStruct((groups, HD, 4 * rows), jnp.bfloat16),
+            jax.ShapeDtypeStruct((kvw // HD, HD, 4 * rows), jnp.bfloat16),
         ],
-        in_specs=[SMEM] + [VMEM] * (5 + len(partners)),
-        out_specs=[VMEM] * 4,
+        in_specs=[SMEM] + [VMEM] * (3 + len(partners)),
+        out_specs=[VMEM] * 2,
         compiler_params=params(VM_SMALL),
-        cost_estimate=cost(6.0),
-    )(info, stream, gain, own, near, far, *partners)
+        cost_estimate=cost(1.0),
+    )(info, own, near, far, *partners)
 
 
 def local_kernel(info, cot, queries, slots, raised_all, gws_all, peaks, totals, weighted):
@@ -414,7 +426,9 @@
     block0 = jnp.where(device == top, block_top, own)
     for b in range(1, bits):
         block0 = jnp.where(device == (1 << b), partners[b], block0)
-    block0, far = lax.optimization_barrier((block0, far))
+    kept, near = lax.optimization_barrier((gain, near))
+    queries, inverse = norm(hidden, kept)
+    block0, far, inverse = lax.optimization_barrier((block0, far, inverse))
     for pairs in global_rounds(count, [0, top] + [1 << b for b in range(1, bits)]):
         masks = {i ^ j for i, j in pairs}
         if len(masks) == 1:
@@ -423,7 +437,7 @@
             route = pairs
         moved = permuted(block0, route)
         block0 = jnp.where(among(device, [t for _, t in pairs]), moved, block0)
-    queries, inverse, slots, key_cols = prepare(info, hidden, gain, own, near, far, partners[1:])
+    slots, key_cols = arrange(info, own, near, far, partners[1:])
     locals_ = list(local(info, upstream, queries, slots))
     block0, locals_[2] = lax.optimization_barrier((block0, locals_[2]))
     odd_block = permuted(block0, swaps[0])

time: 75.3 us -> 73.9 us (0.981)
  starting transfers between devices: 25.5 us -> 23.2 us
  waiting for transfers between devices: 27.1 us -> 28.8 us
  other arithmetic: 2.34 us -> 1.4 us
    ppermute x23, starting transfers between devices: 25.5 us -> 23.2 us  [permuted(): return lax.ppermute(value, axis, pairs)]
    ppermute x23, waiting for transfers between devices: 27.1 us -> 28.8 us  [permuted(): return lax.ppermute(value, axis, pairs)]
    select_n x1, other arithmetic: 1.18 us -> 0.2 us  [on_device(): block0 = jnp.where(device == 1 << b, partners[b], block0)]
    unnamed x10 -> x14, local copies, waits for them, and re-layouts: 1.96 us -> 1.96 us
  transfers between devices with their start and end apart: 23 -> 23, of which waited for: 12 -> 12; matrix products, arithmetic and copies ran while one was open for 2% -> 0% of each run, Pallas kernels for 13% -> 13%
where the time goes in v5:
time: 73.9 us; the launch traced here: 73.6 us
  waiting for transfers between devices  28.8 us (39%)
  starting transfers between devices  23.2 us (31%)
  Pallas kernels  16.8 us (23%)
  local copies, waits for them, and re-layouts  1.96 us (3%)
  between operations  1.49 us (2%)
  other arithmetic  1.4 us (2%)
    ppermute x23, waiting for transfers between devices, permuted(): return lax.ppermute(value, axis, pairs)  28.8 us
    ppermute x23, starting transfers between devices, permuted(): return lax.ppermute(value, axis, pairs)  23.2 us
    pallas_call x1, Pallas kernels, attend(): pl.pallas_call(attend_kernel, out_shape=[jax.ShapeDtypeStruct((rows, widt...  5.38 us
    pallas_call x1, Pallas kernels, local(): pl.pallas_call(local_kernel, out_shape=[tall, tall, flat, flat, flat], in...  5.06 us
    pallas_call x1, Pallas kernels, terms_of(): pl.pallas_call(functools.partial(terms_kernel, partner_count), out_shape=...  3.09 us
    unnamed x14, local copies, waits for them, and re-layouts  1.96 us
    pallas_call x1, Pallas kernels, finish(): pl.pallas_call(functools.partial(finish_kernel, len(parts)), out_shape=[j...  1.76 us
  transfers between devices with their start and end apart: 23, of which 12 were waited for; matrix products, arithmetic and copies ran while one was open for 0% of the time, Pallas kernels for 13%

profile of v5, /device:TPU:0, one launch (start us, length us, event | category | flops | bytes accessed | tf_op | source)
XLA Modules:
  0.0 73.6 jit_solution(6887038819655308798)
XLA Ops:
  0.7 1.0 %pad_maximum_fusion.own = bf16[128,1024]{1,0:T(8,128)(2,1)S(1)} fusion(bf16[128,512]{1,0:T(8,128)(2,1)} %bitcast.15, bf16[128,512]{1,0:T(8,128)(2,1)} %bitcast.17), kind=kLoop, calls=%fused_computation | loop fusion | flops 524288 | bytes 524288 | tf_op jit(solution)/shard_map/concatenate | solution.py:411
  2.2 6.5 %collective-permute-start.4 = (bf16[128,1024]{1,0:T(8,128)(2,1)S(1)}, bf16[128,1024]{1,0:T(8,128)(2,1)S(1)}, u32[]{:S(2)}, u32[]{:S(2)}) collective-permute-start(bf16[128,1024]{1,0:T(8,128)(2,1)S(1)} %pad_maximum_fusion.own), channel_id=1, source_target_pairs={{0,12},{16,28}} | collective-permute-start | bytes 786440 | tf_op jit(solution)/shard_map/ppermute | solution.py:379
  11.1 1.2 %copy-done = bf16[1,128,4096]{2,1,0:T(8,128)(2,1)S(1)} copy-done((bf16[1,128,4096]{2,1,0:T(8,128)(2,1)S(1)}, bf16[1,128,4096]{2,1,0:T(8,128)(2,1)}, u32[]{:S(2)}) %copy-start) | copy-done | bytes 1048600
  13.6 1.9 %collective-permute-done.4 = bf16[128,1024]{1,0:T(8,128)(2,1)S(1)} collective-permute-done((bf16[128,1024]{1,0:T(8,128)(2,1)S(1)}, bf16[128,1024]{1,0:T(8,128)(2,1)S(1)}, u32[]{:S(2)}, u32[]{:S(2)}) %collective-permute-start.4) | collective-permute-done | bytes 262176 | tf_op jit(solution)/shard_map/ppermute | solution.py:379
  15.5 3.8 %collective-permute-done.2.rest_1_ = bf16[128,1024]{1,0:T(8,128)(2,1)S(1)} collective-permute-done((bf16[128,1024]{1,0:T(8,128)(2,1)S(1)}, bf16[128,1024]{1,0:T(8,128)(2,1)S(1)}, u32[]{:S(2)}, u32[]{:S(2)}) %collective-permute-start.2) | collective-permute-done | bytes 262176 | tf_op jit(solution)/shard_map/ppermute | solution.py:379
  19.3 2.6 %collective-permute-done.1.rest_2_ = bf16[128,1024]{1,0:T(8,128)(2,1)S(1)} collective-permute-done((bf16[128,1024]{1,0:T(8,128)(2,1)S(1)}, bf16[128,1024]{1,0:T(8,128)(2,1)S(1)}, u32[]{:S(2)}, u32[]{:S(2)}) %collective-permute-start.1) | collective-permute-done | bytes 262176 | tf_op jit(solution)/shard_map/ppermute | solution.py:379
  22.2 1.8 %collective-permute-start.6 = (bf16[128,1024]{1,0:T(8,128)(2,1)S(1)}, bf16[128,1024]{1,0:T(8,128)(2,1)S(1)}, u32[]{:S(2)}, u32[]{:S(2)}) collective-permute-start(bf16[128,1024]{1,0:T(8,128)(2,1)S(1)} %select_select_fusion), channel_id=1, source_target_pairs={{0,2},{1,3},{2,0},{3,1},{4,6},{5,7},{6,4},{7,5},{8,10},{9,11},{10,... | collective-permute-start | bytes 786440 | tf_op jit(solution)/shard_map/ppermute | solution.py:379
  24.9 5.1 %shard_map.87 = (f32[16,512,256]{2,1,0:T(8,128)S(1)}, f32[16,512,256]{2,1,0:T(8,128)S(1)}, f32[16,1,256]{2,1,0:T(1,128)S(1)}, f32[16,1,256]{2,1,0:T(1,128)S(1)}, f32[16,1,256]{2,1,0:T(1,128)S(1)}) custom-call(s32[3]{0:T(128)S(1)} %pad_add_fusion.info, bf16[128,4096]{1,0:T(8,128)(2,1)S(1)} %bitcast.12, bf16[128,4096]{1,0:T(8,128)(2,1)S(1)} %get-tuple-element.36.queries, ...), custom_call_target="tpu_custom_call" | custom-call | flops 6899999744 | bytes 1048576 | tf_op jit(solution)/shard_map/pallas_call | solution.py:145
  30.4 1.5 %collective-permute-done.7.odd_block = bf16[128,1024]{1,0:T(8,128)(2,1)S(1)} collective-permute-done((bf16[128,1024]{1,0:T(8,128)(2,1)S(1)}, bf16[128,1024]{1,0:T(8,128)(2,1)S(1)}, u32[]{:S(2)}, u32[]{:S(2)}) %collective-permute-start.7) | collective-permute-done | bytes 262176 | tf_op jit(solution)/shard_map/ppermute | solution.py:379
  32.0 5.4 %shard_map.88 = (bf16[128,4096]{1,0:T(8,128)(2,1)S(1)}, f32[32,1024]{1,0:T(8,128)S(1)}, bf16[32,1024]{1,0:T(8,128)(2,1)S(1)}, bf16[32,1024]{1,0:T(8,128)(2,1)S(1...) custom-call(s32[3]{0:T(128)S(1)} %pad_add_fusion.info, ...), custom_call_target="tpu_custom_call" | custom-call | flops 13799999488 | bytes 1048576 | tf_op jit(solution)/shard_map/pallas_call | solution.py:260
  37.5 1.8 %collective-permute-start.12 = (bf16[32,1024]{1,0:T(8,128)(2,1)S(1)}, bf16[32,1024]{1,0:T(8,128)(2,1)S(1)}, u32[]{:S(2)}, u32[]{:S(2)}) collective-permute-start(bf16[32,1024]{1,0:T(8,128)(2,1)S(1)} %get-tuple-element.59), channel_id=1, source_target_pairs={{0,2},{1,3},{2,0},{3,1},{4,6},{5,7},{6,4},{7,5},{8,10},{9,11},{10,... | collective-permute-start | bytes 196616 | tf_op jit(solution)/shard_map/ppermute | solution.py:379
  39.3 1.5 %collective-permute-start.8 = (bf16[128,4096]{1,0:T(8,128)(2,1)S(1)}, bf16[128,4096]{1,0:T(8,128)(2,1)S(1)}, u32[]{:S(2)}, u32[]{:S(2)}) collective-permute-start(bf16[128,4096]{1,0:T(8,128)(2,1)S(1)} %get-tuple-element.51), channel_id=1, source_target_pairs={{16,0},{0,16},{17,1},{1,17},{18,2},{2,18},{19,3},{3,19},{20,4},{4,... | collective-permute-start | bytes 3145736 | tf_op jit(solution)/shard_map/ppermute | solution.py:379
  40.8 1.1 %collective-permute-done.12 = bf16[32,1024]{1,0:T(8,128)(2,1)S(1)} collective-permute-done((bf16[32,1024]{1,0:T(8,128)(2,1)S(1)}, bf16[32,1024]{1,0:T(8,128)(2,1)S(1)}, u32[]{:S(2)}, u32[]{:S(2)}) %collective-permute-start.12) | collective-permute-done | bytes 65568 | tf_op jit(solution)/shard_map/ppermute | solution.py:379
  41.9 1.5 %collective-permute-done.13 = bf16[32,1024]{1,0:T(8,128)(2,1)S(1)} collective-permute-done((bf16[32,1024]{1,0:T(8,128)(2,1)S(1)}, bf16[32,1024]{1,0:T(8,128)(2,1)S(1)}, u32[]{:S(2)}, u32[]{:S(2)}) %collective-permute-start.13) | collective-permute-done | bytes 65568 | tf_op jit(solution)/shard_map/ppermute | solution.py:379
  43.5 3.3 %collective-permute-start.19 = (bf16[32,1024]{1,0:T(8,128)(2,1)S(1)}, bf16[32,1024]{1,0:T(8,128)(2,1)S(1)}, u32[]{:S(2)}, u32[]{:S(2)}) collective-permute-start(bf16[32,1024]{1,0:T(8,128)(2,1)S(1)} %get-tuple-element.67), channel_id=1, source_target_pairs={{0,12},{1,13},{2,14},{3,15},{4,8},{5,9},{6,10},{7,11},{8,4},{9,5},... | collective-permute-start | bytes 196616 | tf_op jit(solution)/shard_map/ppermute | solution.py:379
  48.0 3.1 %shard_map.89 = (f32[128,1024]{1,0:T(8,128)S(1)}, bf16[128,1024]{1,0:T(8,128)(2,1)S(1)}, bf16[128,1024]{1,0:T(8,128)(2,1)S(1)}, bf16[128,1024]{1,0:T(8,128)(2,1)...) custom-call(s32[3]{0:T(128)S(1)} %pad_add_fusion.info, bf16[128,4096]{1,0:T(8,128)(2,1)S(1)} %bitcast.14, ...), custom_call_target="tpu_custom_call" | custom-call | flops 5750000128 | bytes 1048576 | tf_op jit(solution)/shard_map/pallas_call | solution.py:314
  51.1 1.1 %collective-permute-start.9 = (bf16[128,1024]{1,0:T(8,128)(2,1)S(1)}, bf16[128,1024]{1,0:T(8,128)(2,1)S(1)}, u32[]{:S(2)}, u32[]{:S(2)}) collective-permute-start(bf16[128,1024]{1,0:T(8,128)(2,1)S(1)} %get-tuple-element.55), channel_id=1, source_target_pairs={{0,4},{1,5},{2,6},{3,7},{4,0},{5,1},{6,2},{7,3},{8,12},{9,13},{10,... | collective-permute-start | bytes 786440 | tf_op jit(solution)/shard_map/ppermute | solution.py:379
  52.2 1.8 %collective-permute-done.18.rest_4_ = bf16[32,1024]{1,0:T(8,128)(2,1)S(1)} collective-permute-done((bf16[32,1024]{1,0:T(8,128)(2,1)S(1)}, bf16[32,1024]{1,0:T(8,128)(2,1)S(1)}, u32[]{:S(2)}, u32[]{:S(2)}) %collective-permute-start.18) | collective-permute-done | bytes 65568 | tf_op jit(solution)/shard_map/ppermute | solution.py:379
  54.0 1.5 %collective-permute-start.21 = (bf16[32,1024]{1,0:T(8,128)(2,1)S(1)}, bf16[32,1024]{1,0:T(8,128)(2,1)S(1)}, u32[]{:S(2)}, u32[]{:S(2)}) collective-permute-start(bf16[32,1024]{1,0:T(8,128)(2,1)S(1)} %add_convert_fusion), channel_id=1, source_target_pairs={{0,2},{1,3},{2,0},{3,1},{4,6},{5,7},{6,4},{7,5},{8,10},{9,11},{10,... | collective-permute-start | bytes 196616 | tf_op jit(solution)/shard_map/ppermute | solution.py:379
  56.2 2.2 %collective-permute-done.22.rest_8_ = bf16[32,1024]{1,0:T(8,128)(2,1)S(1)} collective-permute-done((bf16[32,1024]{1,0:T(8,128)(2,1)S(1)}, bf16[32,1024]{1,0:T(8,128)(2,1)S(1)}, u32[]{:S(2)}, u32[]{:S(2)}) %collective-permute-start.22) | collective-permute-done | bytes 65568 | tf_op jit(solution)/shard_map/ppermute | solution.py:379
  58.6 1.2 %collective-permute-done.21.rest_7_ = bf16[32,1024]{1,0:T(8,128)(2,1)S(1)} collective-permute-done((bf16[32,1024]{1,0:T(8,128)(2,1)S(1)}, bf16[32,1024]{1,0:T(8,128)(2,1)S(1)}, u32[]{:S(2)}, u32[]{:S(2)}) %collective-permute-start.21) | collective-permute-done | bytes 65568 | tf_op jit(solution)/shard_map/ppermute | solution.py:379
  61.1 9.5 %collective-permute-done.10.rest_1_ = bf16[128,1024]{1,0:T(8,128)(2,1)S(1)} collective-permute-done((bf16[128,1024]{1,0:T(8,128)(2,1)S(1)}, bf16[128,1024]{1,0:T(8,128)(2,1)S(1)}, u32[]{:S(2)}, u32[]{:S(2)}) %collective-permute-start.10) | collective-permute-done | bytes 262176 | tf_op jit(solution)/shard_map/ppermute | solution.py:379
  70.7 1.2 %collective-permute-done.20.rest_6_ = bf16[32,1024]{1,0:T(8,128)(2,1)S(1)} collective-permute-done((bf16[32,1024]{1,0:T(8,128)(2,1)S(1)}, bf16[32,1024]{1,0:T(8,128)(2,1)S(1)}, u32[]{:S(2)}, u32[]{:S(2)}) %collective-permute-start.20) | collective-permute-done | bytes 65568 | tf_op jit(solution)/shard_map/ppermute | solution.py:379
  71.9 1.8 %shard_map.91 = (bf16[128,4096]{1,0:T(8,128)(2,1)}, bf16[128,512]{1,0:T(8,128)(2,1)}, bf16[128,512]{1,0:T(8,128)(2,1)}) custom-call(s32[3]{0:T(128)S(1)} %pad_add_fusion.info, bf16[128,4096]{1,0:T(8,128)(2,1)S(1)} %collective-permute-done.8.received, f32[128,1024]{1,0:T(8,128)S(1)} %shard_map.90.own, f32[32,1024]{1,0:T(8,128)S(1)} %get-tuple-element.68.acc, ...), custom_call_target="tpu_custom_call" | custom-call | flops 575000000 | bytes 1048576 | tf_op jit(solution)/shard_map/pallas_call | solution.py:368
  (49 shorter events, 8.7 us)
Async XLA Ops:
  0.6 21.3 %copy-start.5 = (bf16[1,128,512]{2,1,0:T(8,128)(2,1)S(1)}, bf16[1,128,512]{2,1,0:T(8,128)(2,1)}, u32[]{:S(2)}) copy-start(bf16[1,128,512]{2,1,0:T(8,128)(2,1)} %param.9) | copy-start | bytes 393220
  1.7 8.7 %collective-permute-start = (bf16[128,1024]{1,0:T(8,128)(2,1)S(1)}, bf16[128,1024]{1,0:T(8,128)(2,1)S(1)}, u32[]{:S(2)}, u32[]{:S(2)}) collective-permute-start(bf16[128,1024]{1,0:T(8,128)(2,1)S(1)} %pad_maximum_fusion.own), channel_id=1, source_target_pairs={{0,1},{1,0},{2,3},{3,2},{4,5},{5,4},{6,7},{7,6},{8,9},{9,8},{10,11... | collective-permute-start | bytes 786440 | tf_op jit(solution)/shard_map/ppermute | solution.py:379
  2.2 13.3 %collective-permute-start.4 = (bf16[128,1024]{1,0:T(8,128)(2,1)S(1)}, bf16[128,1024]{1,0:T(8,128)(2,1)S(1)}, u32[]{:S(2)}, u32[]{:S(2)}) collective-permute-start(bf16[128,1024]{1,0:T(8,128)(2,1)S(1)} %pad_maximum_fusion.own), channel_id=1, source_target_pairs={{0,12},{16,28}} | collective-permute-start | bytes 786440 | tf_op jit(solution)/shard_map/ppermute | solution.py:379
  8.7 6.8 %collective-permute-start.3 = (bf16[128,1024]{1,0:T(8,128)(2,1)S(1)}, bf16[128,1024]{1,0:T(8,128)(2,1)S(1)}, u32[]{:S(2)}, u32[]{:S(2)}) collective-permute-start(bf16[128,1024]{1,0:T(8,128)(2,1)S(1)} %pad_maximum_fusion.own), channel_id=1, source_target_pairs={{0,2},{1,3},{2,0},{3,1},{4,6},{5,7},{6,4},{7,5},{8,10},{9,11},{10,... | collective-permute-start | bytes 786440 | tf_op jit(solution)/shard_map/ppermute | solution.py:379
  8.8 10.5 %collective-permute-start.2 = (bf16[128,1024]{1,0:T(8,128)(2,1)S(1)}, bf16[128,1024]{1,0:T(8,128)(2,1)S(1)}, u32[]{:S(2)}, u32[]{:S(2)}) collective-permute-start(bf16[128,1024]{1,0:T(8,128)(2,1)S(1)} %pad_maximum_fusion.own), channel_id=1, source_target_pairs={{0,4},{1,5},{2,6},{3,7},{4,0},{5,1},{6,2},{7,3},{8,12},{9,13},{10,... | collective-permute-start | bytes 786440 | tf_op jit(solution)/shard_map/ppermute | solution.py:379
  8.9 13.1 %collective-permute-start.1 = (bf16[128,1024]{1,0:T(8,128)(2,1)S(1)}, bf16[128,1024]{1,0:T(8,128)(2,1)S(1)}, u32[]{:S(2)}, u32[]{:S(2)}) collective-permute-start(bf16[128,1024]{1,0:T(8,128)(2,1)S(1)} %pad_maximum_fusion.own), channel_id=1, source_target_pairs={{0,8},{1,9},{2,10},{3,11},{4,12},{5,13},{6,14},{7,15},{8,0},{9,1},... | collective-permute-start | bytes 786440 | tf_op jit(solution)/shard_map/ppermute | solution.py:379
  10.4 11.8 %collective-permute-start.5 = (bf16[128,1024]{1,0:T(8,128)(2,1)S(1)}, bf16[128,1024]{1,0:T(8,128)(2,1)S(1)}, u32[]{:S(2)}, u32[]{:S(2)}) collective-permute-start(bf16[128,1024]{1,0:T(8,128)(2,1)S(1)} %pad_maximum_fusion.own), channel_id=1, source_target_pairs={{1,2},{3,4},{5,6},{7,8},{9,10},{11,12},{13,14},{2,1},{4,3},{6,5},{... | collective-permute-start | bytes 786440 | tf_op jit(solution)/shard_map/ppermute | solution.py:379
  22.2 8.1 %collective-permute-start.6 = (bf16[128,1024]{1,0:T(8,128)(2,1)S(1)}, bf16[128,1024]{1,0:T(8,128)(2,1)S(1)}, u32[]{:S(2)}, u32[]{:S(2)}) collective-permute-start(bf16[128,1024]{1,0:T(8,128)(2,1)S(1)} %select_select_fusion), channel_id=1, source_target_pairs={{0,2},{1,3},{2,0},{3,1},{4,6},{5,7},{6,4},{7,5},{8,10},{9,11},{10,... | collective-permute-start | bytes 786440 | tf_op jit(solution)/shard_map/ppermute | solution.py:379
  30.3 1.6 %collective-permute-start.7 = (bf16[128,1024]{1,0:T(8,128)(2,1)S(1)}, bf16[128,1024]{1,0:T(8,128)(2,1)S(1)}, u32[]{:S(2)}, u32[]{:S(2)}) collective-permute-start(bf16[128,1024]{1,0:T(8,128)(2,1)S(1)} %broadcast_select_fusion.even_block), channel_id=1, source_target_pairs={{0,1},{1,0},{2,3},{3,2},{4,5},{5,4},{6,7},{7,6},{8,9},{9,8},{10,11... | collective-permute-start | bytes 786440 | tf_op jit(solution)/shard_map/ppermute | solution.py:379
  37.3 3.5 %collective-permute-start.11 = (bf16[32,1024]{1,0:T(8,128)(2,1)S(1)}, bf16[32,1024]{1,0:T(8,128)(2,1)S(1)}, u32[]{:S(2)}, u32[]{:S(2)}) collective-permute-start(bf16[32,1024]{1,0:T(8,128)(2,1)S(1)} %get-tuple-element.58), channel_id=1, source_target_pairs={{0,1},{1,0},{2,3},{3,2},{4,5},{5,4},{6,7},{7,6},{8,9},{9,8},{10,11... | collective-permute-start | bytes 196616 | tf_op jit(solution)/shard_map/ppermute | solution.py:379
  37.5 4.4 %collective-permute-start.12 = (bf16[32,1024]{1,0:T(8,128)(2,1)S(1)}, bf16[32,1024]{1,0:T(8,128)(2,1)S(1)}, u32[]{:S(2)}, u32[]{:S(2)}) collective-permute-start(bf16[32,1024]{1,0:T(8,128)(2,1)S(1)} %get-tuple-element.59), channel_id=1, source_target_pairs={{0,2},{1,3},{2,0},{3,1},{4,6},{5,7},{6,4},{7,5},{8,10},{9,11},{10,... | collective-permute-start | bytes 196616 | tf_op jit(solution)/shard_map/ppermute | solution.py:379
  39.3 4.1 %collective-permute-start.13 = (bf16[32,1024]{1,0:T(8,128)(2,1)S(1)}, bf16[32,1024]{1,0:T(8,128)(2,1)S(1)}, u32[]{:S(2)}, u32[]{:S(2)}) collective-permute-start(bf16[32,1024]{1,0:T(8,128)(2,1)S(1)} %get-tuple-element.60), channel_id=1, source_target_pairs={{0,3},{1,2},{2,1},{3,0},{4,7},{5,6},{6,5},{7,4},{8,11},{9,10},{10,... | collective-permute-start | bytes 196616 | tf_op jit(solution)/shard_map/ppermute | solution.py:379
  39.3 32.5 %collective-permute-start.8 = (bf16[128,4096]{1,0:T(8,128)(2,1)S(1)}, bf16[128,4096]{1,0:T(8,128)(2,1)S(1)}, u32[]{:S(2)}, u32[]{:S(2)}) collective-permute-start(bf16[128,4096]{1,0:T(8,128)(2,1)S(1)} %get-tuple-element.51), channel_id=1, source_target_pairs={{16,0},{0,16},{17,1},{1,17},{18,2},{2,18},{19,3},{3,19},{20,4},{4,... | collective-permute-start | bytes 3145736 | tf_op jit(solution)/shard_map/ppermute | solution.py:379
  43.5 8.7 %collective-permute-start.19 = (bf16[32,1024]{1,0:T(8,128)(2,1)S(1)}, bf16[32,1024]{1,0:T(8,128)(2,1)S(1)}, u32[]{:S(2)}, u32[]{:S(2)}) collective-permute-start(bf16[32,1024]{1,0:T(8,128)(2,1)S(1)} %get-tuple-element.67), channel_id=1, source_target_pairs={{0,12},{1,13},{2,14},{3,15},{4,8},{5,9},{6,10},{7,11},{8,4},{9,5},... | collective-permute-start | bytes 196616 | tf_op jit(solution)/shard_map/ppermute | solution.py:379
  46.8 7.1 %collective-permute-start.18 = (bf16[32,1024]{1,0:T(8,128)(2,1)S(1)}, bf16[32,1024]{1,0:T(8,128)(2,1)S(1)}, u32[]{:S(2)}, u32[]{:S(2)}) collective-permute-start(bf16[32,1024]{1,0:T(8,128)(2,1)S(1)} %get-tuple-element.67), channel_id=1, source_target_pairs={{0,8},{1,9},{2,10},{3,11},{4,12},{5,13},{6,14},{7,15},{8,0},{9,1},... | collective-permute-start | bytes 196616 | tf_op jit(solution)/shard_map/ppermute | solution.py:379
  47.0 6.9 %collective-permute-start.17 = (bf16[32,1024]{1,0:T(8,128)(2,1)S(1)}, bf16[32,1024]{1,0:T(8,128)(2,1)S(1)}, u32[]{:S(2)}, u32[]{:S(2)}) collective-permute-start(bf16[32,1024]{1,0:T(8,128)(2,1)S(1)} %get-tuple-element.67), channel_id=1, source_target_pairs={{0,4},{1,5},{2,6},{3,7},{4,0},{5,1},{6,2},{7,3},{8,12},{9,13},{10,... | collective-permute-start | bytes 196616 | tf_op jit(solution)/shard_map/ppermute | solution.py:379
  51.1 9.3 %collective-permute-start.9 = (bf16[128,1024]{1,0:T(8,128)(2,1)S(1)}, bf16[128,1024]{1,0:T(8,128)(2,1)S(1)}, u32[]{:S(2)}, u32[]{:S(2)}) collective-permute-start(bf16[128,1024]{1,0:T(8,128)(2,1)S(1)} %get-tuple-element.55), channel_id=1, source_target_pairs={{0,4},{1,5},{2,6},{3,7},{4,0},{5,1},{6,2},{7,3},{8,12},{9,13},{10,... | collective-permute-start | bytes 786440 | tf_op jit(solution)/shard_map/ppermute | solution.py:379
  54.0 4.4 %collective-permute-start.22 = (bf16[32,1024]{1,0:T(8,128)(2,1)S(1)}, bf16[32,1024]{1,0:T(8,128)(2,1)S(1)}, u32[]{:S(2)}, u32[]{:S(2)}) collective-permute-start(bf16[32,1024]{1,0:T(8,128)(2,1)S(1)} %add_convert_fusion), channel_id=1, source_target_pairs={{0,3},{1,2},{2,1},{3,0},{4,7},{5,6},{6,5},{7,4},{8,11},{9,10},{10,... | collective-permute-start | bytes 196616 | tf_op jit(solution)/shard_map/ppermute | solution.py:379
  54.0 5.8 %collective-permute-start.21 = (bf16[32,1024]{1,0:T(8,128)(2,1)S(1)}, bf16[32,1024]{1,0:T(8,128)(2,1)S(1)}, u32[]{:S(2)}, u32[]{:S(2)}) collective-permute-start(bf16[32,1024]{1,0:T(8,128)(2,1)S(1)} %add_convert_fusion), channel_id=1, source_target_pairs={{0,2},{1,3},{2,0},{3,1},{4,6},{5,7},{6,4},{7,5},{8,10},{9,11},{10,... | collective-permute-start | bytes 196616 | tf_op jit(solution)/shard_map/ppermute | solution.py:379
  55.5 15.1 %collective-permute-start.10 = (bf16[128,1024]{1,0:T(8,128)(2,1)S(1)}, bf16[128,1024]{1,0:T(8,128)(2,1)S(1)}, u32[]{:S(2)}, u32[]{:S(2)}) collective-permute-start(bf16[128,1024]{1,0:T(8,128)(2,1)S(1)} %get-tuple-element.56), channel_id=1, source_target_pairs={{0,8},{1,9},{2,10},{3,11},{4,12},{5,13},{6,14},{7,15},{8,0},{9,1},... | collective-permute-start | bytes 786440 | tf_op jit(solution)/shard_map/ppermute | solution.py:379
  58.4 13.5 %collective-permute-start.14 = (bf16[128,1024]{1,0:T(8,128)(2,1)S(1)}, bf16[128,1024]{1,0:T(8,128)(2,1)S(1)}, u32[]{:S(2)}, u32[]{:S(2)}) collective-permute-start(bf16[128,1024]{1,0:T(8,128)(2,1)S(1)} %get-tuple-element.61), channel_id=1, source_target_pairs={{0,1},{1,0},{2,3},{3,2},{4,5},{5,4},{6,7},{7,6},{8,9},{9,8},{10,11... | collective-permute-start | bytes 786440 | tf_op jit(solution)/shard_map/ppermute | solution.py:379
  59.8 12.0 %collective-permute-start.15 = (bf16[128,1024]{1,0:T(8,128)(2,1)S(1)}, bf16[128,1024]{1,0:T(8,128)(2,1)S(1)}, u32[]{:S(2)}, u32[]{:S(2)}) collective-permute-start(bf16[128,1024]{1,0:T(8,128)(2,1)S(1)} %get-tuple-element.62), channel_id=1, source_target_pairs={{0,2},{1,3},{2,0},{3,1},{4,6},{5,7},{6,4},{7,5},{8,10},{9,11},{10,... | collective-permute-start | bytes 786440 | tf_op jit(solution)/shard_map/ppermute | solution.py:379
  60.4 11.5 %collective-permute-start.16 = (bf16[128,1024]{1,0:T(8,128)(2,1)S(1)}, bf16[128,1024]{1,0:T(8,128)(2,1)S(1)}, u32[]{:S(2)}, u32[]{:S(2)}) collective-permute-start(bf16[128,1024]{1,0:T(8,128)(2,1)S(1)} %get-tuple-element.63), channel_id=1, source_target_pairs={{1,2},{3,4},{5,6},{7,8},{9,10},{11,12},{13,14},{2,1},{4,3},{6,5},{... | collective-permute-start | bytes 786440 | tf_op jit(solution)/shard_map/ppermute | solution.py:379
  70.6 1.3 %collective-permute-start.20 = (bf16[32,1024]{1,0:T(8,128)(2,1)S(1)}, bf16[32,1024]{1,0:T(8,128)(2,1)S(1)}, u32[]{:S(2)}, u32[]{:S(2)}) collective-permute-start(bf16[32,1024]{1,0:T(8,128)(2,1)S(1)} %add_convert_fusion), channel_id=1, source_target_pairs={{0,1},{1,0},{2,3},{3,2},{4,5},{5,4},{6,7},{7,6},{8,9},{9,8},{10,11... | collective-permute-start | bytes 196616 | tf_op jit(solution)/shard_map/ppermute | solution.py:379
  (6 other events, 49.3 us)

commit v6 on v5

--- a/solution.py
+++ b/solution.py
@@ -469,8 +469,8 @@
         terms = [swapped(low, k << b) for k in range(1, 1 << min(2, bits - b))]
     mine = (acc + sum(t.astype(jnp.float32) for t in terms)).astype(jnp.bfloat16)
     others = [swapped(mine, mask) for mask in (1, 2, 3)]
-    own_g = collect(own_g, z_r)
-    parts = [near_r, y_r, far_r]
+    own_g = collect(own_g, [y_r] + z_r)
+    parts = [near_r, far_r]
     previous, key_grads, value_grads = finish(info, received, own_g, parts, acc, terms, others)
     return (previous[None], key_grads[None], value_grads[None])
 

time: 73.9 us -> 72.9 us (0.986)
  waiting for transfers between devices: 28.8 us -> 25.4 us
  starting transfers between devices: 23.2 us -> 25.6 us
    ppermute x23, waiting for transfers between devices: 28.8 us -> 25.4 us  [permuted(): return lax.ppermute(value, axis, pairs)]
    ppermute x23, starting transfers between devices: 23.2 us -> 25.6 us  [permuted(): return lax.ppermute(value, axis, pairs)]
where the time goes in v6:
time: 72.9 us; the launch traced here: 72.6 us
  starting transfers between devices  25.6 us (35%)
  waiting for transfers between devices  25.4 us (35%)
  Pallas kernels  16.8 us (23%)
  local copies, waits for them, and re-layouts  1.96 us (3%)
  between operations  1.49 us (2%)
  other arithmetic  1.4 us (2%)
    ppermute x23, starting transfers between devices, permuted(): return lax.ppermute(value, axis, pairs)  25.6 us
    ppermute x23, waiting for transfers between devices, permuted(): return lax.ppermute(value, axis, pairs)  25.4 us
    pallas_call x1, Pallas kernels, attend(): pl.pallas_call(attend_kernel, out_shape=[jax.ShapeDtypeStruct((rows, widt...  5.38 us
    pallas_call x1, Pallas kernels, local(): pl.pallas_call(local_kernel, out_shape=[tall, tall, flat, flat, flat], in...  5.06 us
    pallas_call x1, Pallas kernels, terms_of(): pl.pallas_call(functools.partial(terms_kernel, partner_count), out_shape=...  3.09 us
    unnamed x14, local copies, waits for them, and re-layouts  1.96 us
    pallas_call x1, Pallas kernels, finish(): pl.pallas_call(functools.partial(finish_kernel, len(parts)), out_shape=[j...  1.73 us
  transfers between devices with their start and end apart: 23, of which 12 were waited for; matrix products, arithmetic and copies ran while one was open for 0% of the time, Pallas kernels for 13%

profile of v6, /device:TPU:0, one launch (start us, length us, event | category | flops | bytes accessed | tf_op | source)
XLA Modules:
  0.0 72.6 jit_solution(17097614434207799076)
XLA Ops:
  2.2 6.5 %collective-permute-start.4 = (bf16[128,1024]{1,0:T(8,128)(2,1)S(1)}, bf16[128,1024]{1,0:T(8,128)(2,1)S(1)}, u32[]{:S(2)}, u32[]{:S(2)}) collective-permute-start(bf16[128,1024]{1,0:T(8,128)(2,1)S(1)} %pad_maximum_fusion.own), channel_id=1, source_target_pairs={{0,12},{16,28}} | collective-permute-start | bytes 786440 | tf_op jit(solution)/shard_map/ppermute | solution.py:379
  11.1 1.2 %copy-done = bf16[1,128,4096]{2,1,0:T(8,128)(2,1)S(1)} copy-done((bf16[1,128,4096]{2,1,0:T(8,128)(2,1)S(1)}, bf16[1,128,4096]{2,1,0:T(8,128)(2,1)}, u32[]{:S(2)}) %copy-start) | copy-done | bytes 1048600
  13.6 1.9 %collective-permute-done.4 = bf16[128,1024]{1,0:T(8,128)(2,1)S(1)} collective-permute-done((bf16[128,1024]{1,0:T(8,128)(2,1)S(1)}, bf16[128,1024]{1,0:T(8,128)(2,1)S(1)}, u32[]{:S(2)}, u32[]{:S(2)}) %collective-permute-start.4) | collective-permute-done | bytes 262176 | tf_op jit(solution)/shard_map/ppermute | solution.py:379
  15.5 3.8 %collective-permute-done.2.rest_1_ = bf16[128,1024]{1,0:T(8,128)(2,1)S(1)} collective-permute-done((bf16[128,1024]{1,0:T(8,128)(2,1)S(1)}, bf16[128,1024]{1,0:T(8,128)(2,1)S(1)}, u32[]{:S(2)}, u32[]{:S(2)}) %collective-permute-start.2) | collective-permute-done | bytes 262176 | tf_op jit(solution)/shard_map/ppermute | solution.py:379
  19.3 2.6 %collective-permute-done.1.rest_2_ = bf16[128,1024]{1,0:T(8,128)(2,1)S(1)} collective-permute-done((bf16[128,1024]{1,0:T(8,128)(2,1)S(1)}, bf16[128,1024]{1,0:T(8,128)(2,1)S(1)}, u32[]{:S(2)}, u32[]{:S(2)}) %collective-permute-start.1) | collective-permute-done | bytes 262176 | tf_op jit(solution)/shard_map/ppermute | solution.py:379
  22.2 1.8 %collective-permute-start.6 = (bf16[128,1024]{1,0:T(8,128)(2,1)S(1)}, bf16[128,1024]{1,0:T(8,128)(2,1)S(1)}, u32[]{:S(2)}, u32[]{:S(2)}) collective-permute-start(bf16[128,1024]{1,0:T(8,128)(2,1)S(1)} %select_select_fusion), channel_id=1, source_target_pairs={{0,2},{1,3},{2,0},{3,1},{4,6},{5,7},{6,4},{7,5},{8,10},{9,11},{10,... | collective-permute-start | bytes 786440 | tf_op jit(solution)/shard_map/ppermute | solution.py:379
  24.9 5.1 %shard_map.87 = (f32[16,512,256]{2,1,0:T(8,128)S(1)}, f32[16,512,256]{2,1,0:T(8,128)S(1)}, f32[16,1,256]{2,1,0:T(1,128)S(1)}, f32[16,1,256]{2,1,0:T(1,128)S(1)}, f32[16,1,256]{2,1,0:T(1,128)S(1)}) custom-call(s32[3]{0:T(128)S(1)} %pad_add_fusion.info, bf16[128,4096]{1,0:T(8,128)(2,1)S(1)} %bitcast.12, bf16[128,4096]{1,0:T(8,128)(2,1)S(1)} %get-tuple-element.36.queries, ...), custom_call_target="tpu_custom_call" | custom-call | flops 6899999744 | bytes 1048576 | tf_op jit(solution)/shard_map/pallas_call | solution.py:145
  30.4 1.5 %collective-permute-done.7.odd_block = bf16[128,1024]{1,0:T(8,128)(2,1)S(1)} collective-permute-done((bf16[128,1024]{1,0:T(8,128)(2,1)S(1)}, bf16[128,1024]{1,0:T(8,128)(2,1)S(1)}, u32[]{:S(2)}, u32[]{:S(2)}) %collective-permute-start.7) | collective-permute-done | bytes 262176 | tf_op jit(solution)/shard_map/ppermute | solution.py:379
  32.0 5.4 %shard_map.88 = (bf16[128,4096]{1,0:T(8,128)(2,1)S(1)}, f32[32,1024]{1,0:T(8,128)S(1)}, bf16[32,1024]{1,0:T(8,128)(2,1)S(1)}, bf16[32,1024]{1,0:T(8,128)(2,1)S(1...) custom-call(s32[3]{0:T(128)S(1)} %pad_add_fusion.info, ...), custom_call_target="tpu_custom_call" | custom-call | flops 13799999488 | bytes 1048576 | tf_op jit(solution)/shard_map/pallas_call | solution.py:260
  37.5 1.8 %collective-permute-start.13 = (bf16[32,1024]{1,0:T(8,128)(2,1)S(1)}, bf16[32,1024]{1,0:T(8,128)(2,1)S(1)}, u32[]{:S(2)}, u32[]{:S(2)}) collective-permute-start(bf16[32,1024]{1,0:T(8,128)(2,1)S(1)} %get-tuple-element.60), channel_id=1, source_target_pairs={{0,2},{1,3},{2,0},{3,1},{4,6},{5,7},{6,4},{7,5},{8,10},{9,11},{10,... | collective-permute-start | bytes 196616 | tf_op jit(solution)/shard_map/ppermute | solution.py:379
  39.3 1.5 %collective-permute-start.8 = (bf16[128,4096]{1,0:T(8,128)(2,1)S(1)}, bf16[128,4096]{1,0:T(8,128)(2,1)S(1)}, u32[]{:S(2)}, u32[]{:S(2)}) collective-permute-start(bf16[128,4096]{1,0:T(8,128)(2,1)S(1)} %get-tuple-element.51), channel_id=1, source_target_pairs={{16,0},{0,16},{17,1},{1,17},{18,2},{2,18},{19,3},{3,19},{20,4},{4,... | collective-permute-start | bytes 3145736 | tf_op jit(solution)/shard_map/ppermute | solution.py:379
  40.8 1.1 %collective-permute-done.13 = bf16[32,1024]{1,0:T(8,128)(2,1)S(1)} collective-permute-done((bf16[32,1024]{1,0:T(8,128)(2,1)S(1)}, bf16[32,1024]{1,0:T(8,128)(2,1)S(1)}, u32[]{:S(2)}, u32[]{:S(2)}) %collective-permute-start.13) | collective-permute-done | bytes 65568 | tf_op jit(solution)/shard_map/ppermute | solution.py:379
  41.9 1.5 %collective-permute-done.14 = bf16[32,1024]{1,0:T(8,128)(2,1)S(1)} collective-permute-done((bf16[32,1024]{1,0:T(8,128)(2,1)S(1)}, bf16[32,1024]{1,0:T(8,128)(2,1)S(1)}, u32[]{:S(2)}, u32[]{:S(2)}) %collective-permute-start.14) | collective-permute-done | bytes 65568 | tf_op jit(solution)/shard_map/ppermute | solution.py:379
  43.5 3.3 %collective-permute-start.19 = (bf16[32,1024]{1,0:T(8,128)(2,1)S(1)}, bf16[32,1024]{1,0:T(8,128)(2,1)S(1)}, u32[]{:S(2)}, u32[]{:S(2)}) collective-permute-start(bf16[32,1024]{1,0:T(8,128)(2,1)S(1)} %get-tuple-element.67), channel_id=1, source_target_pairs={{0,12},{1,13},{2,14},{3,15},{4,8},{5,9},{6,10},{7,11},{8,4},{9,5},... | collective-permute-start | bytes 196616 | tf_op jit(solution)/shard_map/ppermute | solution.py:379
  48.0 3.1 %shard_map.89 = (f32[128,1024]{1,0:T(8,128)S(1)}, bf16[128,1024]{1,0:T(8,128)(2,1)S(1)}, bf16[128,1024]{1,0:T(8,128)(2,1)S(1)}, bf16[128,1024]{1,0:T(8,128)(2,1)...) custom-call(s32[3]{0:T(128)S(1)} %pad_add_fusion.info, bf16[128,4096]{1,0:T(8,128)(2,1)S(1)} %bitcast.14, ...), custom_call_target="tpu_custom_call" | custom-call | flops 5750000128 | bytes 1048576 | tf_op jit(solution)/shard_map/pallas_call | solution.py:314
  51.1 1.1 %collective-permute-start.9 = (bf16[128,1024]{1,0:T(8,128)(2,1)S(1)}, bf16[128,1024]{1,0:T(8,128)(2,1)S(1)}, u32[]{:S(2)}, u32[]{:S(2)}) collective-permute-start(bf16[128,1024]{1,0:T(8,128)(2,1)S(1)} %get-tuple-element.55), channel_id=1, source_target_pairs={{0,2},{1,3},{2,0},{3,1},{4,6},{5,7},{6,4},{7,5},{8,10},{9,11},{10,... | collective-permute-start | bytes 786440 | tf_op jit(solution)/shard_map/ppermute | solution.py:379
  52.1 1.1 %collective-permute-start.10 = (bf16[128,1024]{1,0:T(8,128)(2,1)S(1)}, bf16[128,1024]{1,0:T(8,128)(2,1)S(1)}, u32[]{:S(2)}, u32[]{:S(2)}) collective-permute-start(bf16[128,1024]{1,0:T(8,128)(2,1)S(1)} %get-tuple-element.56), channel_id=1, source_target_pairs={{0,4},{1,5},{2,6},{3,7},{4,0},{5,1},{6,2},{7,3},{8,12},{9,13},{10,... | collective-permute-start | bytes 786440 | tf_op jit(solution)/shard_map/ppermute | solution.py:379
  54.0 2.2 %collective-permute-start.11 = (bf16[128,1024]{1,0:T(8,128)(2,1)S(1)}, bf16[128,1024]{1,0:T(8,128)(2,1)S(1)}, u32[]{:S(2)}, u32[]{:S(2)}) collective-permute-start(bf16[128,1024]{1,0:T(8,128)(2,1)S(1)} %get-tuple-element.57), channel_id=1, source_target_pairs={{0,8},{1,9},{2,10},{3,11},{4,12},{5,13},{6,14},{7,15},{8,0},{9,1},... | collective-permute-start | bytes 786440 | tf_op jit(solution)/shard_map/ppermute | solution.py:379
  56.2 3.0 %collective-permute-done.22.rest_7_ = bf16[32,1024]{1,0:T(8,128)(2,1)S(1)} collective-permute-done((bf16[32,1024]{1,0:T(8,128)(2,1)S(1)}, bf16[32,1024]{1,0:T(8,128)(2,1)S(1)}, u32[]{:S(2)}, u32[]{:S(2)}) %collective-permute-start.22) | collective-permute-done | bytes 65568 | tf_op jit(solution)/shard_map/ppermute | solution.py:379
  59.1 1.2 %collective-permute-start.15 = (bf16[128,1024]{1,0:T(8,128)(2,1)S(1)}, bf16[128,1024]{1,0:T(8,128)(2,1)S(1)}, u32[]{:S(2)}, u32[]{:S(2)}) collective-permute-start(bf16[128,1024]{1,0:T(8,128)(2,1)S(1)} %get-tuple-element.62), channel_id=1, source_target_pairs={{0,1},{1,0},{2,3},{3,2},{4,5},{5,4},{6,7},{7,6},{8,9},{9,8},{10,11... | collective-permute-start | bytes 786440 | tf_op jit(solution)/shard_map/ppermute | solution.py:379
  61.0 2.1 %collective-permute-done.10.rest_1_ = bf16[128,1024]{1,0:T(8,128)(2,1)S(1)} collective-permute-done((bf16[128,1024]{1,0:T(8,128)(2,1)S(1)}, bf16[128,1024]{1,0:T(8,128)(2,1)S(1)}, u32[]{:S(2)}, u32[]{:S(2)}) %collective-permute-start.10) | collective-permute-done | bytes 262176 | tf_op jit(solution)/shard_map/ppermute | solution.py:379
  64.0 5.6 %collective-permute-done.11.rest_2_ = bf16[128,1024]{1,0:T(8,128)(2,1)S(1)} collective-permute-done((bf16[128,1024]{1,0:T(8,128)(2,1)S(1)}, bf16[128,1024]{1,0:T(8,128)(2,1)S(1)}, u32[]{:S(2)}, u32[]{:S(2)}) %collective-permute-start.11) | collective-permute-done | bytes 262176 | tf_op jit(solution)/shard_map/ppermute | solution.py:379
  69.8 1.1 %collective-permute-done.20.rest_5_ = bf16[32,1024]{1,0:T(8,128)(2,1)S(1)} collective-permute-done((bf16[32,1024]{1,0:T(8,128)(2,1)S(1)}, bf16[32,1024]{1,0:T(8,128)(2,1)S(1)}, u32[]{:S(2)}, u32[]{:S(2)}) %collective-permute-start.20) | collective-permute-done | bytes 65568 | tf_op jit(solution)/shard_map/ppermute | solution.py:379
  70.9 1.7 %shard_map.91 = (bf16[128,4096]{1,0:T(8,128)(2,1)}, bf16[128,512]{1,0:T(8,128)(2,1)}, bf16[128,512]{1,0:T(8,128)(2,1)}) custom-call(s32[3]{0:T(128)S(1)} %pad_add_fusion.info, bf16[128,4096]{1,0:T(8,128)(2,1)S(1)} %collective-permute-done.8.received, f32[128,1024]{1,0:T(8,128)S(1)} %shard_map.90.own, f32[32,1024]{1,0:T(8,128)S(1)} %get-tuple-element.68.acc, ...), custom_call_target="tpu_custom_call" | custom-call | flops 575000000 | bytes 1048576 | tf_op jit(solution)/shard_map/pallas_call | solution.py:368
  (49 shorter events, 9.8 us)
Async XLA Ops:
  0.6 21.3 %copy-start.5 = (bf16[1,128,512]{2,1,0:T(8,128)(2,1)S(1)}, bf16[1,128,512]{2,1,0:T(8,128)(2,1)}, u32[]{:S(2)}) copy-start(bf16[1,128,512]{2,1,0:T(8,128)(2,1)} %param.9) | copy-start | bytes 393220
  1.7 8.7 %collective-permute-start = (bf16[128,1024]{1,0:T(8,128)(2,1)S(1)}, bf16[128,1024]{1,0:T(8,128)(2,1)S(1)}, u32[]{:S(2)}, u32[]{:S(2)}) collective-permute-start(bf16[128,1024]{1,0:T(8,128)(2,1)S(1)} %pad_maximum_fusion.own), channel_id=1, source_target_pairs={{0,1},{1,0},{2,3},{3,2},{4,5},{5,4},{6,7},{7,6},{8,9},{9,8},{10,11... | collective-permute-start | bytes 786440 | tf_op jit(solution)/shard_map/ppermute | solution.py:379
  2.2 13.3 %collective-permute-start.4 = (bf16[128,1024]{1,0:T(8,128)(2,1)S(1)}, bf16[128,1024]{1,0:T(8,128)(2,1)S(1)}, u32[]{:S(2)}, u32[]{:S(2)}) collective-permute-start(bf16[128,1024]{1,0:T(8,128)(2,1)S(1)} %pad_maximum_fusion.own), channel_id=1, source_target_pairs={{0,12},{16,28}} | collective-permute-start | bytes 786440 | tf_op jit(solution)/shard_map/ppermute | solution.py:379
  8.7 6.8 %collective-permute-start.3 = (bf16[128,1024]{1,0:T(8,128)(2,1)S(1)}, bf16[128,1024]{1,0:T(8,128)(2,1)S(1)}, u32[]{:S(2)}, u32[]{:S(2)}) collective-permute-start(bf16[128,1024]{1,0:T(8,128)(2,1)S(1)} %pad_maximum_fusion.own), channel_id=1, source_target_pairs={{0,2},{1,3},{2,0},{3,1},{4,6},{5,7},{6,4},{7,5},{8,10},{9,11},{10,... | collective-permute-start | bytes 786440 | tf_op jit(solution)/shard_map/ppermute | solution.py:379
  8.8 10.5 %collective-permute-start.2 = (bf16[128,1024]{1,0:T(8,128)(2,1)S(1)}, bf16[128,1024]{1,0:T(8,128)(2,1)S(1)}, u32[]{:S(2)}, u32[]{:S(2)}) collective-permute-start(bf16[128,1024]{1,0:T(8,128)(2,1)S(1)} %pad_maximum_fusion.own), channel_id=1, source_target_pairs={{0,4},{1,5},{2,6},{3,7},{4,0},{5,1},{6,2},{7,3},{8,12},{9,13},{10,... | collective-permute-start | bytes 786440 | tf_op jit(solution)/shard_map/ppermute | solution.py:379
  8.9 13.1 %collective-permute-start.1 = (bf16[128,1024]{1,0:T(8,128)(2,1)S(1)}, bf16[128,1024]{1,0:T(8,128)(2,1)S(1)}, u32[]{:S(2)}, u32[]{:S(2)}) collective-permute-start(bf16[128,1024]{1,0:T(8,128)(2,1)S(1)} %pad_maximum_fusion.own), channel_id=1, source_target_pairs={{0,8},{1,9},{2,10},{3,11},{4,12},{5,13},{6,14},{7,15},{8,0},{9,1},... | collective-permute-start | bytes 786440 | tf_op jit(solution)/shard_map/ppermute | solution.py:379
  10.4 11.8 %collective-permute-start.5 = (bf16[128,1024]{1,0:T(8,128)(2,1)S(1)}, bf16[128,1024]{1,0:T(8,128)(2,1)S(1)}, u32[]{:S(2)}, u32[]{:S(2)}) collective-permute-start(bf16[128,1024]{1,0:T(8,128)(2,1)S(1)} %pad_maximum_fusion.own), channel_id=1, source_target_pairs={{1,2},{3,4},{5,6},{7,8},{9,10},{11,12},{13,14},{2,1},{4,3},{6,5},{... | collective-permute-start | bytes 786440 | tf_op jit(solution)/shard_map/ppermute | solution.py:379
  22.2 8.1 %collective-permute-start.6 = (bf16[128,1024]{1,0:T(8,128)(2,1)S(1)}, bf16[128,1024]{1,0:T(8,128)(2,1)S(1)}, u32[]{:S(2)}, u32[]{:S(2)}) collective-permute-start(bf16[128,1024]{1,0:T(8,128)(2,1)S(1)} %select_select_fusion), channel_id=1, source_target_pairs={{0,2},{1,3},{2,0},{3,1},{4,6},{5,7},{6,4},{7,5},{8,10},{9,11},{10,... | collective-permute-start | bytes 786440 | tf_op jit(solution)/shard_map/ppermute | solution.py:379
  30.3 1.6 %collective-permute-start.7 = (bf16[128,1024]{1,0:T(8,128)(2,1)S(1)}, bf16[128,1024]{1,0:T(8,128)(2,1)S(1)}, u32[]{:S(2)}, u32[]{:S(2)}) collective-permute-start(bf16[128,1024]{1,0:T(8,128)(2,1)S(1)} %broadcast_select_fusion.even_block), channel_id=1, source_target_pairs={{0,1},{1,0},{2,3},{3,2},{4,5},{5,4},{6,7},{7,6},{8,9},{9,8},{10,11... | collective-permute-start | bytes 786440 | tf_op jit(solution)/shard_map/ppermute | solution.py:379
  37.3 3.5 %collective-permute-start.12 = (bf16[32,1024]{1,0:T(8,128)(2,1)S(1)}, bf16[32,1024]{1,0:T(8,128)(2,1)S(1)}, u32[]{:S(2)}, u32[]{:S(2)}) collective-permute-start(bf16[32,1024]{1,0:T(8,128)(2,1)S(1)} %get-tuple-element.59), channel_id=1, source_target_pairs={{0,1},{1,0},{2,3},{3,2},{4,5},{5,4},{6,7},{7,6},{8,9},{9,8},{10,11... | collective-permute-start | bytes 196616 | tf_op jit(solution)/shard_map/ppermute | solution.py:379
  37.5 4.4 %collective-permute-start.13 = (bf16[32,1024]{1,0:T(8,128)(2,1)S(1)}, bf16[32,1024]{1,0:T(8,128)(2,1)S(1)}, u32[]{:S(2)}, u32[]{:S(2)}) collective-permute-start(bf16[32,1024]{1,0:T(8,128)(2,1)S(1)} %get-tuple-element.60), channel_id=1, source_target_pairs={{0,2},{1,3},{2,0},{3,1},{4,6},{5,7},{6,4},{7,5},{8,10},{9,11},{10,... | collective-permute-start | bytes 196616 | tf_op jit(solution)/shard_map/ppermute | solution.py:379
  39.3 4.1 %collective-permute-start.14 = (bf16[32,1024]{1,0:T(8,128)(2,1)S(1)}, bf16[32,1024]{1,0:T(8,128)(2,1)S(1)}, u32[]{:S(2)}, u32[]{:S(2)}) collective-permute-start(bf16[32,1024]{1,0:T(8,128)(2,1)S(1)} %get-tuple-element.61), channel_id=1, source_target_pairs={{0,3},{1,2},{2,1},{3,0},{4,7},{5,6},{6,5},{7,4},{8,11},{9,10},{10,... | collective-permute-start | bytes 196616 | tf_op jit(solution)/shard_map/ppermute | solution.py:379
  39.3 31.6 %collective-permute-start.8 = (bf16[128,4096]{1,0:T(8,128)(2,1)S(1)}, bf16[128,4096]{1,0:T(8,128)(2,1)S(1)}, u32[]{:S(2)}, u32[]{:S(2)}) collective-permute-start(bf16[128,4096]{1,0:T(8,128)(2,1)S(1)} %get-tuple-element.51), channel_id=1, source_target_pairs={{16,0},{0,16},{17,1},{1,17},{18,2},{2,18},{19,3},{3,19},{20,4},{4,... | collective-permute-start | bytes 3145736 | tf_op jit(solution)/shard_map/ppermute | solution.py:379
  43.5 8.6 %collective-permute-start.19 = (bf16[32,1024]{1,0:T(8,128)(2,1)S(1)}, bf16[32,1024]{1,0:T(8,128)(2,1)S(1)}, u32[]{:S(2)}, u32[]{:S(2)}) collective-permute-start(bf16[32,1024]{1,0:T(8,128)(2,1)S(1)} %get-tuple-element.67), channel_id=1, source_target_pairs={{0,12},{1,13},{2,14},{3,15},{4,8},{5,9},{6,10},{7,11},{8,4},{9,5},... | collective-permute-start | bytes 196616 | tf_op jit(solution)/shard_map/ppermute | solution.py:379
  46.8 7.1 %collective-permute-start.18 = (bf16[32,1024]{1,0:T(8,128)(2,1)S(1)}, bf16[32,1024]{1,0:T(8,128)(2,1)S(1)}, u32[]{:S(2)}, u32[]{:S(2)}) collective-permute-start(bf16[32,1024]{1,0:T(8,128)(2,1)S(1)} %get-tuple-element.67), channel_id=1, source_target_pairs={{0,8},{1,9},{2,10},{3,11},{4,12},{5,13},{6,14},{7,15},{8,0},{9,1},... | collective-permute-start | bytes 196616 | tf_op jit(solution)/shard_map/ppermute | solution.py:379
  47.0 6.9 %collective-permute-start.17 = (bf16[32,1024]{1,0:T(8,128)(2,1)S(1)}, bf16[32,1024]{1,0:T(8,128)(2,1)S(1)}, u32[]{:S(2)}, u32[]{:S(2)}) collective-permute-start(bf16[32,1024]{1,0:T(8,128)(2,1)S(1)} %get-tuple-element.67), channel_id=1, source_target_pairs={{0,4},{1,5},{2,6},{3,7},{4,0},{5,1},{6,2},{7,3},{8,12},{9,13},{10,... | collective-permute-start | bytes 196616 | tf_op jit(solution)/shard_map/ppermute | solution.py:379
  51.1 9.3 %collective-permute-start.9 = (bf16[128,1024]{1,0:T(8,128)(2,1)S(1)}, bf16[128,1024]{1,0:T(8,128)(2,1)S(1)}, u32[]{:S(2)}, u32[]{:S(2)}) collective-permute-start(bf16[128,1024]{1,0:T(8,128)(2,1)S(1)} %get-tuple-element.55), channel_id=1, source_target_pairs={{0,2},{1,3},{2,0},{3,1},{4,6},{5,7},{6,4},{7,5},{8,10},{9,11},{10,... | collective-permute-start | bytes 786440 | tf_op jit(solution)/shard_map/ppermute | solution.py:379
  52.1 11.0 %collective-permute-start.10 = (bf16[128,1024]{1,0:T(8,128)(2,1)S(1)}, bf16[128,1024]{1,0:T(8,128)(2,1)S(1)}, u32[]{:S(2)}, u32[]{:S(2)}) collective-permute-start(bf16[128,1024]{1,0:T(8,128)(2,1)S(1)} %get-tuple-element.56), channel_id=1, source_target_pairs={{0,4},{1,5},{2,6},{3,7},{4,0},{5,1},{6,2},{7,3},{8,12},{9,13},{10,... | collective-permute-start | bytes 786440 | tf_op jit(solution)/shard_map/ppermute | solution.py:379
  53.9 5.2 %collective-permute-start.22 = (bf16[32,1024]{1,0:T(8,128)(2,1)S(1)}, bf16[32,1024]{1,0:T(8,128)(2,1)S(1)}, u32[]{:S(2)}, u32[]{:S(2)}) collective-permute-start(bf16[32,1024]{1,0:T(8,128)(2,1)S(1)} %add_convert_fusion), channel_id=1, source_target_pairs={{0,3},{1,2},{2,1},{3,0},{4,7},{5,6},{6,5},{7,4},{8,11},{9,10},{10,... | collective-permute-start | bytes 196616 | tf_op jit(solution)/shard_map/ppermute | solution.py:379
  54.0 15.7 %collective-permute-start.11 = (bf16[128,1024]{1,0:T(8,128)(2,1)S(1)}, bf16[128,1024]{1,0:T(8,128)(2,1)S(1)}, u32[]{:S(2)}, u32[]{:S(2)}) collective-permute-start(bf16[128,1024]{1,0:T(8,128)(2,1)S(1)} %get-tuple-element.57), channel_id=1, source_target_pairs={{0,8},{1,9},{2,10},{3,11},{4,12},{5,13},{6,14},{7,15},{8,0},{9,1},... | collective-permute-start | bytes 786440 | tf_op jit(solution)/shard_map/ppermute | solution.py:379
  59.1 11.7 %collective-permute-start.15 = (bf16[128,1024]{1,0:T(8,128)(2,1)S(1)}, bf16[128,1024]{1,0:T(8,128)(2,1)S(1)}, u32[]{:S(2)}, u32[]{:S(2)}) collective-permute-start(bf16[128,1024]{1,0:T(8,128)(2,1)S(1)} %get-tuple-element.62), channel_id=1, source_target_pairs={{0,1},{1,0},{2,3},{3,2},{4,5},{5,4},{6,7},{7,6},{8,9},{9,8},{10,11... | collective-permute-start | bytes 786440 | tf_op jit(solution)/shard_map/ppermute | solution.py:379
  60.4 10.5 %collective-permute-start.16 = (bf16[128,1024]{1,0:T(8,128)(2,1)S(1)}, bf16[128,1024]{1,0:T(8,128)(2,1)S(1)}, u32[]{:S(2)}, u32[]{:S(2)}) collective-permute-start(bf16[128,1024]{1,0:T(8,128)(2,1)S(1)} %get-tuple-element.63), channel_id=1, source_target_pairs={{1,2},{3,4},{5,6},{7,8},{9,10},{11,12},{13,14},{2,1},{4,3},{6,5},{... | collective-permute-start | bytes 786440 | tf_op jit(solution)/shard_map/ppermute | solution.py:379
  63.2 6.6 %collective-permute-start.21 = (bf16[32,1024]{1,0:T(8,128)(2,1)S(1)}, bf16[32,1024]{1,0:T(8,128)(2,1)S(1)}, u32[]{:S(2)}, u32[]{:S(2)}) collective-permute-start(bf16[32,1024]{1,0:T(8,128)(2,1)S(1)} %add_convert_fusion), channel_id=1, source_target_pairs={{0,2},{1,3},{2,0},{3,1},{4,6},{5,7},{6,4},{7,5},{8,10},{9,11},{10,... | collective-permute-start | bytes 196616 | tf_op jit(solution)/shard_map/ppermute | solution.py:379
  69.6 1.3 %collective-permute-start.20 = (bf16[32,1024]{1,0:T(8,128)(2,1)S(1)}, bf16[32,1024]{1,0:T(8,128)(2,1)S(1)}, u32[]{:S(2)}, u32[]{:S(2)}) collective-permute-start(bf16[32,1024]{1,0:T(8,128)(2,1)S(1)} %add_convert_fusion), channel_id=1, source_target_pairs={{0,1},{1,0},{2,3},{3,2},{4,5},{5,4},{6,7},{7,6},{8,9},{9,8},{10,11... | collective-permute-start | bytes 196616 | tf_op jit(solution)/shard_map/ppermute | solution.py:379
  (6 other events, 49.3 us)
